TPU v7x, 256 devices: a whole 4x4x8 slice. The times are simulated.
256 devices in a mesh: req: 16 (over z, core), wa: 16 (over x, y).
Axes of the slice: x: 4, y: 4, z: 8, core: 2. Of those that a mesh axis runs over, the one named last changes fastest.
Arguments:
- projected: bfloat16 [3, 2048, 2, 8192], P(None, 'req', None, 'wa'), may hold values from -6 to 6
- conv_weight: bfloat16 [4, 8192], P(None, 'wa'), may hold values from -3 to 3
- conv_bias: float32 [8192], P('wa'), may hold values from -3 to 3
- xproj_weight: bfloat16 [8192, 544], P('wa'), may hold values from -0.0625 to 0.0625
- dtproj_weight: bfloat16 [512, 8192], P(None, 'wa'), may hold values from -0.25 to 0.25
- dt_bias: float32 [8192], P('wa'), may hold values from -4 to -0.5
- a_rate: float32 [16, 8192], P(None, 'wa'), may hold values from 0.1 to 8
- skip_gain: float32 [8192], P('wa'), may hold values from 0.5 to 1.5
- ssm_state: float32 [2048, 16, 8192], P('req', None, 'wa'), may hold values from -6 to 6
- conv_cache: bfloat16 [2048, 3, 8192], P('req', None, 'wa'), may hold values from -6 to 6
- send_dest: int32 [2048], P('req'), may hold values from 0 to 15, as said below
- recv_source: int32 [2048], P('req'), may hold values from 0 to 15, as said below
- active: int32 [2048], P('req'), may hold values from 0 to 1, as said below
Outputs:
- gated_out: bfloat16 [3, 2048, 8192], P(None, 'req', 'wa')
- state_out: float32 [2048, 16, 8192], P('req', None, 'wa')
- cache_out: bfloat16 [2048, 3, 8192], P('req', None, 'wa')
Inputs may be any that keep to these rules, and one draw needn't show every extreme that they name: `send_dest`: A slot whose request stays names its own device. From one device to one other device at most 2 requests move, and in every draw some device receives exactly 2 from every other device. No slot both leaves and receives. `recv_source`: A slot that receives nothing names its own device. The number of slots of device j naming device i equals the number of slots of i whose send_dest is j. `active`: every receiving slot is 1 and every slot left by a leaving request without a new one is 0.
All inputs are finite; a program needn't handle non-finite values.
Results may differ from a plain program's by a relative error of at most 0.0056.
Values sent between devices are 32-bit elements; how exact they have to be, the bound alone decides.
No kernel may reach another device: no remote copies, remote signals or barrier semaphores. Data moves between devices by JAX's collectives and lax.ppermute only.
A program may use at most 64 MiB of HBM per device.

v0:
```python
import jax
import jax.numpy as jnp
from jax import lax
from jax.sharding import PartitionSpec as P

CAP = 2


def local_ranks(targets, peer_count):
    onehot = (targets[:, None] == jnp.arange(peer_count, dtype=jnp.int32)[None, :]).astype(
        jnp.int32
    )
    earlier = jnp.cumsum(onehot, axis=0) - onehot
    return jnp.sum(earlier * onehot, axis=1)


def on_device(
    projected,
    conv_weight,
    conv_bias,
    xproj_weight,
    dtproj_weight,
    dt_bias,
    a_rate,
    skip_gain,
    ssm_state,
    conv_cache,
    send_dest,
    recv_source,
    active,
):
    step_count, slot_count = (projected.shape[0], projected.shape[1])
    rank_width = dtproj_weight.shape[0]
    state_width = a_rate.shape[0]
    taps_count = conv_weight.shape[0]
    peer_count = lax.axis_size("req")
    own_index = lax.axis_index("req")
    send_rank = local_ranks(send_dest, peer_count)
    leaving = send_dest != own_index
    buckets = jnp.arange(peer_count * CAP, dtype=jnp.int32)
    matches = (
        leaving[None, :]
        & (send_dest[None, :] == (buckets // CAP)[:, None])
        & (send_rank[None, :] == (buckets % CAP)[:, None])
    )
    picked = jnp.sum(
        jnp.where(matches, jnp.arange(slot_count, dtype=jnp.int32)[None, :], 0), axis=1
    )
    filled = jnp.any(matches, axis=1)[:, None, None]
    out_state = jnp.where(filled, ssm_state[picked], jnp.float32(0.0))
    out_cache = jnp.where(filled, conv_cache[picked].astype(jnp.float32), jnp.float32(0.0))
    got_state, got_cache = (
        lax.all_to_all(out_state, "req", split_axis=0, concat_axis=0, tiled=True),
        lax.all_to_all(out_cache, "req", split_axis=0, concat_axis=0, tiled=True),
    )
    arriving = recv_source != own_index
    recv_rank = jnp.minimum(local_ranks(recv_source, peer_count), CAP - 1)
    where_from = jnp.where(arriving, recv_source * CAP + recv_rank, 0)
    arriving_b = arriving[:, None, None]
    leaving_b = leaving[:, None, None]
    moved_state = jnp.where(
        arriving_b, got_state[where_from], jnp.where(leaving_b, jnp.float32(0.0), ssm_state)
    )
    moved_cache = jnp.where(
        arriving_b,
        got_cache[where_from],
        jnp.where(leaving_b, jnp.float32(0.0), conv_cache.astype(jnp.float32)),
    )
    x_part = projected[:, :, 0]
    z_part = projected[:, :, 1]
    window = jnp.concatenate(
        [jnp.transpose(moved_cache, (1, 0, 2)), x_part.astype(jnp.float32)], axis=0
    )
    conv_taps = conv_weight.astype(jnp.float32)

    def conv_at(step_index):
        total = conv_bias[None, :]
        for tap_index in range(taps_count):
            total = total + conv_taps[tap_index][None, :] * window[step_index + tap_index]
        return jax.nn.silu(total).astype(jnp.bfloat16)

    conv_list = [conv_at(step_index) for step_index in range(step_count)]
    alive = active == 1
    alive_b = alive[:, None, None]
    state = moved_state
    results = []
    for step_index in range(step_count):
        conv_now = conv_list[step_index]
        mixed_now = lax.psum(
            jnp.dot(conv_now, xproj_weight, preferred_element_type=jnp.float32), "wa"
        )
        rank_part = mixed_now[:, :rank_width].astype(jnp.bfloat16)
        step_now = jax.nn.softplus(
            jnp.dot(rank_part, dtproj_weight, preferred_element_type=jnp.float32) + dt_bias[None, :]
        )
        b_part = mixed_now[:, rank_width : rank_width + state_width]
        c_part = mixed_now[:, rank_width + state_width :]
        conv_value = conv_now.astype(jnp.float32)
        decay = jnp.exp(-step_now[:, None, :] * a_rate[None, :, :])
        updated = decay * state + (step_now * conv_value)[:, None, :] * b_part[:, :, None]
        state = jnp.where(alive_b, updated, state)
        readout = jnp.sum(c_part[:, :, None] * state, axis=1) + skip_gain[None, :] * conv_value
        gated = readout * jax.nn.silu(z_part[step_index].astype(jnp.float32))
        results.append(jnp.where(alive[:, None], gated, jnp.float32(0.0)).astype(jnp.bfloat16))
    gated_out = jnp.stack(results)
    new_cache = jnp.transpose(window[step_count:], (1, 0, 2))
    cache_out = jnp.where(alive_b, new_cache, moved_cache).astype(jnp.bfloat16)
    return (gated_out, state, cache_out)


def solution(mesh):
    return jax.shard_map(
        on_device,
        mesh=mesh,
        in_specs=(
            P(None, "req", None, "wa"),
            P(None, "wa"),
            P("wa"),
            P("wa", None),
            P(None, "wa"),
            P("wa"),
            P(None, "wa"),
            P("wa"),
            P("req", None, "wa"),
            P("req", None, "wa"),
            P("req"),
            P("req"),
            P("req"),
        ),
        out_specs=(P(None, "req", "wa"), P("req", None, "wa"), P("req", None, "wa")),
        check_vma=False,
    )
```

profile of v0, /device:TPU:32, one launch (start us, length us, event | category | flops | bytes accessed | tf_op | source)
XLA Modules:
  0.0 169.6 jit_solution(3492807102914181820)
XLA Ops:
  9.7 0.8 fusion.39
  10.6 0.8 select_reduce_fusion.2
  11.4 1.9 %gather_fusion = bf16[32,3,512]{2,0,1:T(8,128)(2,1)S(1)} fusion(bf16[128,3,512]{2,0,1:T(8,128)(2,1)} %param.22, s32[1024]{0:T(1024)S(1)} %pad_clamp_fusion.1), kind=kCustom, calls=%fused_computation | custom fusion | bytes 196736 | tf_op jit(solution)/shard_map/gather | solution.py:51
  13.5 0.8 copy.50
  14.3 8.6 %all-to-all-start = ((f32[32,3,512]{2,1,0:T(4,128)}), f32[32,3,512]{2,1,0:T(4,128)S(1)}, u32[]{:S(2)}, u32[]{:S(2)}) async-start(f32[32,3,512]{2,1,0:T(4,128)} %copy.50), calls=%async_computation | async-start | bytes 524288 | tf_op jit(solution)/shard_map/all_to_all | solution.py:54
  23.0 0.8 fusion.49
  26.9 3.8 %gather_fusion.2 = f32[32,16,512]{2,1,0:T(8,128)} fusion(f32[128,16,512]{2,1,0:T(8,128)} %param.21, s32[1024]{0:T(1024)S(1)} %pad_clamp_fusion.1), kind=kCustom, calls=%fused_computation.2 | custom fusion | bytes 2097280 | tf_op jit(solution)/shard_map/gather | solution.py:50
  30.7 1.8 %all-to-all-done = f32[32,3,512]{2,1,0:T(4,128)S(1)} async-done(((f32[32,3,512]{2,1,0:T(4,128)}), f32[32,3,512]{2,1,0:T(4,128)S(1)}, u32[]{:S(2)}, u32[]{:S(2)}) %all-to-all-start) | async-done | bytes 196640 | tf_op jit(solution)/shard_map/all_to_all | solution.py:54
  32.5 1.2 gather_fusion.1
  34.2 0.9 copy-done.1
  35.5 1.0 fusion.51
  36.5 1.0 fusion.52
  37.5 1.0 fusion.50
  38.6 1.1 broadcast_select_fusion
  39.7 5.4 %all-to-all-start.1 = ((f32[32,16,512]{2,1,0:T(8,128)}), f32[32,16,512]{2,1,0:T(8,128)S(1)}, u32[]{:S(2)}, u32[]{:S(2)}) async-start(f32[32,16,512]{2,1,0:T(8,128)} %broadcast_select_fusion), calls=%async_computation.1 | async-start | bytes 2097152 | tf_op jit(solution)/shard_map/all_to_all | solution.py:53
  45.1 2.8 %fusion.42 = (bf16[1,128,1,512]{3,2,1,0:T(2,128)(2,1)}, bf16[1,128,1,512]{3,2,1,0:T(2,128)(2,1)}, bf16[1,128,1,512]{3,2,1,0:T(2,128)(2,1)}) fusion(bf16[3,128,2,512]{3,2,1,0:T(2,128)(2,1)} %param.13), kind=kLoop, calls=%fused_computation.124 | loop fusion | bytes 786432 | tf_op jit(solution)/shard_map/slice | solution.py:103
  47.9 2.4 %fusion = bf16[128,3,512]{2,0,1:T(8,128)(2,1)} fusion(pred[128]{0:T(512)(128)(4,1)S(1)} %broadcast_compare_fusion.2, bf16[3,128,1,512]{3,2,1,0:T(2,128)(2,1)} %bitcast.194, bf16[128,3,512]{2,0,1:T(8,128)(2,1)} %param.22, pred[128]{0:T(512)(128)(4,1)S(1)} %broadcast_compare_fusion, f32[128,3,512]{2,1,0:T(4,128)S(1)} %gather_fusion.1, ...), kind=kLoop, calls=%fused_computation.14 | loop fusion | flops 983040 | bytes 1966464 | tf_op jit(solution)/shard_map/convert_element_type | solution.py:107
  50.3 84.2 %all-reduce.3.cloned.1.call-done = (f32[128,544]{0,1:T(8,128)}, f32[128,544]{0,1:T(8,128)}, f32[128,544]{0,1:T(8,128)}) async-done(((f32[128,544]{0,1:T(8,128)}, f32[128,544]{0,1:T(8,128)}, f32[128,544]{0,1:T(8,128)}), (f32[128,544]{0,1:T(8,128)}, f32[128,544]{0,1:T(8,128)}, f32[128,544]{0,1:T(8,128)})) %all-reduce.3.cloned.1.call-update) | async-done | bytes 835600 | tf_op jit(solution)/shard_map/psum | solution.py:89
  140.4 1.5 fusion.48
  141.9 2.3 %fusion.46 = (f32[128,512]{1,0:T(8,128)}, f32[128,512]{1,0:T(8,128)}) fusion(bf16[128,512]{1,0:T(8,128)(2,1)} %copy-done.7, f32[512]{0:T(512)S(1)} %copy-done.17, bf16[512,512]{1,0:T(8,128)(2,1)} %param.17, f32[128,544]{0,1:T(8,128)} %get-tuple-element.6), kind=kOutput, calls=%fused_computation.128 | convolution fusion | flops 67764224 | bytes 1312768 | tf_op jit(solution)/shard_map/dot_general | solution.py:94
  144.2 1.5 fusion.47
  145.8 3.0 %gather_fusion.3 = f32[128,16,512]{2,1,0:T(8,128)} fusion(f32[32,16,512]{2,1,0:T(8,128)S(1)} %all-to-all-done.1, s32[1024]{0:T(1024)} %copy-done.24), kind=kCustom, calls=%fused_computation.3 | custom fusion | bytes 8389120 | tf_op jit(solution)/shard_map/gather | solution.py:62
  148.8 8.1 %multiply_reduce_fusion.2 = (f32[128,512]{1,0:T(8,128)S(1)}, f32[128,512]{1,0:T(8,128)S(1)}, f32[128,16,512]{2,1,0:T(8,128)S(1)}) fusion(f32[128,16]{1,0:T(8,128)} %copy.53, f32[128,16]{1,0:T(8,128)S(1)} %copy.57, f32[128,512]{1,0:T(8,128)S(1)} %get-tuple-element.30, f32[16,512]{1,0:T(8,128)S(1)} %copy-done.16, f32[128,512]{1,0:T(8,128)S(1)} %get-tuple-element.29, ...), kind=kLoop, calls=%fused_computation.8 | loop fusion | flops 16646144 | bytes 14221696 | tf_op jit(solution)/shard_map/reduce_sum | solution.py:102
  157.0 4.2 %multiply_reduce_fusion = (f32[128,512]{1,0:T(8,128)S(1)}, f32[128,16,512]{2,1,0:T(8,128)}) fusion(f32[128,16]{1,0:T(8,128)S(1)} %copy-done.15, f32[128,16]{1,0:T(8,128)S(1)} %copy-done.14, f32[128,512]{1,0:T(8,128)S(1)} %copy-done.13, f32[128,16,512]{2,1,0:T(8,128)S(1)} %get-tuple-element.8, f32[128,16]{1,0:T(8,128)S(1)} %copy.57, ...), kind=kLoop, calls=%fused_computation.4 | loop fusion | flops 12517376 | bytes 9756800 | tf_op jit(solution)/shard_map/reduce_sum | solution.py:102
  (86 shorter events, 14.1 us)
Async XLA Ops:
  7.2 28.3 %copy-start = (bf16[512,544]{0,1:T(8,128)(2,1)S(1)}, bf16[512,544]{0,1:T(8,128)(2,1)}, u32[]{:S(2)}) copy-start(bf16[512,544]{0,1:T(8,128)(2,1)} %param.16) | copy-start | bytes 1671172
  7.2 23.5 %copy-start.4 = (bf16[3,128,2,512]{3,2,1,0:T(2,128)(2,1)S(1)}, bf16[3,128,2,512]{3,2,1,0:T(2,128)(2,1)}, u32[]{:S(2)}) copy-start(bf16[3,128,2,512]{3,2,1,0:T(2,128)(2,1)} %param.13) | copy-start | bytes 2359300
  8.7 39.2 %copy-start.22 = (pred[128]{0:T(512)(128)(4,1)}, pred[128]{0:T(512)(128)(4,1)S(1)}, u32[]{:S(2)}) copy-start(pred[128]{0:T(512)(128)(4,1)S(1)} %broadcast_compare_fusion) | copy-start | bytes 388
  11.4 22.3 %copy-start.3 = (bf16[128,3,512]{2,0,1:T(8,128)(2,1)S(1)}, bf16[128,3,512]{2,0,1:T(8,128)(2,1)}, u32[]{:S(2)}) copy-start(bf16[128,3,512]{2,0,1:T(8,128)(2,1)} %param.22) | copy-start | bytes 1179652
  14.3 18.2 %all-to-all-start = ((f32[32,3,512]{2,1,0:T(4,128)}), f32[32,3,512]{2,1,0:T(4,128)S(1)}, u32[]{:S(2)}, u32[]{:S(2)}) async-start(f32[32,3,512]{2,1,0:T(4,128)} %copy.50), calls=%async_computation | async-start | bytes 524288 | tf_op jit(solution)/shard_map/all_to_all | solution.py:54
  22.9 12.2 %copy-start.18 = (f32[512]{0:T(512)S(1)}, f32[512]{0:T(512)}, u32[]{:S(2)}) copy-start(f32[512]{0:T(512)} %param.15) | copy-start | bytes 6148
  22.9 111.6 %all-reduce.3.cloned.1.call-start = ((), (), s32[]{:S(2)}) async-start(), calls=%async_computation.2 | async-start | bytes 1671168 | tf_op jit(solution)/shard_map/psum | solution.py:89
  26.9 21.0 %copy-start.25 = (pred[128]{0:T(512)(128)(4,1)}, pred[128]{0:T(512)(128)(4,1)S(1)}, u32[]{:S(2)}) copy-start(pred[128]{0:T(512)(128)(4,1)S(1)} %broadcast_compare_fusion.1) | copy-start | bytes 388
  30.7 5.8 %copy-start.24 = (s32[1024]{0:T(1024)}, s32[1024]{0:T(1024)S(1)}, u32[]{:S(2)}) copy-start(s32[1024]{0:T(1024)S(1)} %pad_clamp_fusion) | copy-start | bytes 12292
  34.2 4.4 %copy-start.5 = (f32[32,16,512]{2,1,0:T(8,128)S(1)}, f32[32,16,512]{2,1,0:T(8,128)}, u32[]{:S(2)}) copy-start(f32[32,16,512]{2,1,0:T(8,128)} %gather_fusion.2) | copy-start | bytes 3145732
  35.4 9.7 %copy-start.26 = (s32[128]{0:T(128)S(1)}, s32[128]{0:T(128)}, u32[]{:S(2)}) copy-start(s32[128]{0:T(128)} %param.25) | copy-start | bytes 1540
  38.5 101.8 %copy-start.17 = (f32[512]{0:T(512)S(1)}, f32[512]{0:T(512)}, u32[]{:S(2)}) copy-start(f32[512]{0:T(512)} %param.18) | copy-start | bytes 6148
  39.7 106.1 %all-to-all-start.1 = ((f32[32,16,512]{2,1,0:T(8,128)}), f32[32,16,512]{2,1,0:T(8,128)S(1)}, u32[]{:S(2)}, u32[]{:S(2)}) async-start(f32[32,16,512]{2,1,0:T(8,128)} %broadcast_select_fusion), calls=%async_computation.1 | async-start | bytes 2097152 | tf_op jit(solution)/shard_map/all_to_all | solution.py:53
  45.1 99.1 %copy-start.20 = (pred[128]{0:T(512)(128)(4,1)}, pred[128]{0:T(512)(128)(4,1)S(1)}, u32[]{:S(2)}) copy-start(pred[128]{0:T(512)(128)(4,1)S(1)} %broadcast_compare_fusion.2) | copy-start | bytes 388
  148.8 8.1 %copy-start.12 = (f32[128,512]{1,0:T(8,128)S(1)}, f32[128,512]{1,0:T(8,128)}, u32[]{:S(2)}) copy-start(f32[128,512]{1,0:T(8,128)} %get-tuple-element.25) | copy-start | bytes 786436
  148.8 8.1 %copy-start.13 = (f32[128,512]{1,0:T(8,128)S(1)}, f32[128,512]{1,0:T(8,128)}, u32[]{:S(2)}) copy-start(f32[128,512]{1,0:T(8,128)} %get-tuple-element.26) | copy-start | bytes 786436
  148.8 8.1 %copy-start.14 = (f32[128,16]{1,0:T(8,128)S(1)}, f32[128,16]{1,0:T(8,128)}, u32[]{:S(2)}) copy-start(f32[128,16]{1,0:T(8,128)} %copy.60) | copy-start | bytes 24580
  148.8 8.1 %copy-start.15 = (f32[128,16]{1,0:T(8,128)S(1)}, f32[128,16]{1,0:T(8,128)}, u32[]{:S(2)}) copy-start(f32[128,16]{1,0:T(8,128)} %copy.59) | copy-start | bytes 24580
  148.8 8.1 %copy-start.21 = (pred[128]{0:T(512)(128)(4,1)S(1)}, pred[128]{0:T(512)(128)(4,1)}, u32[]{:S(2)}) copy-start(pred[128]{0:T(512)(128)(4,1)} %copy-done.20) | copy-start | bytes 388
  156.9 4.3 %copy-start.2 = (f32[3,128,512]{2,1,0:T(8,128)S(1)}, f32[3,128,512]{2,1,0:T(8,128)}, u32[]{:S(2)}) copy-start(f32[3,128,512]{2,1,0:T(8,128)} %copy-done.1) | copy-start | bytes 2359300
  156.9 4.3 %copy-start.11 = (bf16[1,128,1,512]{3,2,1,0:T(2,128)(2,1)S(1)}, bf16[1,128,1,512]{3,2,1,0:T(2,128)(2,1)}, u32[]{:S(2)}) copy-start(bf16[1,128,1,512]{3,2,1,0:T(2,128)(2,1)} %get-tuple-element.18) | copy-start | bytes 393220
  156.9 4.3 %copy-start.19 = (f32[512]{0:T(512)S(1)}, f32[512]{0:T(512)}, u32[]{:S(2)}) copy-start(f32[512]{0:T(512)} %param.15) | copy-start | bytes 6148
  157.0 4.5 %copy-start.9 = (bf16[1,128,1,512]{3,2,1,0:T(2,128)(2,1)S(1)}, bf16[1,128,1,512]{3,2,1,0:T(2,128)(2,1)}, u32[]{:S(2)}) copy-start(bf16[1,128,1,512]{3,2,1,0:T(2,128)(2,1)} %get-tuple-element.16) | copy-start | bytes 393220
  157.0 4.5 %copy-start.10 = (bf16[1,128,1,512]{3,2,1,0:T(2,128)(2,1)S(1)}, bf16[1,128,1,512]{3,2,1,0:T(2,128)(2,1)}, u32[]{:S(2)}) copy-start(bf16[1,128,1,512]{3,2,1,0:T(2,128)(2,1)} %get-tuple-element.17) | copy-start | bytes 393220
  (6 other events, 13.3 us)
Sparse Core Ops, SparseCore 0:
  38.7 95.7 all-reduce.2
where the time goes:
time: 170 us
  waiting for transfers between devices  86 us (51%)
  other arithmetic  25.5 us (15%)
  local copies, waits for them, and re-layouts  21.2 us (12%)
  between operations  14.5 us (9%)
  starting transfers between devices  14.1 us (8%)
  matrix products  8.43 us (5%)
    psum x1, waiting for transfers between devices, on_device(): lax.psum(jnp.dot(conv_now, xproj_weight, preferred_element_type=jnp.float...  84.2 us
    reduce_sum x2, other arithmetic, on_device(): jnp.sum(c_part[:, :, None] * state, axis=1)  12.3 us
    all_to_all x1, starting transfers between devices, on_device(): lax.all_to_all(out_cache, 'req', split_axis=0, concat_axis=0, tiled=True)  8.59 us
    all_to_all x1, starting transfers between devices, on_device(): lax.all_to_all(out_state, 'req', split_axis=0, concat_axis=0, tiled=True)  5.45 us
    dot_general x3, matrix products, on_device(): jnp.dot(rank_part, dtproj_weight, preferred_element_type=jnp.float32)  5.4 us
    gather x1, local copies, waits for them, and re-layouts, on_device(): out_state = jnp.where(filled, ssm_state[picked], jnp.float32(0.0))  3.77 us
  transfers between devices with their start and end apart: 3, of which 2 were waited for; matrix products, arithmetic and copies ran while one was open for 15% of the time, Pallas kernels for 0%

commit v1 on v0

v1 whole, which is shorter than its diff:
```python
import math

import jax
import jax.numpy as jnp
from jax import lax
from jax.experimental import pallas as pl
from jax.experimental.pallas import tpu as pltpu
from jax.sharding import PartitionSpec as P

CAP = 2
SIDE = 4
MIB = 1 << 20
F32 = jnp.float32
BF16 = jnp.bfloat16
VM = pl.BlockSpec(memory_space=pltpu.VMEM)
SM = pl.BlockSpec(memory_space=pltpu.SMEM)
HB = pl.BlockSpec(memory_space=pl.ANY)


def shift(axis, amount):
    pairs = []
    for x in range(SIDE):
        for y in range(SIDE):
            tx, ty = (x + amount) % SIDE, y
            if axis == 1:
                tx, ty = x, (y + amount) % SIDE
            pairs.append((x * SIDE + y, tx * SIDE + ty))
    return pairs


def dot_t(lhs, rhs):
    return lax.dot_general(lhs, rhs, (((1,), (1,)), ((), ())), preferred_element_type=F32)


def dot_n(lhs, rhs):
    return jnp.dot(lhs, rhs, preferred_element_type=F32)


def iota(shape, dim):
    return lax.broadcasted_iota(jnp.int32, shape, dim)


def as_column(row, size):
    eye = iota((size, size), 0) == iota((size, size), 1)
    return jnp.sum(jnp.where(eye, jnp.broadcast_to(row, (size, size)), 0), axis=1, keepdims=True)


def ranks_row(row, col, size):
    earlier = (col == row) & (iota((size, size), 0) < iota((size, size), 1))
    return jnp.sum(jnp.where(earlier, 1, 0), axis=0, keepdims=True)


def ranks_col(row, col, size):
    earlier = (col == row) & (iota((size, size), 1) < iota((size, size), 0))
    return jnp.sum(jnp.where(earlier, 1, 0), axis=1, keepdims=True)


def pick_cache_kernel(pos_ref, dest_ref, cache_ref, out_ref):
    taps, slots, _ = cache_ref.shape
    own = pos_ref[0]
    row = dest_ref[...]
    rank = ranks_row(row, as_column(row, slots), slots)
    rows = out_ref.shape[0]
    shape = (rows, slots)
    target = iota(shape, 0) // 8
    place = iota(shape, 0) % 8
    total = jnp.zeros(out_ref.shape, F32)
    hit = (row == target) & (row != own) & (rank == place % CAP)
    for tap in range(taps):
        pick = jnp.where(hit & (place // CAP == tap), 1.0, 0.0).astype(BF16)
        total = total + dot_n(pick, cache_ref[tap])
    out_ref[...] = total


def pick_state_kernel(pos_ref, dest_ref, source_ref, state_ref, out_ref, from_ref, pick, count, sems):
    slots = state_ref.shape[0]
    buckets = out_ref.shape[0]
    own = pos_ref[0]

    def clear(i, carry):
        pick[i] = 0
        count[i] = 0
        return carry

    lax.fori_loop(0, buckets, clear, 0)
    peers = buckets // CAP

    def plan(s, carry):
        target = dest_ref[s]
        leaving = target != own
        source = source_ref[s]
        arriving = source != own
        from_ref[s] = jnp.where(leaving, -2, -1)

        @pl.when(leaving)
        def _():
            rank = count[target]
            pick[target * CAP + jnp.minimum(rank, CAP - 1)] = s
            count[target] = rank + 1

        @pl.when(arriving)
        def _():
            rank = count[peers + source]
            from_ref[s] = source * CAP + jnp.minimum(rank, CAP - 1)
            count[peers + source] = rank + 1

        return carry

    lax.fori_loop(0, slots, plan, 0)
    for b in range(buckets):
        pltpu.make_async_copy(state_ref.at[pick[b]], out_ref.at[b], sems.at[b]).start()
    for b in range(buckets):
        pltpu.make_async_copy(state_ref.at[pick[b]], out_ref.at[b], sems.at[b]).wait()


def conv_steps(window, taps_ref, bias, steps):
    taps = taps_ref[...].astype(F32)
    outs = []
    for t in range(steps):
        total = bias
        for k in range(taps.shape[0]):
            total = total + taps[k : k + 1, :] * window[t + k]
        outs.append(jax.nn.silu(total).astype(BF16))
    return outs


def main_kernel(pos_ref, dest_ref, active_ref, x_ref, cache_ref, taps_ref, bias_ref, proj_ref,
                conv_ref, cache_out_ref, a0, a1, a2, a3, b0, b1, b2, b3, mix, low):
    steps, slots, width = x_ref.shape
    taps = cache_ref.shape[0]
    rank_width = width
    own = pos_ref[0]
    dest = as_column(dest_ref[...], slots)
    alive = as_column(active_ref[...], slots)
    step = 16
    for r in range(0, slots, step):
        rows = slice(r, r + step)
        keep = [cache_ref[j, rows, :] for j in range(taps)]
        new = [x_ref[t, rows, :] for t in range(steps)]
        outs = conv_steps([v.astype(F32) for v in keep + new], taps_ref, bias_ref[...], steps)
        for t in range(steps):
            conv_ref[t, rows, :] = outs[t]
        on = alive[rows, :] == 1
        gone = dest[rows, :] != own
        for j in range(taps):
            old = jnp.where(gone, 0.0, keep[j].astype(F32))
            cache_out_ref[j, rows, :] = jnp.where(on, new[j].astype(F32), old).astype(BF16)
    lhs = conv_ref[...].reshape(steps * slots, width)
    mix[...] = dot_t(lhs, proj_ref[0:rank_width, :])
    rest = proj_ref.shape[0] - rank_width
    low[:, 0:rest] = dot_t(lhs, proj_ref[rank_width:, :])
    quarter = slots // 2 // SIDE
    for half, outs in ((0, (a0, a1, a2, a3)), (1, (b0, b1, b2, b3))):
        for d in range(SIDE):
            q = lax.rem(pos_ref[1 + half] + d, SIDE)
            out = outs[d]
            out[steps * quarter :, :] = jnp.zeros((8, width), F32)
            for t in range(steps):
                start = pl.multiple_of(t * slots + half * (slots // 2) + q * quarter, quarter)
                out[t * quarter : (t + 1) * quarter, :] = mix[pl.ds(start, quarter), :]
                for g in range(quarter // 8):
                    lane = 32 * (t * (quarter // 8) + g)
                    out[steps * quarter :, lane : lane + rest] = low[pl.ds(start + 8 * g, 8), 0:rest]


def merge_kernel(pos_ref, source_ref, got_ref, x_ref, taps_ref, bias_ref, proj_ref,
                 a0, a1, a2, a3, b0, b1, b2, b3, conv_ref, to_x, to_y):
    steps, slots, width = x_ref.shape
    own = pos_ref[0]
    row = source_ref[...]
    rank = ranks_row(row, as_column(row, slots), slots)
    peers = got_ref.shape[0] // 8
    buckets = peers * CAP
    shape = (buckets, slots)
    peer, order = iota(shape, 0) % peers, iota(shape, 0) // peers
    hit = (row == peer) & (row != own) & (rank == order)
    pick = jnp.where(hit, 1.0, 0.0).astype(BF16)
    got = got_ref[...].astype(BF16)
    shape = (buckets, got.shape[0])
    peer, order = iota(shape, 0) % peers, iota(shape, 0) // peers
    window = []
    for j in range(taps_ref.shape[0] - 1):
        place = peer * 8 + j * CAP + order
        window.append(dot_n(jnp.where(iota(shape, 1) == place, 1.0, 0.0).astype(BF16), got))
    for t in range(steps):
        window.append(dot_n(pick, x_ref[t]))
    outs = conv_steps(window, taps_ref, bias_ref[...], steps)
    for t in range(steps):
        conv_ref[t * buckets : (t + 1) * buckets, :] = outs[t]
    lhs = conv_ref[...]
    mix = dot_t(lhs, proj_ref[0:width, :])
    low = dot_t(lhs, proj_ref[width:, :])
    rest = low.shape[1]
    half = steps * peers
    for part, out, pieces in ((0, to_x, (b0, b1, b2, b3)), (1, to_y, (a0, a1, a2, a3))):
        total = pieces[0][...] + pieces[1][...] + pieces[2][...] + pieces[3][...]
        out[0:half, :] = total[0:half, :]
        out[2 * half :, :] = total[half:, :]
        for t in range(steps):
            start = t * buckets + part * peers
            out[half + t * peers : half + (t + 1) * peers, :] = mix[start : start + peers, :]
            for g in range(peers // 8):
                lane = 32 * ((steps + t) * (peers // 8) + g)
                out[2 * half :, lane : lane + rest] = low[start + 8 * g : start + 8 * g + 8, :]


def scan_kernel(pos_ref, from_ref, source_ref, active_ref, x0, x1, x2, x3, y0, y1, y2, y3,
                conv_ref, conv_arr_ref, z_ref, dtw_ref, dtb_ref, rate_ref, gain_ref, state_ref, got_ref,
                gated_ref, out_ref, rank_s, low_s, step_s, conv_s, alive_s, rate_s, arr_s, state_s, in_sems, out_sems):
    steps, slots, width = conv_ref.shape
    states = rate_ref.shape[0]
    block = slots // in_sems.shape[0]

    def prepare():
        rate_s[...] = rate_ref[...] * (-1.0 / math.log(2.0))
        quarter = slots // 2 // SIDE
        half = steps * quarter
        groups = quarter // 8
        peers = got_ref.shape[0] // states // CAP
        buckets = peers * CAP
        rest = 2 * states
        for axis, pieces in ((0, (x0, x1, x2, x3)), (1, (y0, y1, y2, y3))):
            for d in range(SIDE):
                q = lax.rem(pos_ref[1 + axis] + (SIDE - d), SIDE)
                for t in range(steps):
                    start = pl.multiple_of(t * slots + axis * (slots // 2) + q * quarter, quarter)
                    rank_s[pl.ds(start, quarter), :] = pieces[d][t * quarter : (t + 1) * quarter, :].astype(BF16)
                    for g in range(groups):
                        lane = 32 * (t * groups + g)
                        low_s[pl.ds(start + 8 * g, 8), 0:rest] = pieces[d][2 * half :, lane : lane + rest]
        row = source_ref[...]
        col = as_column(row, slots)
        rank = ranks_col(row, col, slots)
        alive = as_column(active_ref[...], slots) == 1
        alive_s[...] = jnp.broadcast_to(jnp.where(alive, 1.0, 0.0), alive_s.shape)
        arriving = col != pos_ref[0]
        shape = (slots, buckets)
        hit = arriving & (col == iota(shape, 1) % peers) & (rank == iota(shape, 1) // peers)
        pick = jnp.where(hit, 1.0, 0.0)
        pick_low = pick.astype(BF16)
        total_x = x0[half:, :] + x1[half:, :] + x2[half:, :] + x3[half:, :]
        total_y = y0[half:, :] + y1[half:, :] + y2[half:, :] + y3[half:, :]
        for t in range(steps):
            rows = slice(t * slots, (t + 1) * slots)
            part = slice(t * peers, (t + 1) * peers)
            arr = jnp.concatenate([total_y[part, :], total_x[part, :]], axis=0).astype(BF16)
            rank_s[rows, :] = jnp.where(arriving, dot_n(pick_low, arr), rank_s[rows, :].astype(F32)).astype(BF16)
            for g in range(peers // 8):
                lane = 32 * ((steps + t) * (peers // 8) + g)
                arr_s[8 * g : 8 * g + 8, 0:rest] = total_y[half:, lane : lane + rest]
                arr_s[peers + 8 * g : peers + 8 * g + 8, 0:rest] = total_x[half:, lane : lane + rest]
            low_arr = jnp.dot(pick, arr_s[:, 0:rest], precision=lax.Precision.HIGHEST, preferred_element_type=F32)
            low_s[rows, 0:rest] = jnp.where(arriving, low_arr, low_s[rows, 0:rest])
            conv_arr = dot_n(pick_low, conv_arr_ref[t * buckets : (t + 1) * buckets, :])
            conv_s[rows, :] = jnp.where(arriving, conv_arr, conv_ref[t].astype(F32))
            raw = dot_n(rank_s[rows, :], dtw_ref[...]) + dtb_ref[...]
            soft = jnp.maximum(raw, 0.0) + jnp.log1p(jnp.exp(-jnp.abs(raw)))
            step_s[rows, :] = jnp.where(alive, soft, 0.0)

    tiles = width // 128

    def load(i, l):
        rows = pl.ds(i * block * states, block * states)
        return pltpu.make_async_copy(state_ref.at[rows, pl.ds(l * 128, 128)], state_s.at[l, rows], in_sems.at[i, l])

    def store(i, l):
        rows = pl.ds(i * block * states, block * states)
        return pltpu.make_async_copy(state_s.at[l, rows], out_ref.at[rows, pl.ds(l * 128, 128)], out_sems.at[i, l])

    for i in range(slots // block):
        for l in range(tiles):
            load(i, l).start()
    prepare()

    def group(base):
        for i in range(8):
            source = from_ref[base + i]
            here = pl.ds(pl.multiple_of((base + i) * states, states), states)

            @pl.when(source == -2)
            def _():
                for l in range(tiles):
                    state_s[l, here, :] = jnp.zeros((states, 128), F32)

            @pl.when(source >= 0)
            def _():
                there = pl.ds(pl.multiple_of(source * states, states), states)
                for l in range(tiles):
                    state_s[l, here, :] = got_ref[there, l * 128 : (l + 1) * 128]

        dts, dxs, lows, accs = [], [], [], []
        for t in range(steps):
            rows = pl.ds(pl.multiple_of(t * slots + base, 8), 8)
            lows.append(low_s[rows, :])
            for l in range(tiles):
                lanes = slice(l * 128, (l + 1) * 128)
                dt = step_s[rows, lanes]
                cv = conv_s[rows, lanes]
                dts.append(dt)
                dxs.append(dt * cv)
                accs.append(gain_ref[:, lanes] * cv)
        for n in range(states):
            place = pl.ds(base * states + n, 8, stride=states)
            gives = [jnp.broadcast_to(low[:, n : n + 1], (8, 128)) for low in lows]
            takes = [jnp.broadcast_to(low[:, states + n : states + n + 1], (8, 128)) for low in lows]
            for l in range(tiles):
                st = state_s[l, place, :]
                rate = rate_s[n : n + 1, l * 128 : (l + 1) * 128]
                for t in range(steps):
                    k = t * tiles + l
                    st = jnp.exp2(dts[k] * rate) * st + dxs[k] * gives[t]
                    accs[k] = accs[k] + st * takes[t]
                state_s[l, place, :] = st
        return accs

    def pair(i, carry):
        base = pl.multiple_of(i * 16, 16)
        accs = [group(base), group(pl.multiple_of(base + 8, 8))]
        on = alive_s[pl.ds(base, 16), :] > 0.5
        for t in range(steps):
            for l in range(tiles):
                lanes = slice(l * 128, (l + 1) * 128)
                gate = jax.nn.silu(z_ref[t, pl.ds(base, 16), lanes].astype(F32))
                value = jnp.concatenate([accs[0][t * tiles + l], accs[1][t * tiles + l]], axis=0) * gate
                gated_ref[t, pl.ds(base, 16), lanes] = jnp.where(on, value, 0.0).astype(BF16)
        return carry

    def chunk(i, carry):
        for l in range(tiles):
            load(i, l).wait()
        lax.fori_loop(i * (block // 16), (i + 1) * (block // 16), pair, 0)
        for l in range(tiles):
            store(i, l).start()
        return carry

    lax.fori_loop(0, slots // block, chunk, 0)
    for i in range(slots // block):
        for l in range(tiles):
            store(i, l).wait()


def on_device(projected, conv_weight, conv_bias, xproj_weight, dtproj_weight, dt_bias, a_rate, skip_gain,
              ssm_state, conv_cache, send_dest, recv_source, active):
    steps, slots, _, width = projected.shape
    rank_width = dtproj_weight.shape[0]
    states = a_rate.shape[0]
    taps = conv_weight.shape[0]
    peers = lax.axis_size("req")
    buckets = peers * CAP
    place = lax.axis_index("wa")
    pos = jnp.stack([lax.axis_index("req"), place // SIDE, place % SIDE]).astype(jnp.int32)
    send_row, recv_row, active_row = (v.reshape(1, slots) for v in (send_dest, recv_source, active))
    bias, dt_row, gain = (v.reshape(1, width) for v in (conv_bias, dt_bias, skip_gain))
    cache = jnp.transpose(conv_cache, (1, 0, 2))
    proj = jnp.transpose(xproj_weight, (1, 0))
    x_part = projected[:, :, 0]
    z_part = projected[:, :, 1]
    sds = jax.ShapeDtypeStruct

    out_cache = pl.pallas_call(
        pick_cache_kernel,
        out_shape=sds((peers * 8, width), F32),
        in_specs=[SM, VM, VM],
        out_specs=VM,
        compiler_params=pltpu.CompilerParams(vmem_limit_bytes=12 * MIB),
        name="pick_cache",
    )(pos, send_row, cache)
    got_cache = lax.all_to_all(
        out_cache.reshape(peers, 8, width), "req", split_axis=0, concat_axis=0, tiled=True
    ).reshape(peers * 8, width)

    out_state, came_from = pl.pallas_call(
        pick_state_kernel,
        out_shape=(sds((buckets, states, width), F32), sds((slots,), jnp.int32)),
        in_specs=[SM, SM, SM, HB],
        out_specs=(HB, SM),
        scratch_shapes=[
            pltpu.SMEM((buckets,), jnp.int32),
            pltpu.SMEM((buckets,), jnp.int32),
            pltpu.SemaphoreType.DMA((buckets,)),
        ],
        compiler_params=pltpu.CompilerParams(vmem_limit_bytes=4 * MIB),
        name="pick_state",
    )(pos, send_dest, recv_source, ssm_state)
    got_state = lax.all_to_all(out_state, "req", split_axis=0, concat_axis=0, tiled=True)

    half = steps * (slots // 2 // SIDE)
    main = pl.pallas_call(
        main_kernel,
        out_shape=(
            sds((steps, slots, width), BF16),
            sds((taps - 1, slots, width), BF16),
        )
        + (sds((half + 8, width), F32),) * (2 * SIDE),
        in_specs=[SM] + [VM] * 7,
        out_specs=(VM,) * (2 + 2 * SIDE),
        scratch_shapes=[pltpu.VMEM((steps * slots, width), F32), pltpu.VMEM((steps * slots, 128), F32)],
        compiler_params=pltpu.CompilerParams(vmem_limit_bytes=24 * MIB),
        name="conv_project",
    )(pos, send_row, active_row, x_part, cache, conv_weight, bias, proj)
    conv_main, cache_out = main[0], main[1]
    own_a, own_b = main[2 : 2 + SIDE], main[2 + SIDE :]
    piece_a = [own_a[0]] + [lax.ppermute(own_a[d], "wa", shift(0, d)) for d in range(1, SIDE)]
    piece_b = [own_b[0]] + [lax.ppermute(own_b[d], "wa", shift(1, d)) for d in range(1, SIDE)]

    conv_arr, to_x, to_y = pl.pallas_call(
        merge_kernel,
        out_shape=(
            sds((steps * buckets, width), BF16),
            sds((2 * half + 8, width), F32),
            sds((2 * half + 8, width), F32),
        ),
        in_specs=[SM] + [VM] * 14,
        out_specs=(VM,) * 3,
        compiler_params=pltpu.CompilerParams(vmem_limit_bytes=16 * MIB),
        name="merge_arrivals",
    )(pos, recv_row, got_cache, x_part, conv_weight, bias, proj, *piece_a, *piece_b)

    def summed(value, axis):
        others = [lax.ppermute(value, "wa", shift(axis, d)) for d in range(1, SIDE)]
        return value + others[0] + others[1] + others[2]

    from_y = summed(to_y, 1)
    from_x = summed(to_x, 0)
    last_x = [from_y] + [lax.ppermute(from_y, "wa", shift(0, d)) for d in range(1, SIDE)]
    last_y = [from_x] + [lax.ppermute(from_x, "wa", shift(1, d)) for d in range(1, SIDE)]

    gated_out, state_out = pl.pallas_call(
        scan_kernel,
        out_shape=(sds((steps, slots, width), BF16), sds((slots * states, width), F32)),
        in_specs=[SM, SM] + [VM] * 17 + [HB, VM],
        out_specs=(VM, HB),
        scratch_shapes=[
            pltpu.VMEM((steps * slots, width), BF16),
            pltpu.VMEM((steps * slots, 128), F32),
            pltpu.VMEM((steps * slots, width), F32),
            pltpu.VMEM((steps * slots, width), F32),
            pltpu.VMEM((slots, 128), F32),
            pltpu.VMEM((states, width), F32),
            pltpu.VMEM((buckets, 128), F32),
            pltpu.VMEM((width // 128, slots * states, 128), F32),
            pltpu.SemaphoreType.DMA((4, width // 128)),
            pltpu.SemaphoreType.DMA((4, width // 128)),
        ],
        compiler_params=pltpu.CompilerParams(vmem_limit_bytes=24 * MIB),
        name="scan",
    )(
        pos, came_from, recv_row, active_row, *last_x, *last_y, conv_main, conv_arr, z_part,
        dtproj_weight, dt_row, a_rate, gain, ssm_state.reshape(slots * states, width),
        got_state.reshape(buckets * states, width),
    )
    return (
        gated_out,
        state_out.reshape(slots, states, width),
        jnp.transpose(cache_out, (1, 0, 2)),
    )


def solution(mesh):
    return jax.shard_map(
        on_device,
        mesh=mesh,
        in_specs=(
            P(None, "req", None, "wa"),
            P(None, "wa"),
            P("wa"),
            P("wa", None),
            P(None, "wa"),
            P("wa"),
            P(None, "wa"),
            P("wa"),
            P("req", None, "wa"),
            P("req", None, "wa"),
            P("req"),
            P("req"),
            P("req"),
        ),
        out_specs=(P(None, "req", "wa"), P("req", None, "wa"), P("req", None, "wa")),
        check_vma=False,
    )
```

time: 170 us -> 104 us (0.61)
  waiting for transfers between devices: 86 us -> 18.5 us
  starting transfers between devices: 14.1 us -> 47.3 us
  other arithmetic: 25.5 us -> 0.2 us
  Pallas kernels: 0 us -> 21.5 us
  between operations: 14.5 us -> 1.08 us
  matrix products: 8.43 us -> 0 us
  local copies, waits for them, and re-layouts: 21.2 us -> 15.1 us
    psum x1 -> x0, waiting for transfers between devices: 84.2 us -> none  [on_device(): lax.psum(jnp.dot(conv_now, xproj_weight, preferred_element_type=jnp.float...]
    ppermute x0 -> x18, starting transfers between devices: none -> 32.3 us  [the longest x3 10.6 us: on_device(): lax.ppermute(from_x, 'wa', shift(1, d))]
    pallas_call x0 -> x5, Pallas kernels: none -> 21.5 us  [the longest x1 11.6 us: on_device(): pl.pallas_call(scan_kernel, out_shape=(sds((steps, slots, width), BF16),...]
    ppermute x0 -> x18, waiting for transfers between devices: none -> 17.5 us  [the longest x6 7.74 us: summed(): others = [lax.ppermute(value, 'wa', shift(axis, d)) for d in range(1, SIDE)]]
    reduce_sum x5 -> x0, other arithmetic: 14.8 us -> none  [the longest x2 12.3 us: on_device(): jnp.sum(c_part[:, :, None] * state, axis=1)]
    unnamed x54, local copies, waits for them, and re-layouts: 1 us -> 14 us
    gather x4 -> x0, local copies, waits for them, and re-layouts: 9.83 us -> none  [the longest x1 3.77 us: on_device(): out_state = jnp.where(filled, ssm_state[picked], jnp.float32(0.0))]
    dot_general x6 -> x0, matrix products: 8.43 us -> none  [the longest x3 5.4 us: on_device(): jnp.dot(rank_part, dtproj_weight, preferred_element_type=jnp.float32)]
  transfers between devices with their start and end apart: 3 -> 20, of which waited for: 2 -> 11; matrix products, arithmetic and copies ran while one was open for 15% -> 1% of each run, Pallas kernels for 0% -> 8%
where the time goes in v1:
time: 104 us
  starting transfers between devices  47.3 us (45%)
  Pallas kernels  21.5 us (21%)
  waiting for transfers between devices  18.5 us (18%)
  local copies, waits for them, and re-layouts  15.1 us (15%)
  between operations  1.08 us (1%)
    unnamed x54, local copies, waits for them, and re-layouts  14 us
    pallas_call x1, Pallas kernels, on_device(): pl.pallas_call(scan_kernel, out_shape=(sds((steps, slots, width), BF16),...  11.6 us
    ppermute x3, starting transfers between devices, on_device(): lax.ppermute(from_x, 'wa', shift(1, d))  10.6 us
    all_to_all x1, starting transfers between devices, on_device(): lax.all_to_all(out_cache.reshape(peers, 8, width), 'req', split_axis=0, c...  8.59 us
    ppermute x6, waiting for transfers between devices, summed(): others = [lax.ppermute(value, 'wa', shift(axis, d)) for d in range(1, SIDE)]  7.74 us
    ppermute x6, starting transfers between devices, summed(): others = [lax.ppermute(value, 'wa', shift(axis, d)) for d in range(1, SIDE)]  7.29 us
    all_to_all x1, starting transfers between devices, on_device(): lax.all_to_all(out_state, 'req', split_axis=0, concat_axis=0, tiled=True)  6.34 us
    ppermute x3, waiting for transfers between devices, on_device(): lax.ppermute(from_x, 'wa', shift(1, d))  6.23 us
  transfers between devices with their start and end apart: 20, of which 11 were waited for; matrix products, arithmetic and copies ran while one was open for 1% of the time, Pallas kernels for 8%

profile of v1, /device:TPU:32, one launch (start us, length us, event | category | flops | bytes accessed | tf_op | source)
XLA Modules:
  0.0 103.6 jit_solution(14523365473020610094)
XLA Ops:
  2.4 1.6 %pick_cache.1 = f32[128,512]{1,0:T(8,128)} custom-call(s32[3]{0:T(128)S(1)} %pad_add_fusion.pos_ref, s32[1,128]{1,0:T(1,128)S(1)} %bitcast.35, bf16[3,128,512]{2,1,0:T(8,128)(2,1)S(1)} %bitcast.30), custom_call_target="tpu_custom_call" | custom-call | tf_op jit(solution)/shard_map/pick_cache/pallas_call | solution.py:360
  4.0 8.6 %all-to-all-start = ((f32[16,8,512]{2,1,0:T(8,128)}), f32[16,8,512]{2,1,0:T(8,128)S(1)}, u32[]{:S(2)}, u32[]{:S(2)}) async-start(f32[16,8,512]{2,1,0:T(8,128)} %bitcast.7), calls=%async_computation | async-start | bytes 524288 | tf_op jit(solution)/shard_map/all_to_all | solution.py:368
  12.6 2.2 %copy-done = f32[128,16,512]{2,1,0:T(8,128)S(1)} copy-done((f32[128,16,512]{2,1,0:T(8,128)S(1)}, f32[128,16,512]{2,1,0:T(8,128)}, u32[]{:S(2)}) %copy-start) | copy-done | bytes 4194328
  16.1 5.0 %pick_state.1 = (f32[32,16,512]{2,1,0:T(8,128)}, s32[128]{0:T(128)S(1)}) custom-call(s32[3]{0:T(128)S(1)} %pad_add_fusion.pos_ref, s32[128]{0:T(128)S(1)} %copy-done.18, s32[128]{0:T(128)S(1)} %copy-done.20, f32[128,16,512]{2,1,0:T(8,128)S(1)} %copy-done), custom_call_target="tpu_custom_call" | custom-call | tf_op jit(solution)/shard_map/pick_state/pallas_call | solution.py:372
  22.2 6.3 %all-to-all-start.1 = ((f32[32,16,512]{2,1,0:T(8,128)}), f32[32,16,512]{2,1,0:T(8,128)S(1)}, u32[]{:S(2)}, u32[]{:S(2)}) async-start(f32[32,16,512]{2,1,0:T(8,128)} %get-tuple-element.33), calls=%async_computation.1 | async-start | bytes 2097152 | tf_op jit(solution)/shard_map/all_to_all | solution.py:385
  29.8 2.2 %conv_project.1 = (bf16[3,128,512]{2,1,0:T(8,128)(2,1)S(1)}, bf16[3,128,512]{2,1,0:T(8,128)(2,1)}, f32[56,512]{1,0:T(8,128)S(1)}, f32[56,512]{1,0:T(8,128)S(1)},...) custom-call(s32[3]{0:T(128)S(1)} %pad_add_fusion.pos_ref, ...), custom_call_target="tpu_custom_call" | custom-call | tf_op jit(solution)/shard_map/conv_project/pallas_call | solution.py:388
  32.0 1.5 %collective-permute-start = (f32[56,512]{1,0:T(8,128)S(1)}, f32[56,512]{1,0:T(8,128)S(1)}, u32[]{:S(2)}, u32[]{:S(2)}) collective-permute-start(f32[56,512]{1,0:T(8,128)S(1)} %get-tuple-element.22), channel_id=1, source_target_pairs={{0,4},{1,5},{2,6},{3,7},{4,8},{5,9},{6,10},{7,11},{8,12},{9,13},{1... | collective-permute-start | bytes 344072 | tf_op jit(solution)/shard_map/ppermute | solution.py:403
  33.5 2.7 %collective-permute-start.1 = (f32[56,512]{1,0:T(8,128)S(1)}, f32[56,512]{1,0:T(8,128)S(1)}, u32[]{:S(2)}, u32[]{:S(2)}) collective-permute-start(f32[56,512]{1,0:T(8,128)S(1)} %get-tuple-element.23), channel_id=1, source_target_pairs={{0,8},{1,9},{2,10},{3,11},{4,12},{5,13},{6,14},{7,15},{8,0},{9,1},... | collective-permute-start | bytes 344072 | tf_op jit(solution)/shard_map/ppermute | solution.py:403
  36.3 1.4 %collective-permute-start.2 = (f32[56,512]{1,0:T(8,128)S(1)}, f32[56,512]{1,0:T(8,128)S(1)}, u32[]{:S(2)}, u32[]{:S(2)}) collective-permute-start(f32[56,512]{1,0:T(8,128)S(1)} %get-tuple-element.24), channel_id=1, source_target_pairs={{0,12},{1,13},{2,14},{3,15},{4,0},{5,1},{6,2},{7,3},{8,4},{9,5},{1... | collective-permute-start | bytes 344072 | tf_op jit(solution)/shard_map/ppermute | solution.py:403
  37.7 1.6 %collective-permute-start.3 = (f32[56,512]{1,0:T(8,128)S(1)}, f32[56,512]{1,0:T(8,128)S(1)}, u32[]{:S(2)}, u32[]{:S(2)}) collective-permute-start(f32[56,512]{1,0:T(8,128)S(1)} %get-tuple-element.26), channel_id=1, source_target_pairs={{0,1},{1,2},{2,3},{3,0},{4,5},{5,6},{6,7},{7,4},{8,9},{9,10},{10,1... | collective-permute-start | bytes 344072 | tf_op jit(solution)/shard_map/ppermute | solution.py:404
  39.3 2.9 %collective-permute-start.4 = (f32[56,512]{1,0:T(8,128)S(1)}, f32[56,512]{1,0:T(8,128)S(1)}, u32[]{:S(2)}, u32[]{:S(2)}) collective-permute-start(f32[56,512]{1,0:T(8,128)S(1)} %get-tuple-element.27), channel_id=1, source_target_pairs={{0,2},{1,3},{2,0},{3,1},{4,6},{5,7},{6,4},{7,5},{8,10},{9,11},{10,... | collective-permute-start | bytes 344072 | tf_op jit(solution)/shard_map/ppermute | solution.py:404
  42.2 1.3 %collective-permute-start.5 = (f32[56,512]{1,0:T(8,128)S(1)}, f32[56,512]{1,0:T(8,128)S(1)}, u32[]{:S(2)}, u32[]{:S(2)}) collective-permute-start(f32[56,512]{1,0:T(8,128)S(1)} %get-tuple-element.28), channel_id=1, source_target_pairs={{0,3},{1,0},{2,1},{3,2},{4,7},{5,4},{6,5},{7,6},{8,11},{9,8},{10,9... | collective-permute-start | bytes 344072 | tf_op jit(solution)/shard_map/ppermute | solution.py:404
  44.6 2.3 %collective-permute-done.4.b2 = f32[56,512]{1,0:T(8,128)S(1)} collective-permute-done((f32[56,512]{1,0:T(8,128)S(1)}, f32[56,512]{1,0:T(8,128)S(1)}, u32[]{:S(2)}, u32[]{:S(2)}) %collective-permute-start.4) | collective-permute-done | bytes 114720 | tf_op jit(solution)/shard_map/ppermute | solution.py:404
  47.0 1.1 %merge_arrivals.1 = (bf16[96,512]{1,0:T(8,128)(2,1)S(1)}, f32[104,512]{1,0:T(8,128)S(1)}, f32[104,512]{1,0:T(8,128)S(1)}) custom-call(s32[3]{0:T(128)S(1)} %pad_add_fusion.pos_ref, s32[1,128]{1,0:T(1,128)S(1)} %bitcast.37, f32[128,512]{1,0:T(8,128)S(1)} %bitcast.32, bf16[3,128,512]{2,1,0:T(8,128)(2,1)S(1)} %bitcast.26, bf16[4,512]{1,0:T(4,128)(2,1)S(1)} %copy-done.15, ...), custom_call_target="tpu_custom_call" | custom-call | tf_op jit(solution)/shard_map/merge_arrivals/pallas_call | solution.py:406
  48.2 2.7 %collective-permute-start.8 = (f32[104,512]{1,0:T(8,128)S(1)}, f32[104,512]{1,0:T(8,128)S(1)}, u32[]{:S(2)}, u32[]{:S(2)}) collective-permute-start(f32[104,512]{1,0:T(8,128)S(1)} %get-tuple-element.29), channel_id=1, source_target_pairs={{0,3},{1,0},{2,1},{3,2},{4,7},{5,4},{6,5},{7,6},{8,11},{9,8},{10,9... | collective-permute-start | bytes 638984 | tf_op jit(solution)/shard_map/ppermute | solution.py:420
  52.4 2.4 %collective-permute-start.13 = (f32[104,512]{1,0:T(8,128)S(1)}, f32[104,512]{1,0:T(8,128)S(1)}, u32[]{:S(2)}, u32[]{:S(2)}) collective-permute-start(f32[104,512]{1,0:T(8,128)S(1)} %get-tuple-element.30), channel_id=1, source_target_pairs={{0,8},{1,9},{2,10},{3,11},{4,12},{5,13},{6,14},{7,15},{8,0},{9,1},... | collective-permute-start | bytes 638984 | tf_op jit(solution)/shard_map/ppermute | solution.py:420
  54.8 4.3 %collective-permute-done.8 = f32[104,512]{1,0:T(8,128)S(1)} collective-permute-done((f32[104,512]{1,0:T(8,128)S(1)}, f32[104,512]{1,0:T(8,128)S(1)}, u32[]{:S(2)}, u32[]{:S(2)}) %collective-permute-start.8) | collective-permute-done | bytes 213024 | tf_op jit(solution)/shard_map/ppermute | solution.py:420
  60.6 1.9 %collective-permute-done.6 = f32[104,512]{1,0:T(8,128)S(1)} collective-permute-done((f32[104,512]{1,0:T(8,128)S(1)}, f32[104,512]{1,0:T(8,128)S(1)}, u32[]{:S(2)}, u32[]{:S(2)}) %collective-permute-start.6) | collective-permute-done | bytes 213024 | tf_op jit(solution)/shard_map/ppermute | solution.py:420
  62.9 2.7 %collective-permute-start.10 = (f32[104,512]{1,0:T(8,128)S(1)}, f32[104,512]{1,0:T(8,128)S(1)}, u32[]{:S(2)}, u32[]{:S(2)}) collective-permute-start(f32[104,512]{1,0:T(8,128)S(1)} %add_add_fusion.1.x0), channel_id=1, source_target_pairs={{0,8},{1,9},{2,10},{3,11},{4,12},{5,13},{6,14},{7,15},{8,0},{9,1},... | collective-permute-start | bytes 638984 | tf_op jit(solution)/shard_map/ppermute | solution.py:425
  66.3 9.7 %collective-permute-start.17 = (f32[104,512]{1,0:T(8,128)S(1)}, f32[104,512]{1,0:T(8,128)S(1)}, u32[]{:S(2)}, u32[]{:S(2)}) collective-permute-start(f32[104,512]{1,0:T(8,128)S(1)} %add_add_fusion.y0), channel_id=1, source_target_pairs={{0,3},{1,0},{2,1},{3,2},{4,7},{5,4},{6,5},{7,6},{8,11},{9,8},{10,9... | collective-permute-start | bytes 638984 | tf_op jit(solution)/shard_map/ppermute | solution.py:426
  77.7 3.9 %collective-permute-done.17.y3 = f32[104,512]{1,0:T(8,128)S(1)} collective-permute-done((f32[104,512]{1,0:T(8,128)S(1)}, f32[104,512]{1,0:T(8,128)S(1)}, u32[]{:S(2)}, u32[]{:S(2)}) %collective-permute-start.17) | collective-permute-done | bytes 213024 | tf_op jit(solution)/shard_map/ppermute | solution.py:426
  84.1 1.2 %collective-permute-done.15.y1 = f32[104,512]{1,0:T(8,128)S(1)} collective-permute-done((f32[104,512]{1,0:T(8,128)S(1)}, f32[104,512]{1,0:T(8,128)S(1)}, u32[]{:S(2)}, u32[]{:S(2)}) %collective-permute-start.15) | collective-permute-done | bytes 213024 | tf_op jit(solution)/shard_map/ppermute | solution.py:426
  86.0 2.2 %copy-done.1 = f32[128,16,512]{2,1,0:T(8,128)S(1)} copy-done((f32[128,16,512]{2,1,0:T(8,128)S(1)}, f32[128,16,512]{2,1,0:T(8,128)}, u32[]{:S(2)}) %copy-start.1) | copy-done | bytes 4194328
  91.9 11.6 %scan.1 = (bf16[3,128,512]{2,1,0:T(8,128)(2,1)}, f32[2048,512]{1,0:T(8,128)}) custom-call(s32[3]{0:T(128)S(1)} %pad_add_fusion.pos_ref, s32[128]{0:T(128)S(1)} %get-tuple-element.20.from_ref, s32[1,128]{1,0:T(1,128)S(1)} %bitcast.38, s32[1,128]{1,0:T(1,128)S(1)} %bitcast.42, f32[104,512]{1,0:T(8,128)S(1)} %add_add_fusion.1.x0, f32[104,512]{1,0:T(8,128)S(1)} %copy-done.7, ...), custom_call_target="tpu_custom_call" | custom-call | tf_op jit(solution)/shard_map/scan/pallas_call | solution.py:428
  (79 shorter events, 19.1 us)
Async XLA Ops:
  4.0 18.2 %all-to-all-start = ((f32[16,8,512]{2,1,0:T(8,128)}), f32[16,8,512]{2,1,0:T(8,128)S(1)}, u32[]{:S(2)}, u32[]{:S(2)}) async-start(f32[16,8,512]{2,1,0:T(8,128)} %bitcast.7), calls=%async_computation | async-start | bytes 524288 | tf_op jit(solution)/shard_map/all_to_all | solution.py:368
  22.2 63.8 %all-to-all-start.1 = ((f32[32,16,512]{2,1,0:T(8,128)}), f32[32,16,512]{2,1,0:T(8,128)S(1)}, u32[]{:S(2)}, u32[]{:S(2)}) async-start(f32[32,16,512]{2,1,0:T(8,128)} %get-tuple-element.33), calls=%async_computation.1 | async-start | bytes 2097152 | tf_op jit(solution)/shard_map/all_to_all | solution.py:385
  29.7 56.3 %copy-start.5 = (bf16[512,512]{1,0:T(8,128)(2,1)S(1)}, bf16[512,512]{1,0:T(8,128)(2,1)}, u32[]{:S(2)}) copy-start(bf16[512,512]{1,0:T(8,128)(2,1)} %dtw_ref.1) | copy-start | bytes 1572868
  29.7 56.3 %copy-start.14 = (f32[16,512]{1,0:T(8,128)S(1)}, f32[16,512]{1,0:T(8,128)}, u32[]{:S(2)}) copy-start(f32[16,512]{1,0:T(8,128)} %rate_ref.1) | copy-start | bytes 98308
  29.7 56.3 %copy-start.22 = (f32[512]{0:T(512)S(1)}, f32[512]{0:T(512)}, u32[]{:S(2)}) copy-start(f32[512]{0:T(512)} %param.18) | copy-start | bytes 6148
  29.7 56.3 %copy-start.23 = (f32[512]{0:T(512)S(1)}, f32[512]{0:T(512)}, u32[]{:S(2)}) copy-start(f32[512]{0:T(512)} %param.20) | copy-start | bytes 6148
  32.0 10.1 %collective-permute-start = (f32[56,512]{1,0:T(8,128)S(1)}, f32[56,512]{1,0:T(8,128)S(1)}, u32[]{:S(2)}, u32[]{:S(2)}) collective-permute-start(f32[56,512]{1,0:T(8,128)S(1)} %get-tuple-element.22), channel_id=1, source_target_pairs={{0,4},{1,5},{2,6},{3,7},{4,8},{5,9},{6,10},{7,11},{8,12},{9,13},{1... | collective-permute-start | bytes 344072 | tf_op jit(solution)/shard_map/ppermute | solution.py:403
  33.5 10.0 %collective-permute-start.1 = (f32[56,512]{1,0:T(8,128)S(1)}, f32[56,512]{1,0:T(8,128)S(1)}, u32[]{:S(2)}, u32[]{:S(2)}) collective-permute-start(f32[56,512]{1,0:T(8,128)S(1)} %get-tuple-element.23), channel_id=1, source_target_pairs={{0,8},{1,9},{2,10},{3,11},{4,12},{5,13},{6,14},{7,15},{8,0},{9,1},... | collective-permute-start | bytes 344072 | tf_op jit(solution)/shard_map/ppermute | solution.py:403
  36.3 7.3 %collective-permute-start.2 = (f32[56,512]{1,0:T(8,128)S(1)}, f32[56,512]{1,0:T(8,128)S(1)}, u32[]{:S(2)}, u32[]{:S(2)}) collective-permute-start(f32[56,512]{1,0:T(8,128)S(1)} %get-tuple-element.24), channel_id=1, source_target_pairs={{0,12},{1,13},{2,14},{3,15},{4,0},{5,1},{6,2},{7,3},{8,4},{9,5},{1... | collective-permute-start | bytes 344072 | tf_op jit(solution)/shard_map/ppermute | solution.py:403
  37.7 6.9 %collective-permute-start.3 = (f32[56,512]{1,0:T(8,128)S(1)}, f32[56,512]{1,0:T(8,128)S(1)}, u32[]{:S(2)}, u32[]{:S(2)}) collective-permute-start(f32[56,512]{1,0:T(8,128)S(1)} %get-tuple-element.26), channel_id=1, source_target_pairs={{0,1},{1,2},{2,3},{3,0},{4,5},{5,6},{6,7},{7,4},{8,9},{9,10},{10,1... | collective-permute-start | bytes 344072 | tf_op jit(solution)/shard_map/ppermute | solution.py:404
  39.3 7.7 %collective-permute-start.4 = (f32[56,512]{1,0:T(8,128)S(1)}, f32[56,512]{1,0:T(8,128)S(1)}, u32[]{:S(2)}, u32[]{:S(2)}) collective-permute-start(f32[56,512]{1,0:T(8,128)S(1)} %get-tuple-element.27), channel_id=1, source_target_pairs={{0,2},{1,3},{2,0},{3,1},{4,6},{5,7},{6,4},{7,5},{8,10},{9,11},{10,... | collective-permute-start | bytes 344072 | tf_op jit(solution)/shard_map/ppermute | solution.py:404
  42.2 4.8 %collective-permute-start.5 = (f32[56,512]{1,0:T(8,128)S(1)}, f32[56,512]{1,0:T(8,128)S(1)}, u32[]{:S(2)}, u32[]{:S(2)}) collective-permute-start(f32[56,512]{1,0:T(8,128)S(1)} %get-tuple-element.28), channel_id=1, source_target_pairs={{0,3},{1,0},{2,1},{3,2},{4,7},{5,4},{6,5},{7,6},{8,11},{9,8},{10,9... | collective-permute-start | bytes 344072 | tf_op jit(solution)/shard_map/ppermute | solution.py:404
  48.2 11.0 %collective-permute-start.8 = (f32[104,512]{1,0:T(8,128)S(1)}, f32[104,512]{1,0:T(8,128)S(1)}, u32[]{:S(2)}, u32[]{:S(2)}) collective-permute-start(f32[104,512]{1,0:T(8,128)S(1)} %get-tuple-element.29), channel_id=1, source_target_pairs={{0,3},{1,0},{2,1},{3,2},{4,7},{5,4},{6,5},{7,6},{8,11},{9,8},{10,9... | collective-permute-start | bytes 638984 | tf_op jit(solution)/shard_map/ppermute | solution.py:420
  50.9 9.7 %collective-permute-start.7 = (f32[104,512]{1,0:T(8,128)S(1)}, f32[104,512]{1,0:T(8,128)S(1)}, u32[]{:S(2)}, u32[]{:S(2)}) collective-permute-start(f32[104,512]{1,0:T(8,128)S(1)} %get-tuple-element.29), channel_id=1, source_target_pairs={{0,2},{1,3},{2,0},{3,1},{4,6},{5,7},{6,4},{7,5},{8,10},{9,11},{10,... | collective-permute-start | bytes 638984 | tf_op jit(solution)/shard_map/ppermute | solution.py:420
  51.4 11.1 %collective-permute-start.6 = (f32[104,512]{1,0:T(8,128)S(1)}, f32[104,512]{1,0:T(8,128)S(1)}, u32[]{:S(2)}, u32[]{:S(2)}) collective-permute-start(f32[104,512]{1,0:T(8,128)S(1)} %get-tuple-element.29), channel_id=1, source_target_pairs={{0,1},{1,2},{2,3},{3,0},{4,5},{5,6},{6,7},{7,4},{8,9},{9,10},{10,1... | collective-permute-start | bytes 638984 | tf_op jit(solution)/shard_map/ppermute | solution.py:420
  52.2 13.4 %collective-permute-start.14 = (f32[104,512]{1,0:T(8,128)S(1)}, f32[104,512]{1,0:T(8,128)S(1)}, u32[]{:S(2)}, u32[]{:S(2)}) collective-permute-start(f32[104,512]{1,0:T(8,128)S(1)} %get-tuple-element.30), channel_id=1, source_target_pairs={{0,12},{1,13},{2,14},{3,15},{4,0},{5,1},{6,2},{7,3},{8,4},{9,5},{1... | collective-permute-start | bytes 638984 | tf_op jit(solution)/shard_map/ppermute | solution.py:420
  52.4 13.1 %collective-permute-start.13 = (f32[104,512]{1,0:T(8,128)S(1)}, f32[104,512]{1,0:T(8,128)S(1)}, u32[]{:S(2)}, u32[]{:S(2)}) collective-permute-start(f32[104,512]{1,0:T(8,128)S(1)} %get-tuple-element.30), channel_id=1, source_target_pairs={{0,8},{1,9},{2,10},{3,11},{4,12},{5,13},{6,14},{7,15},{8,0},{9,1},... | collective-permute-start | bytes 638984 | tf_op jit(solution)/shard_map/ppermute | solution.py:420
  59.1 7.1 %collective-permute-start.12 = (f32[104,512]{1,0:T(8,128)S(1)}, f32[104,512]{1,0:T(8,128)S(1)}, u32[]{:S(2)}, u32[]{:S(2)}) collective-permute-start(f32[104,512]{1,0:T(8,128)S(1)} %get-tuple-element.30), channel_id=1, source_target_pairs={{0,4},{1,5},{2,6},{3,7},{4,8},{5,9},{6,10},{7,11},{8,12},{9,13},{1... | collective-permute-start | bytes 638984 | tf_op jit(solution)/shard_map/ppermute | solution.py:420
  62.6 13.4 %collective-permute-start.11 = (f32[104,512]{1,0:T(8,128)S(1)}, f32[104,512]{1,0:T(8,128)S(1)}, u32[]{:S(2)}, u32[]{:S(2)}) collective-permute-start(f32[104,512]{1,0:T(8,128)S(1)} %add_add_fusion.1.x0), channel_id=1, source_target_pairs={{0,12},{1,13},{2,14},{3,15},{4,0},{5,1},{6,2},{7,3},{8,4},{9,5},{1... | collective-permute-start | bytes 638984 | tf_op jit(solution)/shard_map/ppermute | solution.py:425
  62.9 14.1 %collective-permute-start.10 = (f32[104,512]{1,0:T(8,128)S(1)}, f32[104,512]{1,0:T(8,128)S(1)}, u32[]{:S(2)}, u32[]{:S(2)}) collective-permute-start(f32[104,512]{1,0:T(8,128)S(1)} %add_add_fusion.1.x0), channel_id=1, source_target_pairs={{0,8},{1,9},{2,10},{3,11},{4,12},{5,13},{6,14},{7,15},{8,0},{9,1},... | collective-permute-start | bytes 638984 | tf_op jit(solution)/shard_map/ppermute | solution.py:425
  65.5 11.4 %collective-permute-start.9 = (f32[104,512]{1,0:T(8,128)S(1)}, f32[104,512]{1,0:T(8,128)S(1)}, u32[]{:S(2)}, u32[]{:S(2)}) collective-permute-start(f32[104,512]{1,0:T(8,128)S(1)} %add_add_fusion.1.x0), channel_id=1, source_target_pairs={{0,4},{1,5},{2,6},{3,7},{4,8},{5,9},{6,10},{7,11},{8,12},{9,13},{1... | collective-permute-start | bytes 638984 | tf_op jit(solution)/shard_map/ppermute | solution.py:425
  66.3 15.3 %collective-permute-start.17 = (f32[104,512]{1,0:T(8,128)S(1)}, f32[104,512]{1,0:T(8,128)S(1)}, u32[]{:S(2)}, u32[]{:S(2)}) collective-permute-start(f32[104,512]{1,0:T(8,128)S(1)} %add_add_fusion.y0), channel_id=1, source_target_pairs={{0,3},{1,0},{2,1},{3,2},{4,7},{5,4},{6,5},{7,6},{8,11},{9,8},{10,9... | collective-permute-start | bytes 638984 | tf_op jit(solution)/shard_map/ppermute | solution.py:426
  75.9 7.5 %collective-permute-start.16 = (f32[104,512]{1,0:T(8,128)S(1)}, f32[104,512]{1,0:T(8,128)S(1)}, u32[]{:S(2)}, u32[]{:S(2)}) collective-permute-start(f32[104,512]{1,0:T(8,128)S(1)} %add_add_fusion.y0), channel_id=1, source_target_pairs={{0,2},{1,3},{2,0},{3,1},{4,6},{5,7},{6,4},{7,5},{8,10},{9,11},{10,... | collective-permute-start | bytes 638984 | tf_op jit(solution)/shard_map/ppermute | solution.py:426
  75.9 9.3 %collective-permute-start.15 = (f32[104,512]{1,0:T(8,128)S(1)}, f32[104,512]{1,0:T(8,128)S(1)}, u32[]{:S(2)}, u32[]{:S(2)}) collective-permute-start(f32[104,512]{1,0:T(8,128)S(1)} %add_add_fusion.y0), channel_id=1, source_target_pairs={{0,1},{1,2},{2,3},{3,0},{4,5},{5,6},{6,7},{7,4},{8,9},{9,10},{10,1... | collective-permute-start | bytes 638984 | tf_op jit(solution)/shard_map/ppermute | solution.py:426
  (22 other events, 117.9 us)

commit v2 on v1

v2 whole, which is shorter than its diff:
```python
import math

import jax
import jax.numpy as jnp
from jax import lax
from jax.experimental import pallas as pl
from jax.experimental.pallas import tpu as pltpu
from jax.sharding import PartitionSpec as P

CAP = 2
SIDE = 4
MIB = 1 << 20
F32 = jnp.float32
BF16 = jnp.bfloat16
VM = pl.BlockSpec(memory_space=pltpu.VMEM)
SM = pl.BlockSpec(memory_space=pltpu.SMEM)
HB = pl.BlockSpec(memory_space=pltpu.HBM)


def shift(axis, amount):
    pairs = []
    for x in range(SIDE):
        for y in range(SIDE):
            tx, ty = (x + amount) % SIDE, y
            if axis == 1:
                tx, ty = x, (y + amount) % SIDE
            pairs.append((x * SIDE + y, tx * SIDE + ty))
    return pairs


def dot_t(lhs, rhs):
    return lax.dot_general(lhs, rhs, (((1,), (1,)), ((), ())), preferred_element_type=F32)


def dot_n(lhs, rhs):
    return jnp.dot(lhs, rhs, preferred_element_type=F32)


def iota(shape, dim):
    return lax.broadcasted_iota(jnp.int32, shape, dim)


def as_column(row, size):
    eye = iota((size, size), 0) == iota((size, size), 1)
    return jnp.sum(jnp.where(eye, jnp.broadcast_to(row, (size, size)), 0), axis=1, keepdims=True)


def ranks_row(row, col, size):
    earlier = (col == row) & (iota((size, size), 0) < iota((size, size), 1))
    return jnp.sum(jnp.where(earlier, 1, 0), axis=0, keepdims=True)


def ranks_col(row, col, size):
    earlier = (col == row) & (iota((size, size), 1) < iota((size, size), 0))
    return jnp.sum(jnp.where(earlier, 1, 0), axis=1, keepdims=True)


def fetch(pairs, sems):
    copies = [pltpu.make_async_copy(a, b, sems.at[i]) for i, (a, b) in enumerate(pairs)]
    for copy in copies:
        copy.start()
    return copies


def pick_cache_kernel(pos_ref, dest_hbm, source_hbm, cache_hbm, out_ref, plan_ref, dest_ref, source_ref, cache_ref, sems):
    copies = fetch(((dest_hbm, dest_ref), (source_hbm, source_ref), (cache_hbm, cache_ref)), sems)
    for copy in copies[:2]:
        copy.wait()
    taps, slots, _ = cache_ref.shape
    own = pos_ref[0]
    row = dest_ref[...]
    col = as_column(row, slots)
    rank = ranks_row(row, col, slots)
    rows = out_ref.shape[0]
    shape = (rows, slots)
    target = iota(shape, 0) // 8
    place = iota(shape, 0) % 8
    total = jnp.zeros(out_ref.shape, F32)
    copies[2].wait()
    hit = (row == target) & (row != own) & (rank == place % CAP)
    for tap in range(taps):
        pick = jnp.where(hit & (place // CAP == tap), 1.0, 0.0).astype(BF16)
        total = total + dot_n(pick, cache_ref[tap])
    out_ref[...] = total
    shape = (slots, slots)
    bucket = iota(shape, 1)
    hit = (col != own) & (col == bucket // CAP) & (ranks_col(row, col, slots) == bucket % CAP)
    plan_ref[0:1, :] = jnp.sum(jnp.where(hit, iota(shape, 0) + 1, 0), axis=0, keepdims=True) - 1
    row = source_ref[...]
    col = as_column(row, slots)
    hit = (col != own) & (col == bucket // CAP) & (ranks_col(row, col, slots) == bucket % CAP)
    plan_ref[1:2, :] = jnp.sum(jnp.where(hit, iota(shape, 0) + 1, 0), axis=0, keepdims=True) - 1


def pick_state_kernel(plan_ref, state_ref, out_hbm, out_ref, sems, out_sem):
    buckets, states, _ = out_ref.shape
    copies = []
    for b in range(buckets):
        rows = pl.ds(pl.multiple_of(jnp.maximum(plan_ref[0, b], 0) * states, states), states)
        copies.append(pltpu.make_async_copy(state_ref.at[rows], out_ref.at[b], sems.at[b]))
    for copy in copies:
        copy.start()
    for copy in copies:
        copy.wait()
    copy = pltpu.make_async_copy(out_ref, out_hbm, out_sem.at[0])
    copy.start()
    copy.wait()


def conv_steps(window, taps_ref, bias, steps):
    taps = taps_ref[...].astype(F32)
    outs = []
    for t in range(steps):
        total = bias
        for k in range(taps.shape[0]):
            total = total + taps[k : k + 1, :] * window[t + k]
        outs.append(jax.nn.silu(total).astype(BF16))
    return outs


def conv_kernel(pos_ref, dest_hbm, source_hbm, active_hbm, both_ref, cache_hbm, taps_hbm, bias_hbm,
                conv_ref, z_out, cache_out_ref, arr_ref, sems,
                dest_ref, source_ref, active_ref, cache_ref, taps_ref, bias_ref, in_sems):
    x_ref = both_ref.at[0]
    copies = fetch(
        ((dest_hbm, dest_ref), (source_hbm, source_ref), (active_hbm, active_ref), (cache_hbm, cache_ref),
         (taps_hbm, taps_ref), (bias_hbm, bias_ref)),
        in_sems,
    )
    gate_copy = pltpu.make_async_copy(both_ref.at[1], z_out, sems.at[0])
    gate_copy.start()
    for copy in copies:
        copy.wait()
    steps, slots, width = x_ref.shape
    taps = cache_ref.shape[0]
    own = pos_ref[0]
    dest = as_column(dest_ref[...], slots)
    alive = as_column(active_ref[...], slots)
    step = 16
    for r in range(0, slots, step):
        rows = slice(r, r + step)
        keep = [cache_ref[j, rows, :] for j in range(taps)]
        new = [x_ref[t, rows, :] for t in range(steps)]
        outs = conv_steps([v.astype(F32) for v in keep + new], taps_ref, bias_ref[...], steps)
        for t in range(steps):
            conv_ref[t, rows, :] = outs[t]
        on = alive[rows, :] == 1
        gone = dest[rows, :] != own
        for j in range(taps):
            old = jnp.where(gone, 0.0, keep[j].astype(F32))
            cache_out_ref[j, rows, :] = jnp.where(on, new[j].astype(F32), old).astype(BF16)
    buckets = arr_ref.shape[0] // steps
    row = source_ref[...]
    rank = ranks_row(row, as_column(row, slots), slots)
    shape = (buckets, slots)
    hit = (row == iota(shape, 0) // CAP) & (row != own) & (rank == iota(shape, 0) % CAP)
    pick = jnp.where(hit, 1.0, 0.0).astype(BF16)
    for t in range(steps):
        arr_ref[t * buckets : (t + 1) * buckets, :] = dot_n(pick, x_ref[t]).astype(BF16)
    gate_copy.wait()


def project_kernel(pos_ref, source_ref, got_ref, arr_ref, conv_ref, taps_ref, bias_ref, proj_ref,
                   conv_out, a0, a1, a2, a3, b0, b1, b2, b3, conv_s, mix, low, sems):
    steps, slots, width = conv_ref.shape
    buckets = arr_ref.shape[0] // steps
    got = got_ref[...].astype(BF16)
    shape = (buckets, got.shape[0])
    window = []
    for j in range(taps_ref.shape[0] - 1):
        place = (iota(shape, 0) // CAP) * 8 + j * CAP + iota(shape, 0) % CAP
        window.append(dot_n(jnp.where(iota(shape, 1) == place, 1.0, 0.0).astype(BF16), got))
    for t in range(steps):
        window.append(arr_ref[t * buckets : (t + 1) * buckets, :].astype(F32))
    outs = conv_steps(window, taps_ref, bias_ref[...], steps)
    row = source_ref[...]
    col = as_column(row, slots)
    rank = ranks_col(row, col, slots)
    arriving = col != pos_ref[0]
    shape = (slots, buckets)
    hit = arriving & (col == iota(shape, 1) // CAP) & (rank == iota(shape, 1) % CAP)
    pick = jnp.where(hit, 1.0, 0.0).astype(BF16)
    for t in range(steps):
        moved = dot_n(pick, outs[t])
        conv_s[t * slots : (t + 1) * slots, :] = jnp.where(arriving, moved, conv_ref[t].astype(F32)).astype(BF16)
    copy = pltpu.make_async_copy(conv_s, conv_out, sems.at[0])
    copy.start()
    lhs = conv_s[...]
    mix[...] = dot_t(lhs, proj_ref[0:width, :])
    rest = proj_ref.shape[0] - width
    low[:, 0:rest] = dot_t(lhs, proj_ref[width:, :])
    quarter = slots // 2 // SIDE
    for half, outs in ((0, (a0, a1, a2, a3)), (1, (b0, b1, b2, b3))):
        for d in range(SIDE):
            q = lax.rem(pos_ref[1 + half] + d, SIDE)
            out = outs[d]
            out[steps * quarter :, :] = jnp.zeros((8, width), F32)
            for t in range(steps):
                start = pl.multiple_of(t * slots + half * (slots // 2) + q * quarter, quarter)
                out[t * quarter : (t + 1) * quarter, :] = mix[pl.ds(start, quarter), :]
                for g in range(quarter // 8):
                    lane = 32 * (t * (quarter // 8) + g)
                    out[steps * quarter :, lane : lane + rest] = low[pl.ds(start + 8 * g, 8), 0:rest]
    copy.wait()


def prepare(pos_ref, active_ref, pieces_x, pieces_y, conv_ref, dtw_ref, dtb_ref,
            step_ref, conv_out_ref, low_ref, rank_s, wait):
    total, width = conv_ref.shape
    slots = active_ref.shape[1]
    steps = total // slots
    quarter = slots // 2 // SIDE
    half = steps * quarter
    groups = quarter // 8
    rest = 32
    for axis, pieces in ((0, pieces_x), (1, pieces_y)):
        for d in range(SIDE):
            q = lax.rem(pos_ref[1 + axis] + (SIDE - d), SIDE)
            for t in range(steps):
                start = pl.multiple_of(t * slots + axis * (slots // 2) + q * quarter, quarter)
                rank_s[pl.ds(start, quarter), :] = pieces[d][t * quarter : (t + 1) * quarter, :].astype(BF16)
                for g in range(groups):
                    lane = 32 * (t * groups + g)
                    low_ref[pl.ds(start + 8 * g, 8), 0:rest] = pieces[d][half:, lane : lane + rest]
    alive = as_column(active_ref[...], slots) == 1
    wait()
    for t in range(steps):
        rows = slice(t * slots, (t + 1) * slots)
        conv_out_ref[rows, :] = conv_ref[rows, :].astype(F32)
        raw = dot_n(rank_s[rows, :], dtw_ref[...]) + dtb_ref[...]
        soft = jnp.maximum(raw, 0.0) + jnp.log1p(jnp.exp(-jnp.abs(raw)))
        step_ref[rows, :] = jnp.where(alive, soft, 0.0)


def scan_kernel(pos_ref, plan_ref, active_hbm, x0, x1, x2, x3, y0, y1, y2, y3, got_ref,
                conv_hbm, z_hbm, dtw_hbm, dtb_hbm, rate_hbm, gain_hbm, state_ref,
                gated_ref, out_ref, alive_s, rate_s, state_s, step_s, conv_s, low_s, rank_s,
                active_ref, conv_ref, z_ref, dtw_ref, dtb_ref, rate_ref, gain_ref,
                in_sems, out_sems, sems):
    steps, slots, width = z_ref.shape
    states = rate_ref.shape[0]
    block = slots // in_sems.shape[0]
    tiles = width // 128

    def load(i, l):
        rows = pl.ds(i * block * states, block * states)
        return pltpu.make_async_copy(state_ref.at[rows, pl.ds(l * 128, 128)], state_s.at[l, rows], in_sems.at[i, l])

    def store(i, l):
        rows = pl.ds(i * block * states, block * states)
        return pltpu.make_async_copy(state_s.at[l, rows], out_ref.at[rows, pl.ds(l * 128, 128)], out_sems.at[i, l])

    copies = fetch(
        ((active_hbm, active_ref), (dtw_hbm, dtw_ref), (dtb_hbm, dtb_ref), (conv_hbm, conv_ref),
         (rate_hbm, rate_ref), (gain_hbm, gain_ref), (z_hbm, z_ref)),
        sems,
    )
    for i in range(slots // block):
        for l in range(tiles):
            load(i, l).start()
    copies[0].wait()

    def ready():
        for copy in copies[1:]:
            copy.wait()

    prepare(pos_ref, active_ref, (x0, x1, x2, x3), (y0, y1, y2, y3), conv_ref, dtw_ref, dtb_ref,
            step_s, conv_s, low_s, rank_s, ready)
    rate_s[...] = rate_ref[...] * (-1.0 / math.log(2.0))
    alive = as_column(active_ref[...], slots) == 1
    alive_s[...] = jnp.broadcast_to(jnp.where(alive, 1.0, 0.0), alive_s.shape)
    for i in range(slots // block):
        for l in range(tiles):
            load(i, l).wait()
    buckets = got_ref.shape[0] // states

    def patch(b, carry):
        gone = plan_ref[0, b]
        here = plan_ref[1, b]

        @pl.when(gone >= 0)
        def _():
            rows = pl.ds(pl.multiple_of(gone * states, states), states)
            for l in range(tiles):
                state_s[l, rows, :] = jnp.zeros((states, 128), F32)

        @pl.when(here >= 0)
        def _():
            rows = pl.ds(pl.multiple_of(here * states, states), states)
            there = pl.ds(pl.multiple_of(b * states, states), states)
            for l in range(tiles):
                state_s[l, rows, :] = got_ref[there, l * 128 : (l + 1) * 128]

        return carry

    lax.fori_loop(0, buckets, patch, 0)

    def group(base):
        dts, dxs, lows, accs = [], [], [], []
        for t in range(steps):
            rows = pl.ds(pl.multiple_of(t * slots + base, 8), 8)
            lows.append(low_s[rows, :])
            for l in range(tiles):
                lanes = slice(l * 128, (l + 1) * 128)
                dt = step_s[rows, lanes]
                cv = conv_s[rows, lanes]
                dts.append(dt)
                dxs.append(dt * cv)
                accs.append(gain_ref[:, lanes] * cv)
        for n in range(states):
            place = pl.ds(base * states + n, 8, stride=states)
            gives = [jnp.broadcast_to(low[:, n : n + 1], (8, 128)) for low in lows]
            takes = [jnp.broadcast_to(low[:, states + n : states + n + 1], (8, 128)) for low in lows]
            for l in range(tiles):
                st = state_s[l, place, :]
                rate = rate_s[n : n + 1, l * 128 : (l + 1) * 128]
                for t in range(steps):
                    k = t * tiles + l
                    st = jnp.exp2(dts[k] * rate) * st + dxs[k] * gives[t]
                    accs[k] = accs[k] + st * takes[t]
                state_s[l, place, :] = st
        return accs

    def pair(i, carry):
        base = pl.multiple_of(i * 16, 16)
        accs = [group(base), group(pl.multiple_of(base + 8, 8))]
        on = alive_s[pl.ds(base, 16), :] > 0.5
        for t in range(steps):
            for l in range(tiles):
                lanes = slice(l * 128, (l + 1) * 128)
                gate = jax.nn.silu(z_ref[t, pl.ds(base, 16), lanes].astype(F32))
                value = jnp.concatenate([accs[0][t * tiles + l], accs[1][t * tiles + l]], axis=0) * gate
                gated_ref[t, pl.ds(base, 16), lanes] = jnp.where(on, value, 0.0).astype(BF16)
        return carry

    def chunk(i, carry):
        lax.fori_loop(i * (block // 16), (i + 1) * (block // 16), pair, 0)
        for l in range(tiles):
            store(i, l).start()
        return carry

    lax.fori_loop(0, slots // block, chunk, 0)
    for i in range(slots // block):
        for l in range(tiles):
            store(i, l).wait()


def in_hbm(value):
    return pltpu.with_memory_space_constraint(value, pltpu.HBM)


def on_device(projected, conv_weight, conv_bias, xproj_weight, dtproj_weight, dt_bias, a_rate, skip_gain,
              ssm_state, conv_cache, send_dest, recv_source, active):
    steps, slots, _, width = projected.shape
    rank_width = dtproj_weight.shape[0]
    states = a_rate.shape[0]
    taps = conv_weight.shape[0]
    peers = lax.axis_size("req")
    buckets = peers * CAP
    place = lax.axis_index("wa")
    pos = jnp.stack([lax.axis_index("req"), place // SIDE, place % SIDE]).astype(jnp.int32)
    send_row, recv_row, active_row = (in_hbm(v.reshape(1, slots)) for v in (send_dest, recv_source, active))
    recv_rows = recv_source.reshape(1, slots)
    bias, dt_row, gain = (v.reshape(1, width) for v in (conv_bias, dt_bias, skip_gain))
    cache = in_hbm(jnp.transpose(conv_cache, (1, 0, 2)))
    proj = jnp.transpose(xproj_weight, (1, 0))
    state_rows = in_hbm(ssm_state.reshape(slots * states, width))
    sds = jax.ShapeDtypeStruct

    out_cache, plan = pl.pallas_call(
        pick_cache_kernel,
        out_shape=(sds((peers * 8, width), F32), sds((2, slots), jnp.int32)),
        in_specs=[SM, HB, HB, HB],
        out_specs=(VM, VM),
        scratch_shapes=[
            pltpu.VMEM((1, slots), jnp.int32),
            pltpu.VMEM((1, slots), jnp.int32),
            pltpu.VMEM(cache.shape, BF16),
            pltpu.SemaphoreType.DMA((3,)),
        ],
        compiler_params=pltpu.CompilerParams(vmem_limit_bytes=4 * MIB),
        name="pick_cache",
    )(pos, send_row, recv_row, cache)
    both = jnp.transpose(projected, (2, 0, 1, 3))
    got_cache = lax.all_to_all(
        out_cache.reshape(peers, 8, width), "req", split_axis=0, concat_axis=0, tiled=True
    ).reshape(peers * 8, width)

    out_state = pl.pallas_call(
        pick_state_kernel,
        out_shape=pltpu.HBM((buckets, states, width), F32),
        in_specs=[SM, HB],
        out_specs=HB,
        scratch_shapes=[
            pltpu.VMEM((buckets, states, width), F32),
            pltpu.SemaphoreType.DMA((buckets,)),
            pltpu.SemaphoreType.DMA((1,)),
        ],
        cost_estimate=pl.CostEstimate(flops=1, bytes_accessed=1, transcendentals=0),
        compiler_params=pltpu.CompilerParams(vmem_limit_bytes=4 * MIB),
        name="pick_state",
    )(plan, state_rows)

    total = steps * slots
    conv_main, z_part, cache_out, x_arr = pl.pallas_call(
        conv_kernel,
        out_shape=(
            sds((steps, slots, width), BF16),
            pltpu.HBM((steps, slots, width), BF16),
            sds((taps - 1, slots, width), BF16),
            sds((steps * buckets, width), BF16),
        ),
        in_specs=[SM] + [HB] * 3 + [VM] + [HB] * 3,
        out_specs=(VM, HB, VM, VM),
        scratch_shapes=[
            pltpu.SemaphoreType.DMA((1,)),
            pltpu.VMEM((1, slots), jnp.int32),
            pltpu.VMEM((1, slots), jnp.int32),
            pltpu.VMEM((1, slots), jnp.int32),
            pltpu.VMEM(cache.shape, BF16),
            pltpu.VMEM(conv_weight.shape, BF16),
            pltpu.VMEM((1, width), F32),
            pltpu.SemaphoreType.DMA((6,)),
        ],
        compiler_params=pltpu.CompilerParams(vmem_limit_bytes=8 * MIB),
        name="convolve",
    )(pos, send_row, recv_row, active_row, both, cache, in_hbm(conv_weight), in_hbm(bias))

    out_state, conv_main, x_arr = lax.optimization_barrier((out_state, conv_main, x_arr))
    half = steps * (slots // 2 // SIDE)
    projected_parts = pl.pallas_call(
        project_kernel,
        out_shape=(pltpu.HBM((total, width), BF16),) + (sds((half + 8, width), F32),) * (2 * SIDE),
        in_specs=[SM] + [VM] * 7,
        out_specs=(HB,) + (VM,) * (2 * SIDE),
        scratch_shapes=[
            pltpu.VMEM((total, width), BF16),
            pltpu.VMEM((total, width), F32),
            pltpu.VMEM((total, 128), F32),
            pltpu.SemaphoreType.DMA((1,)),
        ],
        compiler_params=pltpu.CompilerParams(vmem_limit_bytes=8 * MIB),
        name="project",
    )(pos, recv_rows, got_cache, x_arr, conv_main, conv_weight, bias, proj)
    conv_all = projected_parts[0]
    own_a, own_b = projected_parts[1 : 1 + SIDE], projected_parts[1 + SIDE :]

    def gathered(value, axis, parts):
        return [value] + [lax.ppermute(parts[d - 1], "wa", shift(axis, d)) for d in range(1, SIDE)]

    def summed(value, axis, parts):
        pieces = gathered(value, axis, parts)
        return pieces[0] + pieces[1] + pieces[2] + pieces[3]

    sum_a = summed(own_a[0], 0, own_a[1:])
    sum_b = summed(own_b[0], 1, own_b[1:])
    got_state = lax.all_to_all(out_state, "req", split_axis=0, concat_axis=0, tiled=True)
    all_a = summed(sum_a, 1, [sum_a] * 3)
    all_b = summed(sum_b, 0, [sum_b] * 3)
    last_x = gathered(all_a, 0, [all_a] * 3)
    last_y = gathered(all_b, 1, [all_b] * 3)

    gated_out, state_out = pl.pallas_call(
        scan_kernel,
        out_shape=(sds((steps, slots, width), BF16), sds((slots * states, width), F32)),
        in_specs=[SM, SM, HB] + [VM] * 9 + [HB] * 7,
        out_specs=(VM, HB),
        scratch_shapes=[
            pltpu.VMEM((slots, 128), F32),
            pltpu.VMEM((states, width), F32),
            pltpu.VMEM((width // 128, slots * states, 128), F32),
            pltpu.VMEM((total, width), F32),
            pltpu.VMEM((total, width), F32),
            pltpu.VMEM((total, 128), F32),
            pltpu.VMEM((total, width), BF16),
            pltpu.VMEM((1, slots), jnp.int32),
            pltpu.VMEM((total, width), BF16),
            pltpu.VMEM((steps, slots, width), BF16),
            pltpu.VMEM(dtproj_weight.shape, BF16),
            pltpu.VMEM((1, width), F32),
            pltpu.VMEM((states, width), F32),
            pltpu.VMEM((1, width), F32),
            pltpu.SemaphoreType.DMA((4, width // 128)),
            pltpu.SemaphoreType.DMA((4, width // 128)),
            pltpu.SemaphoreType.DMA((7,)),
        ],
        compiler_params=pltpu.CompilerParams(vmem_limit_bytes=20 * MIB),
        name="scan",
    )(
        pos, plan, active_row, *last_x, *last_y, got_state.reshape(buckets * states, width),
        in_hbm(conv_all), in_hbm(z_part), in_hbm(dtproj_weight), in_hbm(dt_row),
        in_hbm(a_rate), in_hbm(gain), state_rows,
    )
    return (
        gated_out,
        state_out.reshape(slots, states, width),
        jnp.transpose(cache_out, (1, 0, 2)),
    )


def solution(mesh):
    return jax.shard_map(
        on_device,
        mesh=mesh,
        in_specs=(
            P(None, "req", None, "wa"),
            P(None, "wa"),
            P("wa"),
            P("wa", None),
            P(None, "wa"),
            P("wa"),
            P(None, "wa"),
            P("wa"),
            P("req", None, "wa"),
            P("req", None, "wa"),
            P("req"),
            P("req"),
            P("req"),
        ),
        out_specs=(P(None, "req", "wa"), P("req", None, "wa"), P("req", None, "wa")),
        check_vma=False,
    )
```

time: 104 us -> 78.4 us (0.75)
  local copies, waits for them, and re-layouts: 15.1 us -> 0.11 us
  waiting for transfers between devices: 18.5 us -> 12.4 us
  starting transfers between devices: 47.3 us -> 41.3 us
  Pallas kernels: 21.5 us -> 23 us
    unnamed x54 -> x11, local copies, waits for them, and re-layouts: 14 us -> 0.11 us
    ppermute x18, waiting for transfers between devices: 17.5 us -> 9.2 us  [gathered(): lax.ppermute(parts[d - 1], 'wa', shift(axis, d))]
    ppermute x18, starting transfers between devices: 32.3 us -> 27.6 us  [gathered(): lax.ppermute(parts[d - 1], 'wa', shift(axis, d))]
    all_to_all x1, waiting for transfers between devices: 1.04 us -> 3.15 us  [on_device(): lax.all_to_all(out_cache.reshape(peers, 8, width), 'req', split_axis=0, c...]
    all_to_all x1, starting transfers between devices: 6.34 us -> 5.09 us  [on_device(): lax.all_to_all(out_state, 'req', split_axis=0, concat_axis=0, tiled=True)]
    pallas_call x4, Pallas kernels: 9.96 us -> 11.2 us  [the longest x1 3.18 us: on_device(): pl.pallas_call(pick_state_kernel, out_shape=pltpu.HBM((buckets, states, w...]
    slice x1 -> x0, local copies, waits for them, and re-layouts: 1.09 us -> none  [on_device(): z_part = projected[:, :, 1]]
  transfers between devices with their start and end apart: 20 -> 20, of which waited for: 11 -> 9; matrix products, arithmetic and copies ran while one was open for 1% -> 0% of each run, Pallas kernels for 8% -> 11%
where the time goes in v2:
time: 78.4 us; the launch traced here: 78 us
  starting transfers between devices  41.3 us (53%)
  Pallas kernels  23 us (29%)
  waiting for transfers between devices  12.4 us (16%)
  between operations  0.96 us (1%)
    ppermute x18, starting transfers between devices, gathered(): lax.ppermute(parts[d - 1], 'wa', shift(axis, d))  27.6 us
    pallas_call x1, Pallas kernels, on_device(): pl.pallas_call(scan_kernel, out_shape=(sds((steps, slots, width), BF16),...  11.9 us
    ppermute x18, waiting for transfers between devices, gathered(): lax.ppermute(parts[d - 1], 'wa', shift(axis, d))  9.2 us
    all_to_all x1, starting transfers between devices, on_device(): lax.all_to_all(out_cache.reshape(peers, 8, width), 'req', split_axis=0, c...  8.6 us
    all_to_all x1, starting transfers between devices, on_device(): lax.all_to_all(out_state, 'req', split_axis=0, concat_axis=0, tiled=True)  5.09 us
    pallas_call x1, Pallas kernels, on_device(): pl.pallas_call(pick_state_kernel, out_shape=pltpu.HBM((buckets, states, w...  3.18 us
    pallas_call x1, Pallas kernels, on_device(): pl.pallas_call(conv_kernel, out_shape=(sds((steps, slots, width), BF16),...  3.15 us
    all_to_all x1, waiting for transfers between devices, on_device(): lax.all_to_all(out_cache.reshape(peers, 8, width), 'req', split_axis=0, c...  3.15 us
  transfers between devices with their start and end apart: 20, of which 9 were waited for; matrix products, arithmetic and copies ran while one was open for 0% of the time, Pallas kernels for 11%

profile of v2, /device:TPU:32, one launch (start us, length us, event | category | flops | bytes accessed | tf_op | source)
XLA Modules:
  0.0 78.0 jit_solution(3425115480773221803)
XLA Ops:
  0.7 2.6 %pick_cache.1 = (f32[128,512]{1,0:T(8,128)}, s32[2,128]{1,0:T(2,128)S(1)}) custom-call(s32[3]{0:T(128)S(1)} %pad_add_fusion.pos_ref, s32[1,128]{1,0:T(1,128)} %bitcast.33, s32[1,128]{1,0:T(1,128)} %bitcast.26, bf16[3,128,512]{2,1,0:T(8,128)(2,1)} %bitcast.31), custom_call_target="tpu_custom_call" | custom-call | tf_op jit(solution)/shard_map/pick_cache/pallas_call | solution.py:370
  3.3 8.6 %all-to-all-start = ((f32[16,8,512]{2,1,0:T(8,128)}), f32[16,8,512]{2,1,0:T(8,128)S(1)}, u32[]{:S(2)}, u32[]{:S(2)}) async-start(f32[16,8,512]{2,1,0:T(8,128)} %bitcast.7), calls=%async_computation | async-start | bytes 524288 | tf_op jit(solution)/shard_map/all_to_all | solution.py:385
  12.0 3.2 %pick_state.1 = f32[32,16,512]{2,1,0:T(8,128)} custom-call(s32[2,128]{1,0:T(2,128)S(1)} %get-tuple-element.23.plan_ref, f32[2048,512]{1,0:T(8,128)} %bitcast.29), custom_call_target="tpu_custom_call" | custom-call | flops 1 | bytes 1 | tf_op jit(solution)/shard_map/pick_state/pallas_call | solution.py:389
  15.2 3.2 %convolve.1 = (bf16[3,128,512]{2,1,0:T(8,128)(2,1)S(1)}, bf16[3,128,512]{2,1,0:T(8,128)(2,1)}, bf16[3,128,512]{2,1,0:T(8,128)(2,1)}, bf16[96,512]{1,0:T(8,128)(2,1)S(1)}) custom-call(s32[3]{0:T(128)S(1)} %pad_add_fusion.pos_ref, s32[1,128]{1,0:T(1,128)} %bitcast.34, s32[1,128]{1,0:T(1,128)} %bitcast.27, s32[1,128]{1,0:T(1,128)} %bitcast.35, ...), custom_call_target="tpu_custom_call" | custom-call | tf_op jit(solution)/shard_map/convolve/pallas_call | solution.py:405
  18.4 3.1 %all-to-all-done = f32[16,8,512]{2,1,0:T(8,128)S(1)} async-done(((f32[16,8,512]{2,1,0:T(8,128)}), f32[16,8,512]{2,1,0:T(8,128)S(1)}, u32[]{:S(2)}, u32[]{:S(2)}) %all-to-all-start) | async-done | bytes 262176 | tf_op jit(solution)/shard_map/all_to_all | solution.py:385
  21.6 5.1 %all-to-all-start.1 = ((f32[32,16,512]{2,1,0:T(8,128)}), f32[32,16,512]{2,1,0:T(8,128)S(1)}, u32[]{:S(2)}, u32[]{:S(2)}) async-start(f32[32,16,512]{2,1,0:T(8,128)} %pick_state.1), calls=%async_computation.1 | async-start | bytes 2097152 | tf_op jit(solution)/shard_map/all_to_all | solution.py:457
  26.7 2.3 %project.1 = (bf16[384,512]{1,0:T(8,128)(2,1)}, f32[56,512]{1,0:T(8,128)S(1)}, f32[56,512]{1,0:T(8,128)S(1)}, f32[56,512]{1,0:T(8,128)S(1)}, f32[56,512]{1,0:T(8...) custom-call(s32[3]{0:T(128)S(1)} %pad_add_fusion.pos_ref, ...), custom_call_target="tpu_custom_call" | custom-call | tf_op jit(solution)/shard_map/project/pallas_call | solution.py:431
  28.9 1.6 %collective-permute-start = (f32[56,512]{1,0:T(8,128)S(1)}, f32[56,512]{1,0:T(8,128)S(1)}, u32[]{:S(2)}, u32[]{:S(2)}) collective-permute-start(f32[56,512]{1,0:T(8,128)S(1)} %get-tuple-element.30), channel_id=1, source_target_pairs={{0,4},{1,5},{2,6},{3,7},{4,8},{5,9},{6,10},{7,11},{8,12},{9,13},{1... | collective-permute-start | bytes 344072 | tf_op jit(solution)/shard_map/ppermute | solution.py:449
  30.5 2.7 %collective-permute-start.1 = (f32[56,512]{1,0:T(8,128)S(1)}, f32[56,512]{1,0:T(8,128)S(1)}, u32[]{:S(2)}, u32[]{:S(2)}) collective-permute-start(f32[56,512]{1,0:T(8,128)S(1)} %get-tuple-element.31), channel_id=1, source_target_pairs={{0,8},{1,9},{2,10},{3,11},{4,12},{5,13},{6,14},{7,15},{8,0},{9,1},... | collective-permute-start | bytes 344072 | tf_op jit(solution)/shard_map/ppermute | solution.py:449
  33.2 1.4 %collective-permute-start.2 = (f32[56,512]{1,0:T(8,128)S(1)}, f32[56,512]{1,0:T(8,128)S(1)}, u32[]{:S(2)}, u32[]{:S(2)}) collective-permute-start(f32[56,512]{1,0:T(8,128)S(1)} %get-tuple-element.32), channel_id=1, source_target_pairs={{0,12},{1,13},{2,14},{3,15},{4,0},{5,1},{6,2},{7,3},{8,4},{9,5},{1... | collective-permute-start | bytes 344072 | tf_op jit(solution)/shard_map/ppermute | solution.py:449
  34.7 1.6 %collective-permute-start.9 = (f32[56,512]{1,0:T(8,128)S(1)}, f32[56,512]{1,0:T(8,128)S(1)}, u32[]{:S(2)}, u32[]{:S(2)}) collective-permute-start(f32[56,512]{1,0:T(8,128)S(1)} %get-tuple-element.34), channel_id=1, source_target_pairs={{0,1},{1,2},{2,3},{3,0},{4,5},{5,6},{6,7},{7,4},{8,9},{9,10},{10,1... | collective-permute-start | bytes 344072 | tf_op jit(solution)/shard_map/ppermute | solution.py:449
  36.3 2.9 %collective-permute-start.10 = (f32[56,512]{1,0:T(8,128)S(1)}, f32[56,512]{1,0:T(8,128)S(1)}, u32[]{:S(2)}, u32[]{:S(2)}) collective-permute-start(f32[56,512]{1,0:T(8,128)S(1)} %get-tuple-element.35), channel_id=1, source_target_pairs={{0,2},{1,3},{2,0},{3,1},{4,6},{5,7},{6,4},{7,5},{8,10},{9,11},{10,... | collective-permute-start | bytes 344072 | tf_op jit(solution)/shard_map/ppermute | solution.py:449
  39.2 1.4 %collective-permute-start.11 = (f32[56,512]{1,0:T(8,128)S(1)}, f32[56,512]{1,0:T(8,128)S(1)}, u32[]{:S(2)}, u32[]{:S(2)}) collective-permute-start(f32[56,512]{1,0:T(8,128)S(1)} %get-tuple-element.36), channel_id=1, source_target_pairs={{0,3},{1,0},{2,1},{3,2},{4,7},{5,4},{6,5},{7,6},{8,11},{9,8},{10,9... | collective-permute-start | bytes 344072 | tf_op jit(solution)/shard_map/ppermute | solution.py:449
  40.6 1.5 %collective-permute-start.5 = (f32[56,512]{1,0:T(8,128)S(1)}, f32[56,512]{1,0:T(8,128)S(1)}, u32[]{:S(2)}, u32[]{:S(2)}) collective-permute-start(f32[56,512]{1,0:T(8,128)S(1)} %add_add_fusion.3), channel_id=1, source_target_pairs={{0,3},{1,0},{2,1},{3,2},{4,7},{5,4},{6,5},{7,6},{8,11},{9,8},{10,9... | collective-permute-start | bytes 344072 | tf_op jit(solution)/shard_map/ppermute | solution.py:449
  42.0 1.4 %collective-permute-start.4 = (f32[56,512]{1,0:T(8,128)S(1)}, f32[56,512]{1,0:T(8,128)S(1)}, u32[]{:S(2)}, u32[]{:S(2)}) collective-permute-start(f32[56,512]{1,0:T(8,128)S(1)} %add_add_fusion.3), channel_id=1, source_target_pairs={{0,2},{1,3},{2,0},{3,1},{4,6},{5,7},{6,4},{7,5},{8,10},{9,11},{10,... | collective-permute-start | bytes 344072 | tf_op jit(solution)/shard_map/ppermute | solution.py:449
  43.9 1.3 %collective-permute-done.11 = f32[56,512]{1,0:T(8,128)S(1)} collective-permute-done((f32[56,512]{1,0:T(8,128)S(1)}, f32[56,512]{1,0:T(8,128)S(1)}, u32[]{:S(2)}, u32[]{:S(2)}) %collective-permute-start.11) | collective-permute-done | bytes 114720 | tf_op jit(solution)/shard_map/ppermute | solution.py:449
  46.0 2.0 %collective-permute-start.13 = (f32[56,512]{1,0:T(8,128)S(1)}, f32[56,512]{1,0:T(8,128)S(1)}, u32[]{:S(2)}, u32[]{:S(2)}) collective-permute-start(f32[56,512]{1,0:T(8,128)S(1)} %add_add_fusion.1), channel_id=1, source_target_pairs={{0,8},{1,9},{2,10},{3,11},{4,12},{5,13},{6,14},{7,15},{8,0},{9,1},... | collective-permute-start | bytes 344072 | tf_op jit(solution)/shard_map/ppermute | solution.py:449
  48.9 1.2 %collective-permute-done.3 = f32[56,512]{1,0:T(8,128)S(1)} collective-permute-done((f32[56,512]{1,0:T(8,128)S(1)}, f32[56,512]{1,0:T(8,128)S(1)}, u32[]{:S(2)}, u32[]{:S(2)}) %collective-permute-start.3) | collective-permute-done | bytes 114720 | tf_op jit(solution)/shard_map/ppermute | solution.py:449
  50.1 2.3 %collective-permute-start.8 = (f32[56,512]{1,0:T(8,128)S(1)}, f32[56,512]{1,0:T(8,128)S(1)}, u32[]{:S(2)}, u32[]{:S(2)}) collective-permute-start(f32[56,512]{1,0:T(8,128)S(1)} %add_add_fusion.2.x0), channel_id=1, source_target_pairs={{0,12},{1,13},{2,14},{3,15},{4,0},{5,1},{6,2},{7,3},{8,4},{9,5},{1... | collective-permute-start | bytes 344072 | tf_op jit(solution)/shard_map/ppermute | solution.py:449
  54.1 4.3 %collective-permute-start.17 = (f32[56,512]{1,0:T(8,128)S(1)}, f32[56,512]{1,0:T(8,128)S(1)}, u32[]{:S(2)}, u32[]{:S(2)}) collective-permute-start(f32[56,512]{1,0:T(8,128)S(1)} %add_add_fusion.y0), channel_id=1, source_target_pairs={{0,3},{1,0},{2,1},{3,2},{4,7},{5,4},{6,5},{7,6},{8,11},{9,8},{10,9... | collective-permute-start | bytes 344072 | tf_op jit(solution)/shard_map/ppermute | solution.py:449
  58.4 1.3 %collective-permute-start.16 = (f32[56,512]{1,0:T(8,128)S(1)}, f32[56,512]{1,0:T(8,128)S(1)}, u32[]{:S(2)}, u32[]{:S(2)}) collective-permute-start(f32[56,512]{1,0:T(8,128)S(1)} %add_add_fusion.y0), channel_id=1, source_target_pairs={{0,2},{1,3},{2,0},{3,1},{4,6},{5,7},{6,4},{7,5},{8,10},{9,11},{10,... | collective-permute-start | bytes 344072 | tf_op jit(solution)/shard_map/ppermute | solution.py:449
  60.8 4.0 %collective-permute-done.16.y2 = f32[56,512]{1,0:T(8,128)S(1)} collective-permute-done((f32[56,512]{1,0:T(8,128)S(1)}, f32[56,512]{1,0:T(8,128)S(1)}, u32[]{:S(2)}, u32[]{:S(2)}) %collective-permute-start.16) | collective-permute-done | bytes 114720 | tf_op jit(solution)/shard_map/ppermute | solution.py:449
  64.7 1.2 %collective-permute-done.15.y1 = f32[56,512]{1,0:T(8,128)S(1)} collective-permute-done((f32[56,512]{1,0:T(8,128)S(1)}, f32[56,512]{1,0:T(8,128)S(1)}, u32[]{:S(2)}, u32[]{:S(2)}) %collective-permute-start.15) | collective-permute-done | bytes 114720 | tf_op jit(solution)/shard_map/ppermute | solution.py:449
  65.9 11.9 %scan.1 = (bf16[3,128,512]{2,1,0:T(8,128)(2,1)}, f32[2048,512]{1,0:T(8,128)}) custom-call(s32[3]{0:T(128)S(1)} %pad_add_fusion.pos_ref, s32[2,128]{1,0:T(2,128)S(1)} %get-tuple-element.23.plan_ref, s32[1,128]{1,0:T(1,128)} %bitcast.36, f32[56,512]{1,0:T(8,128)S(1)} %add_add_fusion.2.x0, f32[56,512]{1,0:T(8,128)S(1)} %collective-permute-done.6.x1, ...), custom_call_target="tpu_custom_call" | custom-call | tf_op jit(solution)/shard_map/scan/pallas_call | solution.py:463
  (37 shorter events, 5.2 us)
Async XLA Ops:
  3.3 18.2 %all-to-all-start = ((f32[16,8,512]{2,1,0:T(8,128)}), f32[16,8,512]{2,1,0:T(8,128)S(1)}, u32[]{:S(2)}, u32[]{:S(2)}) async-start(f32[16,8,512]{2,1,0:T(8,128)} %bitcast.7), calls=%async_computation | async-start | bytes 524288 | tf_op jit(solution)/shard_map/all_to_all | solution.py:385
  11.9 14.7 %copy-start = (bf16[512,544]{0,1:T(8,128)(2,1)S(1)}, bf16[512,544]{0,1:T(8,128)(2,1)}, u32[]{:S(2)}) copy-start(bf16[512,544]{0,1:T(8,128)(2,1)} %param.16) | copy-start | bytes 1671172
  11.9 14.7 %copy-start.1 = (bf16[4,512]{1,0:T(4,128)(2,1)S(1)}, bf16[4,512]{1,0:T(4,128)(2,1)}, u32[]{:S(2)}) copy-start(bf16[4,512]{1,0:T(4,128)(2,1)} %taps_ref.1) | copy-start | bytes 12292
  11.9 14.7 %copy-start.2 = (f32[512]{0:T(512)S(1)}, f32[512]{0:T(512)}, u32[]{:S(2)}) copy-start(f32[512]{0:T(512)} %param.15) | copy-start | bytes 6148
  11.9 14.7 %copy-start.3 = (s32[128]{0:T(128)S(1)}, s32[128]{0:T(128)}, u32[]{:S(2)}) copy-start(s32[128]{0:T(128)} %param.24) | copy-start | bytes 1540
  21.6 44.4 %all-to-all-start.1 = ((f32[32,16,512]{2,1,0:T(8,128)}), f32[32,16,512]{2,1,0:T(8,128)S(1)}, u32[]{:S(2)}, u32[]{:S(2)}) async-start(f32[32,16,512]{2,1,0:T(8,128)} %pick_state.1), calls=%async_computation.1 | async-start | bytes 2097152 | tf_op jit(solution)/shard_map/all_to_all | solution.py:457
  28.9 10.2 %collective-permute-start = (f32[56,512]{1,0:T(8,128)S(1)}, f32[56,512]{1,0:T(8,128)S(1)}, u32[]{:S(2)}, u32[]{:S(2)}) collective-permute-start(f32[56,512]{1,0:T(8,128)S(1)} %get-tuple-element.30), channel_id=1, source_target_pairs={{0,4},{1,5},{2,6},{3,7},{4,8},{5,9},{6,10},{7,11},{8,12},{9,13},{1... | collective-permute-start | bytes 344072 | tf_op jit(solution)/shard_map/ppermute | solution.py:449
  30.5 10.0 %collective-permute-start.1 = (f32[56,512]{1,0:T(8,128)S(1)}, f32[56,512]{1,0:T(8,128)S(1)}, u32[]{:S(2)}, u32[]{:S(2)}) collective-permute-start(f32[56,512]{1,0:T(8,128)S(1)} %get-tuple-element.31), channel_id=1, source_target_pairs={{0,8},{1,9},{2,10},{3,11},{4,12},{5,13},{6,14},{7,15},{8,0},{9,1},... | collective-permute-start | bytes 344072 | tf_op jit(solution)/shard_map/ppermute | solution.py:449
  33.2 7.3 %collective-permute-start.2 = (f32[56,512]{1,0:T(8,128)S(1)}, f32[56,512]{1,0:T(8,128)S(1)}, u32[]{:S(2)}, u32[]{:S(2)}) collective-permute-start(f32[56,512]{1,0:T(8,128)S(1)} %get-tuple-element.32), channel_id=1, source_target_pairs={{0,12},{1,13},{2,14},{3,15},{4,0},{5,1},{6,2},{7,3},{8,4},{9,5},{1... | collective-permute-start | bytes 344072 | tf_op jit(solution)/shard_map/ppermute | solution.py:449
  34.7 8.7 %collective-permute-start.9 = (f32[56,512]{1,0:T(8,128)S(1)}, f32[56,512]{1,0:T(8,128)S(1)}, u32[]{:S(2)}, u32[]{:S(2)}) collective-permute-start(f32[56,512]{1,0:T(8,128)S(1)} %get-tuple-element.34), channel_id=1, source_target_pairs={{0,1},{1,2},{2,3},{3,0},{4,5},{5,6},{6,7},{7,4},{8,9},{9,10},{10,1... | collective-permute-start | bytes 344072 | tf_op jit(solution)/shard_map/ppermute | solution.py:449
  36.3 7.7 %collective-permute-start.10 = (f32[56,512]{1,0:T(8,128)S(1)}, f32[56,512]{1,0:T(8,128)S(1)}, u32[]{:S(2)}, u32[]{:S(2)}) collective-permute-start(f32[56,512]{1,0:T(8,128)S(1)} %get-tuple-element.35), channel_id=1, source_target_pairs={{0,2},{1,3},{2,0},{3,1},{4,6},{5,7},{6,4},{7,5},{8,10},{9,11},{10,... | collective-permute-start | bytes 344072 | tf_op jit(solution)/shard_map/ppermute | solution.py:449
  39.2 6.1 %collective-permute-start.11 = (f32[56,512]{1,0:T(8,128)S(1)}, f32[56,512]{1,0:T(8,128)S(1)}, u32[]{:S(2)}, u32[]{:S(2)}) collective-permute-start(f32[56,512]{1,0:T(8,128)S(1)} %get-tuple-element.36), channel_id=1, source_target_pairs={{0,3},{1,0},{2,1},{3,2},{4,7},{5,4},{6,5},{7,6},{8,11},{9,8},{10,9... | collective-permute-start | bytes 344072 | tf_op jit(solution)/shard_map/ppermute | solution.py:449
  40.6 7.5 %collective-permute-start.5 = (f32[56,512]{1,0:T(8,128)S(1)}, f32[56,512]{1,0:T(8,128)S(1)}, u32[]{:S(2)}, u32[]{:S(2)}) collective-permute-start(f32[56,512]{1,0:T(8,128)S(1)} %add_add_fusion.3), channel_id=1, source_target_pairs={{0,3},{1,0},{2,1},{3,2},{4,7},{5,4},{6,5},{7,6},{8,11},{9,8},{10,9... | collective-permute-start | bytes 344072 | tf_op jit(solution)/shard_map/ppermute | solution.py:449
  42.0 6.9 %collective-permute-start.4 = (f32[56,512]{1,0:T(8,128)S(1)}, f32[56,512]{1,0:T(8,128)S(1)}, u32[]{:S(2)}, u32[]{:S(2)}) collective-permute-start(f32[56,512]{1,0:T(8,128)S(1)} %add_add_fusion.3), channel_id=1, source_target_pairs={{0,2},{1,3},{2,0},{3,1},{4,6},{5,7},{6,4},{7,5},{8,10},{9,11},{10,... | collective-permute-start | bytes 344072 | tf_op jit(solution)/shard_map/ppermute | solution.py:449
  43.4 6.7 %collective-permute-start.3 = (f32[56,512]{1,0:T(8,128)S(1)}, f32[56,512]{1,0:T(8,128)S(1)}, u32[]{:S(2)}, u32[]{:S(2)}) collective-permute-start(f32[56,512]{1,0:T(8,128)S(1)} %add_add_fusion.3), channel_id=1, source_target_pairs={{0,1},{1,2},{2,3},{3,0},{4,5},{5,6},{6,7},{7,4},{8,9},{9,10},{10,1... | collective-permute-start | bytes 344072 | tf_op jit(solution)/shard_map/ppermute | solution.py:449
  45.3 8.1 %collective-permute-start.14 = (f32[56,512]{1,0:T(8,128)S(1)}, f32[56,512]{1,0:T(8,128)S(1)}, u32[]{:S(2)}, u32[]{:S(2)}) collective-permute-start(f32[56,512]{1,0:T(8,128)S(1)} %add_add_fusion.1), channel_id=1, source_target_pairs={{0,12},{1,13},{2,14},{3,15},{4,0},{5,1},{6,2},{7,3},{8,4},{9,5},{1... | collective-permute-start | bytes 344072 | tf_op jit(solution)/shard_map/ppermute | solution.py:449
  46.0 8.0 %collective-permute-start.13 = (f32[56,512]{1,0:T(8,128)S(1)}, f32[56,512]{1,0:T(8,128)S(1)}, u32[]{:S(2)}, u32[]{:S(2)}) collective-permute-start(f32[56,512]{1,0:T(8,128)S(1)} %add_add_fusion.1), channel_id=1, source_target_pairs={{0,8},{1,9},{2,10},{3,11},{4,12},{5,13},{6,14},{7,15},{8,0},{9,1},... | collective-permute-start | bytes 344072 | tf_op jit(solution)/shard_map/ppermute | solution.py:449
  48.0 6.0 %collective-permute-start.12 = (f32[56,512]{1,0:T(8,128)S(1)}, f32[56,512]{1,0:T(8,128)S(1)}, u32[]{:S(2)}, u32[]{:S(2)}) collective-permute-start(f32[56,512]{1,0:T(8,128)S(1)} %add_add_fusion.1), channel_id=1, source_target_pairs={{0,4},{1,5},{2,6},{3,7},{4,8},{5,9},{6,10},{7,11},{8,12},{9,13},{1... | collective-permute-start | bytes 344072 | tf_op jit(solution)/shard_map/ppermute | solution.py:449
  50.1 9.6 %collective-permute-start.8 = (f32[56,512]{1,0:T(8,128)S(1)}, f32[56,512]{1,0:T(8,128)S(1)}, u32[]{:S(2)}, u32[]{:S(2)}) collective-permute-start(f32[56,512]{1,0:T(8,128)S(1)} %add_add_fusion.2.x0), channel_id=1, source_target_pairs={{0,12},{1,13},{2,14},{3,15},{4,0},{5,1},{6,2},{7,3},{8,4},{9,5},{1... | collective-permute-start | bytes 344072 | tf_op jit(solution)/shard_map/ppermute | solution.py:449
  52.4 7.8 %collective-permute-start.7 = (f32[56,512]{1,0:T(8,128)S(1)}, f32[56,512]{1,0:T(8,128)S(1)}, u32[]{:S(2)}, u32[]{:S(2)}) collective-permute-start(f32[56,512]{1,0:T(8,128)S(1)} %add_add_fusion.2.x0), channel_id=1, source_target_pairs={{0,8},{1,9},{2,10},{3,11},{4,12},{5,13},{6,14},{7,15},{8,0},{9,1},... | collective-permute-start | bytes 344072 | tf_op jit(solution)/shard_map/ppermute | solution.py:449
  53.4 6.9 %collective-permute-start.6 = (f32[56,512]{1,0:T(8,128)S(1)}, f32[56,512]{1,0:T(8,128)S(1)}, u32[]{:S(2)}, u32[]{:S(2)}) collective-permute-start(f32[56,512]{1,0:T(8,128)S(1)} %add_add_fusion.2.x0), channel_id=1, source_target_pairs={{0,4},{1,5},{2,6},{3,7},{4,8},{5,9},{6,10},{7,11},{8,12},{9,13},{1... | collective-permute-start | bytes 344072 | tf_op jit(solution)/shard_map/ppermute | solution.py:449
  54.1 6.7 %collective-permute-start.17 = (f32[56,512]{1,0:T(8,128)S(1)}, f32[56,512]{1,0:T(8,128)S(1)}, u32[]{:S(2)}, u32[]{:S(2)}) collective-permute-start(f32[56,512]{1,0:T(8,128)S(1)} %add_add_fusion.y0), channel_id=1, source_target_pairs={{0,3},{1,0},{2,1},{3,2},{4,7},{5,4},{6,5},{7,6},{8,11},{9,8},{10,9... | collective-permute-start | bytes 344072 | tf_op jit(solution)/shard_map/ppermute | solution.py:449
  58.4 6.3 %collective-permute-start.16 = (f32[56,512]{1,0:T(8,128)S(1)}, f32[56,512]{1,0:T(8,128)S(1)}, u32[]{:S(2)}, u32[]{:S(2)}) collective-permute-start(f32[56,512]{1,0:T(8,128)S(1)} %add_add_fusion.y0), channel_id=1, source_target_pairs={{0,2},{1,3},{2,0},{3,1},{4,6},{5,7},{6,4},{7,5},{8,10},{9,11},{10,... | collective-permute-start | bytes 344072 | tf_op jit(solution)/shard_map/ppermute | solution.py:449
  59.7 6.2 %collective-permute-start.15 = (f32[56,512]{1,0:T(8,128)S(1)}, f32[56,512]{1,0:T(8,128)S(1)}, u32[]{:S(2)}, u32[]{:S(2)}) collective-permute-start(f32[56,512]{1,0:T(8,128)S(1)} %add_add_fusion.y0), channel_id=1, source_target_pairs={{0,1},{1,2},{2,3},{3,0},{4,5},{5,6},{6,7},{7,4},{8,9},{9,10},{10,1... | collective-permute-start | bytes 344072 | tf_op jit(solution)/shard_map/ppermute | solution.py:449
  (1 other events, 14.5 us)

commit v3 on v2

--- a/solution.py
+++ b/solution.py
@@ -62,7 +62,8 @@
     return copies
 
 
-def pick_cache_kernel(pos_ref, dest_hbm, source_hbm, cache_hbm, out_ref, plan_ref, dest_ref, source_ref, cache_ref, sems):
+def pick_cache_kernel(pos_ref, dest_hbm, source_hbm, cache_hbm, out_ref, plan_ref, dest_ref, source_ref, cache_ref,
+                      full_s, sems):
     copies = fetch(((dest_hbm, dest_ref), (source_hbm, source_ref), (cache_hbm, cache_ref)), sems)
     for copy in copies[:2]:
         copy.wait()
@@ -71,25 +72,30 @@
     row = dest_ref[...]
     col = as_column(row, slots)
     rank = ranks_row(row, col, slots)
-    rows = out_ref.shape[0]
+    rows = full_s.shape[0]
     shape = (rows, slots)
     target = iota(shape, 0) // 8
     place = iota(shape, 0) % 8
-    total = jnp.zeros(out_ref.shape, F32)
+    total = jnp.zeros(full_s.shape, F32)
+    square = (slots, slots)
+    bucket = iota(square, 1)
+    for k, ref in enumerate((dest_ref, source_ref)):
+        plan_row = ref[...]
+        plan_col = as_column(plan_row, slots)
+        hit = (plan_col != own) & (plan_col == bucket // CAP) & (ranks_col(plan_row, plan_col, slots) == bucket % CAP)
+        plan_ref[k : k + 1, :] = jnp.sum(jnp.where(hit, iota(square, 0) + 1, 0), axis=0, keepdims=True) - 1
     copies[2].wait()
     hit = (row == target) & (row != own) & (rank == place % CAP)
     for tap in range(taps):
         pick = jnp.where(hit & (place // CAP == tap), 1.0, 0.0).astype(BF16)
         total = total + dot_n(pick, cache_ref[tap])
-    out_ref[...] = total
-    shape = (slots, slots)
-    bucket = iota(shape, 1)
-    hit = (col != own) & (col == bucket // CAP) & (ranks_col(row, col, slots) == bucket % CAP)
-    plan_ref[0:1, :] = jnp.sum(jnp.where(hit, iota(shape, 0) + 1, 0), axis=0, keepdims=True) - 1
-    row = source_ref[...]
-    col = as_column(row, slots)
-    hit = (col != own) & (col == bucket // CAP) & (ranks_col(row, col, slots) == bucket % CAP)
-    plan_ref[1:2, :] = jnp.sum(jnp.where(hit, iota(shape, 0) + 1, 0), axis=0, keepdims=True) - 1
+    full_s[...] = total
+    used = taps * CAP
+    tiles = full_s.shape[1] // 128
+    for d in range(rows // 8):
+        for l in range(tiles):
+            start = (d * tiles + l) * used
+            out_ref[start : start + used, :] = full_s[8 * d : 8 * d + used, l * 128 : (l + 1) * 128]
 
 
 def pick_state_kernel(plan_ref, state_ref, out_hbm, out_ref, sems, out_sem):
@@ -119,7 +125,7 @@
 
 
 def conv_kernel(pos_ref, dest_hbm, source_hbm, active_hbm, both_ref, cache_hbm, taps_hbm, bias_hbm,
-                conv_ref, z_out, cache_out_ref, arr_ref, sems,
+                conv_ref, gate_out, cache_out_ref, arr_ref, sems,
                 dest_ref, source_ref, active_ref, cache_ref, taps_ref, bias_ref, in_sems):
     x_ref = both_ref.at[0]
     copies = fetch(
@@ -127,7 +133,7 @@
          (taps_hbm, taps_ref), (bias_hbm, bias_ref)),
         in_sems,
     )
-    gate_copy = pltpu.make_async_copy(both_ref.at[1], z_out, sems.at[0])
+    gate_copy = pltpu.make_async_copy(both_ref.at[1], gate_out, sems.at[0])
     gate_copy.start()
     for copy in copies:
         copy.wait()
@@ -161,10 +167,17 @@
 
 
 def project_kernel(pos_ref, source_ref, got_ref, arr_ref, conv_ref, taps_ref, bias_ref, proj_ref,
-                   conv_out, a0, a1, a2, a3, b0, b1, b2, b3, conv_s, mix, low, sems):
+                   conv_out, a0, a1, a2, a3, b0, b1, b2, b3, mix, low, full_s, conv_s, sems):
     steps, slots, width = conv_ref.shape
     buckets = arr_ref.shape[0] // steps
-    got = got_ref[...].astype(BF16)
+    used = (taps_ref.shape[0] - 1) * CAP
+    tiles = width // 128
+    full_s[...] = jnp.zeros(full_s.shape, F32)
+    for d in range(full_s.shape[0] // 8):
+        for l in range(tiles):
+            start = (d * tiles + l) * used
+            full_s[8 * d : 8 * d + used, l * 128 : (l + 1) * 128] = got_ref[start : start + used, :]
+    got = full_s[...].astype(BF16)
     shape = (buckets, got.shape[0])
     window = []
     for j in range(taps_ref.shape[0] - 1):
@@ -180,11 +193,13 @@
     shape = (slots, buckets)
     hit = arriving & (col == iota(shape, 1) // CAP) & (rank == iota(shape, 1) % CAP)
     pick = jnp.where(hit, 1.0, 0.0).astype(BF16)
+    copies = []
     for t in range(steps):
         moved = dot_n(pick, outs[t])
-        conv_s[t * slots : (t + 1) * slots, :] = jnp.where(arriving, moved, conv_ref[t].astype(F32)).astype(BF16)
-    copy = pltpu.make_async_copy(conv_s, conv_out, sems.at[0])
-    copy.start()
+        rows = pl.ds(t * slots, slots)
+        conv_s[rows, :] = jnp.where(arriving, moved, conv_ref[t].astype(F32)).astype(BF16)
+        copies.append(pltpu.make_async_copy(conv_s.at[rows], conv_out.at[rows], sems.at[t]))
+        copies[t].start()
     lhs = conv_s[...]
     mix[...] = dot_t(lhs, proj_ref[0:width, :])
     rest = proj_ref.shape[0] - width
@@ -201,7 +216,8 @@
                 for g in range(quarter // 8):
                     lane = 32 * (t * (quarter // 8) + g)
                     out[steps * quarter :, lane : lane + rest] = low[pl.ds(start + 8 * g, 8), 0:rest]
-    copy.wait()
+    for copy in copies:
+        copy.wait()
 
 
 def prepare(pos_ref, active_ref, pieces_x, pieces_y, conv_ref, dtw_ref, dtb_ref,
@@ -232,47 +248,24 @@
         step_ref[rows, :] = jnp.where(alive, soft, 0.0)
 
 
-def scan_kernel(pos_ref, plan_ref, active_hbm, x0, x1, x2, x3, y0, y1, y2, y3, got_ref,
-                conv_hbm, z_hbm, dtw_hbm, dtb_hbm, rate_hbm, gain_hbm, state_ref,
-                gated_ref, out_ref, alive_s, rate_s, state_s, step_s, conv_s, low_s, rank_s,
-                active_ref, conv_ref, z_ref, dtw_ref, dtb_ref, rate_ref, gain_ref,
-                in_sems, out_sems, sems):
-    steps, slots, width = z_ref.shape
-    states = rate_ref.shape[0]
-    block = slots // in_sems.shape[0]
-    tiles = width // 128
-
-    def load(i, l):
-        rows = pl.ds(i * block * states, block * states)
-        return pltpu.make_async_copy(state_ref.at[rows, pl.ds(l * 128, 128)], state_s.at[l, rows], in_sems.at[i, l])
-
-    def store(i, l):
-        rows = pl.ds(i * block * states, block * states)
-        return pltpu.make_async_copy(state_s.at[l, rows], out_ref.at[rows, pl.ds(l * 128, 128)], out_sems.at[i, l])
-
-    copies = fetch(
-        ((active_hbm, active_ref), (dtw_hbm, dtw_ref), (dtb_hbm, dtb_ref), (conv_hbm, conv_ref),
-         (rate_hbm, rate_ref), (gain_hbm, gain_ref), (z_hbm, z_ref)),
-        sems,
-    )
-    for i in range(slots // block):
-        for l in range(tiles):
-            load(i, l).start()
-    copies[0].wait()
-
-    def ready():
-        for copy in copies[1:]:
-            copy.wait()
-
-    prepare(pos_ref, active_ref, (x0, x1, x2, x3), (y0, y1, y2, y3), conv_ref, dtw_ref, dtb_ref,
-            step_s, conv_s, low_s, rank_s, ready)
-    rate_s[...] = rate_ref[...] * (-1.0 / math.log(2.0))
-    alive = as_column(active_ref[...], slots) == 1
-    alive_s[...] = jnp.broadcast_to(jnp.where(alive, 1.0, 0.0), alive_s.shape)
-    for i in range(slots // block):
-        for l in range(tiles):
-            load(i, l).wait()
-    buckets = got_ref.shape[0] // states
+def stage_kernel(plan_ref, got_ref, state_ref, out_ref, spread_ref, sems):
+    tiles, rows, _ = out_ref.shape
+    buckets = sems.shape[1]
+    states = got_ref.shape[0] // buckets
+    parts = sems.shape[0]
+    copies = []
+    for l in range(tiles):
+        for i in range(parts):
+            here = pl.ds(i * (rows // parts), rows // parts)
+            copies.append(
+                pltpu.make_async_copy(state_ref.at[here, pl.ds(l * 128, 128)], out_ref.at[l, here], sems.at[i, l])
+            )
+    for copy in copies:
+        copy.start()
+    shape = spread_ref.shape
+    spread_ref[...] = jnp.where(iota(shape, 0) % (shape[0] // 2) == iota(shape, 1) // 128, 1.0, 0.0).astype(BF16)
+    for copy in copies:
+        copy.wait()
 
     def patch(b, carry):
         gone = plan_ref[0, b]
@@ -282,24 +275,60 @@
         def _():
             rows = pl.ds(pl.multiple_of(gone * states, states), states)
             for l in range(tiles):
-                state_s[l, rows, :] = jnp.zeros((states, 128), F32)
+                out_ref[l, rows, :] = jnp.zeros((states, 128), F32)
 
         @pl.when(here >= 0)
         def _():
             rows = pl.ds(pl.multiple_of(here * states, states), states)
             there = pl.ds(pl.multiple_of(b * states, states), states)
             for l in range(tiles):
-                state_s[l, rows, :] = got_ref[there, l * 128 : (l + 1) * 128]
+                out_ref[l, rows, :] = got_ref[there, l * 128 : (l + 1) * 128]
 
         return carry
 
     lax.fori_loop(0, buckets, patch, 0)
+
+
+PIECES = (48, 32, 16, 16, 16)
+
+
+def scan_kernel(pos_ref, active_ref, x0, x1, x2, x3, y0, y1, y2, y3, state_s,
+                spread_ref, conv_ref, gate_ref, dtw_ref, dtb_ref, rate_ref, gain_ref,
+                gated_out, out_ref, alive_s, rate_s, final_s, step_s, conv_s, low_s, rank_s, gated_ref, wide_s,
+                out_sems):
+    steps, slots, width = gate_ref.shape
+    states = rate_ref.shape[0]
+    tiles = width // 128
+
+    def stores(k):
+        first = sum(PIECES[:k])
+        slots_here = pl.ds(first, PIECES[k])
+        rows = pl.ds(first * states, PIECES[k] * states)
+        copies = [pltpu.make_async_copy(gated_ref.at[:, slots_here], gated_out.at[:, slots_here], out_sems.at[k, tiles])]
+        for l in range(tiles):
+            copies.append(
+                pltpu.make_async_copy(final_s.at[l, rows], out_ref.at[rows, pl.ds(l * 128, 128)], out_sems.at[k, l])
+            )
+        return copies
+
+    def ready():
+        pass
+
+    prepare(pos_ref, active_ref, (x0, x1, x2, x3), (y0, y1, y2, y3), conv_ref, dtw_ref, dtb_ref,
+            step_s, conv_s, low_s, rank_s, ready)
+    rest = 2 * states
+    high = low_s[:, 0:rest].astype(BF16)
+    rounding = (low_s[:, 0:rest] - high.astype(F32)).astype(BF16)
+    wide_s[...] = dot_n(jnp.concatenate([high, rounding], axis=1), spread_ref[...])
+    rate_s[...] = rate_ref[...] * (-1.0 / math.log(2.0))
+    alive = as_column(active_ref[...], slots) == 1
+    alive_s[...] = jnp.broadcast_to(jnp.where(alive, 1.0, 0.0), alive_s.shape)
 
     def group(base):
         dts, dxs, lows, accs = [], [], [], []
         for t in range(steps):
             rows = pl.ds(pl.multiple_of(t * slots + base, 8), 8)
-            lows.append(low_s[rows, :])
+            lows.append(rows)
             for l in range(tiles):
                 lanes = slice(l * 128, (l + 1) * 128)
                 dt = step_s[rows, lanes]
@@ -309,8 +338,8 @@
                 accs.append(gain_ref[:, lanes] * cv)
         for n in range(states):
             place = pl.ds(base * states + n, 8, stride=states)
-            gives = [jnp.broadcast_to(low[:, n : n + 1], (8, 128)) for low in lows]
-            takes = [jnp.broadcast_to(low[:, states + n : states + n + 1], (8, 128)) for low in lows]
+            gives = [wide_s[rows, n * 128 : (n + 1) * 128] for rows in lows]
+            takes = [wide_s[rows, (states + n) * 128 : (states + n + 1) * 128] for rows in lows]
             for l in range(tiles):
                 st = state_s[l, place, :]
                 rate = rate_s[n : n + 1, l * 128 : (l + 1) * 128]
@@ -318,7 +347,7 @@
                     k = t * tiles + l
                     st = jnp.exp2(dts[k] * rate) * st + dxs[k] * gives[t]
                     accs[k] = accs[k] + st * takes[t]
-                state_s[l, place, :] = st
+                final_s[l, place, :] = st
         return accs
 
     def pair(i, carry):
@@ -328,21 +357,26 @@
         for t in range(steps):
             for l in range(tiles):
                 lanes = slice(l * 128, (l + 1) * 128)
-                gate = jax.nn.silu(z_ref[t, pl.ds(base, 16), lanes].astype(F32))
+                gate = jax.nn.silu(gate_ref[t, pl.ds(base, 16), lanes].astype(F32))
                 value = jnp.concatenate([accs[0][t * tiles + l], accs[1][t * tiles + l]], axis=0) * gate
                 gated_ref[t, pl.ds(base, 16), lanes] = jnp.where(on, value, 0.0).astype(BF16)
         return carry
 
-    def chunk(i, carry):
-        lax.fori_loop(i * (block // 16), (i + 1) * (block // 16), pair, 0)
-        for l in range(tiles):
-            store(i, l).start()
+    def block(i, carry):
+        pair(i, carry)
+        for k in range(len(PIECES)):
+
+            @pl.when(i == sum(PIECES[: k + 1]) // 16 - 1)
+            def _():
+                for copy in stores(k):
+                    copy.start()
+
         return carry
 
-    lax.fori_loop(0, slots // block, chunk, 0)
-    for i in range(slots // block):
-        for l in range(tiles):
-            store(i, l).wait()
+    lax.fori_loop(0, slots // 16, block, 0)
+    for k in range(len(PIECES)):
+        for copy in stores(k):
+            copy.wait()
 
 
 def in_hbm(value):
@@ -367,15 +401,17 @@
     state_rows = in_hbm(ssm_state.reshape(slots * states, width))
     sds = jax.ShapeDtypeStruct
 
+    compact = (taps - 1) * CAP * (width // 128)
     out_cache, plan = pl.pallas_call(
         pick_cache_kernel,
-        out_shape=(sds((peers * 8, width), F32), sds((2, slots), jnp.int32)),
+        out_shape=(sds((peers * compact, 128), F32), sds((2, slots), jnp.int32)),
         in_specs=[SM, HB, HB, HB],
         out_specs=(VM, VM),
         scratch_shapes=[
             pltpu.VMEM((1, slots), jnp.int32),
             pltpu.VMEM((1, slots), jnp.int32),
             pltpu.VMEM(cache.shape, BF16),
+            pltpu.VMEM((peers * 8, width), F32),
             pltpu.SemaphoreType.DMA((3,)),
         ],
         compiler_params=pltpu.CompilerParams(vmem_limit_bytes=4 * MIB),
@@ -383,8 +419,8 @@
     )(pos, send_row, recv_row, cache)
     both = jnp.transpose(projected, (2, 0, 1, 3))
     got_cache = lax.all_to_all(
-        out_cache.reshape(peers, 8, width), "req", split_axis=0, concat_axis=0, tiled=True
-    ).reshape(peers * 8, width)
+        out_cache.reshape(peers, compact, 128), "req", split_axis=0, concat_axis=0, tiled=True
+    ).reshape(peers * compact, 128)
 
     out_state = pl.pallas_call(
         pick_state_kernel,
@@ -402,7 +438,7 @@
     )(plan, state_rows)
 
     total = steps * slots
-    conv_main, z_part, cache_out, x_arr = pl.pallas_call(
+    conv_main, gate, cache_out, x_arr = pl.pallas_call(
         conv_kernel,
         out_shape=(
             sds((steps, slots, width), BF16),
@@ -434,10 +470,11 @@
         in_specs=[SM] + [VM] * 7,
         out_specs=(HB,) + (VM,) * (2 * SIDE),
         scratch_shapes=[
-            pltpu.VMEM((total, width), BF16),
             pltpu.VMEM((total, width), F32),
             pltpu.VMEM((total, 128), F32),
-            pltpu.SemaphoreType.DMA((1,)),
+            pltpu.VMEM((peers * 8, width), F32),
+            pltpu.VMEM((total, width), BF16),
+            pltpu.SemaphoreType.DMA((3,)),
         ],
         compiler_params=pltpu.CompilerParams(vmem_limit_bytes=8 * MIB),
         name="project",
@@ -460,36 +497,40 @@
     last_x = gathered(all_a, 0, [all_a] * 3)
     last_y = gathered(all_b, 1, [all_b] * 3)
 
+    tiles = width // 128
+    staged, spread = pl.pallas_call(
+        stage_kernel,
+        out_shape=(sds((tiles, slots * states, 128), F32), sds((4 * states, 2 * states * 128), BF16)),
+        in_specs=[SM, VM, HB],
+        out_specs=(VM, VM),
+        scratch_shapes=[pltpu.SemaphoreType.DMA((1, buckets))],
+        compiler_params=pltpu.CompilerParams(vmem_limit_bytes=8 * MIB),
+        cost_estimate=pl.CostEstimate(flops=0, bytes_accessed=12 * MIB, transcendentals=0),
+        name="stage_state",
+    )(plan, got_state.reshape(buckets * states, width), state_rows)
+
     gated_out, state_out = pl.pallas_call(
         scan_kernel,
         out_shape=(sds((steps, slots, width), BF16), sds((slots * states, width), F32)),
-        in_specs=[SM, SM, HB] + [VM] * 9 + [HB] * 7,
-        out_specs=(VM, HB),
+        in_specs=[SM] + [VM] * 17,
+        out_specs=(HB, HB),
         scratch_shapes=[
             pltpu.VMEM((slots, 128), F32),
             pltpu.VMEM((states, width), F32),
-            pltpu.VMEM((width // 128, slots * states, 128), F32),
+            pltpu.VMEM((tiles, slots * states, 128), F32),
             pltpu.VMEM((total, width), F32),
             pltpu.VMEM((total, width), F32),
             pltpu.VMEM((total, 128), F32),
             pltpu.VMEM((total, width), BF16),
-            pltpu.VMEM((1, slots), jnp.int32),
-            pltpu.VMEM((total, width), BF16),
             pltpu.VMEM((steps, slots, width), BF16),
-            pltpu.VMEM(dtproj_weight.shape, BF16),
-            pltpu.VMEM((1, width), F32),
-            pltpu.VMEM((states, width), F32),
-            pltpu.VMEM((1, width), F32),
-            pltpu.SemaphoreType.DMA((4, width // 128)),
-            pltpu.SemaphoreType.DMA((4, width // 128)),
-            pltpu.SemaphoreType.DMA((7,)),
+            pltpu.VMEM((total, 2 * states * 128), F32),
+            pltpu.SemaphoreType.DMA((len(PIECES), tiles + 1)),
         ],
         compiler_params=pltpu.CompilerParams(vmem_limit_bytes=20 * MIB),
         name="scan",
     )(
-        pos, plan, active_row, *last_x, *last_y, got_state.reshape(buckets * states, width),
-        in_hbm(conv_all), in_hbm(z_part), in_hbm(dtproj_weight), in_hbm(dt_row),
-        in_hbm(a_rate), in_hbm(gain), state_rows,
+        pos, active.reshape(1, slots), *last_x, *last_y, staged, spread, conv_all, gate, dtproj_weight, dt_row,
+        a_rate, gain,
     )
     return (
         gated_out,

time: 78.4 us -> 73.7 us (0.940)
  waiting for transfers between devices: 12.4 us -> 7.41 us
    pallas_call x1, Pallas kernels: 11.9 us -> 7.95 us  [on_device(): pl.pallas_call(scan_kernel, out_shape=(sds((steps, slots, width), BF16),...]
    ppermute x18, waiting for transfers between devices: 9.2 us -> 5.61 us  [gathered(): lax.ppermute(parts[d - 1], 'wa', shift(axis, d))]
    pallas_call x1 -> x2, Pallas kernels: 2.57 us -> 6.08 us  [the longest x1 3.55 us: on_device(): pl.pallas_call(stage_kernel, out_shape=(sds((tiles, slots * states, 128),...]
    all_to_all x1, waiting for transfers between devices: 3.15 us -> 1.8 us  [on_device(): lax.all_to_all(out_cache.reshape(peers, compact, 128), 'req', split_axis=...]
  transfers between devices with their start and end apart: 20 -> 20, of which waited for: 9 -> 7; matrix products, arithmetic and copies ran while one was open for 0% -> 0% of each run, Pallas kernels for 11% -> 17%
where the time goes in v3:
time: 73.7 us; the launch traced here: 73.2 us
  starting transfers between devices  41.6 us (56%)
  Pallas kernels  22.8 us (31%)
  waiting for transfers between devices  7.41 us (10%)
  between operations  1.08 us (1%)
    ppermute x18, starting transfers between devices, gathered(): lax.ppermute(parts[d - 1], 'wa', shift(axis, d))  27.7 us
    all_to_all x1, starting transfers between devices, on_device(): lax.all_to_all(out_cache.reshape(peers, compact, 128), 'req', split_axis=...  8.6 us
    pallas_call x1, Pallas kernels, on_device(): pl.pallas_call(scan_kernel, out_shape=(sds((steps, slots, width), BF16),...  7.95 us
    ppermute x18, waiting for transfers between devices, gathered(): lax.ppermute(parts[d - 1], 'wa', shift(axis, d))  5.61 us
    all_to_all x1, starting transfers between devices, on_device(): lax.all_to_all(out_state, 'req', split_axis=0, concat_axis=0, tiled=True)  5.33 us
    pallas_call x1, Pallas kernels, on_device(): pl.pallas_call(stage_kernel, out_shape=(sds((tiles, slots * states, 128),...  3.55 us
    pallas_call x1, Pallas kernels, on_device(): pl.pallas_call(pick_state_kernel, out_shape=pltpu.HBM((buckets, states, w...  3.43 us
    pallas_call x1, Pallas kernels, on_device(): pl.pallas_call(conv_kernel, out_shape=(sds((steps, slots, width), BF16),...  3.14 us
  transfers between devices with their start and end apart: 20, of which 7 were waited for; matrix products, arithmetic and copies ran while one was open for 0% of the time, Pallas kernels for 17%

profile of v3, /device:TPU:32, one launch (start us, length us, event | category | flops | bytes accessed | tf_op | source)
XLA Modules:
  0.0 73.2 jit_solution(8983544777899014800)
XLA Ops:
  0.7 2.5 %pick_cache.1 = (f32[384,128]{1,0:T(8,128)}, s32[2,128]{1,0:T(2,128)S(1)}) custom-call(s32[3]{0:T(128)S(1)} %pad_add_fusion.pos_ref, s32[1,128]{1,0:T(1,128)} %bitcast.37, s32[1,128]{1,0:T(1,128)} %bitcast.26, bf16[3,128,512]{2,1,0:T(8,128)(2,1)} %bitcast.35), custom_call_target="tpu_custom_call" | custom-call | tf_op jit(solution)/shard_map/pick_cache/pallas_call | solution.py:405
  3.3 8.6 %all-to-all-start = ((f32[16,24,128]{2,1,0:T(8,128)}), f32[16,24,128]{2,1,0:T(8,128)S(1)}, u32[]{:S(2)}, u32[]{:S(2)}) async-start(f32[16,24,128]{2,1,0:T(8,128)} %bitcast.7), calls=%async_computation | async-start | bytes 393216 | tf_op jit(solution)/shard_map/all_to_all | solution.py:421
  11.9 3.4 %pick_state.1 = f32[32,16,512]{2,1,0:T(8,128)} custom-call(s32[2,128]{1,0:T(2,128)S(1)} %get-tuple-element.26.plan_ref, f32[2048,512]{1,0:T(8,128)} %bitcast.33), custom_call_target="tpu_custom_call" | custom-call | flops 1 | bytes 1 | tf_op jit(solution)/shard_map/pick_state/pallas_call | solution.py:425
  15.5 3.1 %convolve.1 = (bf16[3,128,512]{2,1,0:T(8,128)(2,1)S(1)}, bf16[3,128,512]{2,1,0:T(8,128)(2,1)}, bf16[3,128,512]{2,1,0:T(8,128)(2,1)}, bf16[96,512]{1,0:T(8,128)(2,1)S(1)}) custom-call(s32[3]{0:T(128)S(1)} %pad_add_fusion.pos_ref, s32[1,128]{1,0:T(1,128)} %bitcast.38, s32[1,128]{1,0:T(1,128)} %bitcast.27, s32[1,128]{1,0:T(1,128)} %bitcast.31, ...), custom_call_target="tpu_custom_call" | custom-call | tf_op jit(solution)/shard_map/convolve/pallas_call | solution.py:441
  18.6 1.8 %all-to-all-done = f32[16,24,128]{2,1,0:T(8,128)S(1)} async-done(((f32[16,24,128]{2,1,0:T(8,128)}), f32[16,24,128]{2,1,0:T(8,128)S(1)}, u32[]{:S(2)}, u32[]{:S(2)}) %all-to-all-start) | async-done | bytes 196640 | tf_op jit(solution)/shard_map/all_to_all | solution.py:421
  20.4 5.3 %all-to-all-start.1 = ((f32[32,16,512]{2,1,0:T(8,128)}), f32[32,16,512]{2,1,0:T(8,128)S(1)}, u32[]{:S(2)}, u32[]{:S(2)}) async-start(f32[32,16,512]{2,1,0:T(8,128)} %pick_state.1), calls=%async_computation.1 | async-start | bytes 2097152 | tf_op jit(solution)/shard_map/all_to_all | solution.py:494
  25.8 2.2 %project.1 = (bf16[384,512]{1,0:T(8,128)(2,1)}, f32[56,512]{1,0:T(8,128)S(1)}, f32[56,512]{1,0:T(8,128)S(1)}, f32[56,512]{1,0:T(8,128)S(1)}, f32[56,512]{1,0:T(8...) custom-call(s32[3]{0:T(128)S(1)} %pad_add_fusion.pos_ref, ...), custom_call_target="tpu_custom_call" | custom-call | tf_op jit(solution)/shard_map/project/pallas_call | solution.py:467
  28.0 1.6 %collective-permute-start = (f32[56,512]{1,0:T(8,128)S(1)}, f32[56,512]{1,0:T(8,128)S(1)}, u32[]{:S(2)}, u32[]{:S(2)}) collective-permute-start(f32[56,512]{1,0:T(8,128)S(1)} %get-tuple-element.32), channel_id=1, source_target_pairs={{0,4},{1,5},{2,6},{3,7},{4,8},{5,9},{6,10},{7,11},{8,12},{9,13},{1... | collective-permute-start | bytes 344072 | tf_op jit(solution)/shard_map/ppermute | solution.py:486
  29.6 2.7 %collective-permute-start.1 = (f32[56,512]{1,0:T(8,128)S(1)}, f32[56,512]{1,0:T(8,128)S(1)}, u32[]{:S(2)}, u32[]{:S(2)}) collective-permute-start(f32[56,512]{1,0:T(8,128)S(1)} %get-tuple-element.33), channel_id=1, source_target_pairs={{0,8},{1,9},{2,10},{3,11},{4,12},{5,13},{6,14},{7,15},{8,0},{9,1},... | collective-permute-start | bytes 344072 | tf_op jit(solution)/shard_map/ppermute | solution.py:486
  32.3 1.4 %collective-permute-start.2 = (f32[56,512]{1,0:T(8,128)S(1)}, f32[56,512]{1,0:T(8,128)S(1)}, u32[]{:S(2)}, u32[]{:S(2)}) collective-permute-start(f32[56,512]{1,0:T(8,128)S(1)} %get-tuple-element.34), channel_id=1, source_target_pairs={{0,12},{1,13},{2,14},{3,15},{4,0},{5,1},{6,2},{7,3},{8,4},{9,5},{1... | collective-permute-start | bytes 344072 | tf_op jit(solution)/shard_map/ppermute | solution.py:486
  33.8 1.6 %collective-permute-start.9 = (f32[56,512]{1,0:T(8,128)S(1)}, f32[56,512]{1,0:T(8,128)S(1)}, u32[]{:S(2)}, u32[]{:S(2)}) collective-permute-start(f32[56,512]{1,0:T(8,128)S(1)} %get-tuple-element.36), channel_id=1, source_target_pairs={{0,1},{1,2},{2,3},{3,0},{4,5},{5,6},{6,7},{7,4},{8,9},{9,10},{10,1... | collective-permute-start | bytes 344072 | tf_op jit(solution)/shard_map/ppermute | solution.py:486
  35.3 2.9 %collective-permute-start.10 = (f32[56,512]{1,0:T(8,128)S(1)}, f32[56,512]{1,0:T(8,128)S(1)}, u32[]{:S(2)}, u32[]{:S(2)}) collective-permute-start(f32[56,512]{1,0:T(8,128)S(1)} %get-tuple-element.37), channel_id=1, source_target_pairs={{0,2},{1,3},{2,0},{3,1},{4,6},{5,7},{6,4},{7,5},{8,10},{9,11},{10,... | collective-permute-start | bytes 344072 | tf_op jit(solution)/shard_map/ppermute | solution.py:486
  38.3 1.3 %collective-permute-start.11 = (f32[56,512]{1,0:T(8,128)S(1)}, f32[56,512]{1,0:T(8,128)S(1)}, u32[]{:S(2)}, u32[]{:S(2)}) collective-permute-start(f32[56,512]{1,0:T(8,128)S(1)} %get-tuple-element.38), channel_id=1, source_target_pairs={{0,3},{1,0},{2,1},{3,2},{4,7},{5,4},{6,5},{7,6},{8,11},{9,8},{10,9... | collective-permute-start | bytes 344072 | tf_op jit(solution)/shard_map/ppermute | solution.py:486
  39.7 1.5 %collective-permute-start.5 = (f32[56,512]{1,0:T(8,128)S(1)}, f32[56,512]{1,0:T(8,128)S(1)}, u32[]{:S(2)}, u32[]{:S(2)}) collective-permute-start(f32[56,512]{1,0:T(8,128)S(1)} %add_add_fusion.3), channel_id=1, source_target_pairs={{0,3},{1,0},{2,1},{3,2},{4,7},{5,4},{6,5},{7,6},{8,11},{9,8},{10,9... | collective-permute-start | bytes 344072 | tf_op jit(solution)/shard_map/ppermute | solution.py:486
  41.1 1.4 %collective-permute-start.4 = (f32[56,512]{1,0:T(8,128)S(1)}, f32[56,512]{1,0:T(8,128)S(1)}, u32[]{:S(2)}, u32[]{:S(2)}) collective-permute-start(f32[56,512]{1,0:T(8,128)S(1)} %add_add_fusion.3), channel_id=1, source_target_pairs={{0,2},{1,3},{2,0},{3,1},{4,6},{5,7},{6,4},{7,5},{8,10},{9,11},{10,... | collective-permute-start | bytes 344072 | tf_op jit(solution)/shard_map/ppermute | solution.py:486
  43.1 1.3 %collective-permute-done.11 = f32[56,512]{1,0:T(8,128)S(1)} collective-permute-done((f32[56,512]{1,0:T(8,128)S(1)}, f32[56,512]{1,0:T(8,128)S(1)}, u32[]{:S(2)}, u32[]{:S(2)}) %collective-permute-start.11) | collective-permute-done | bytes 114720 | tf_op jit(solution)/shard_map/ppermute | solution.py:486
  45.1 2.0 %collective-permute-start.13 = (f32[56,512]{1,0:T(8,128)S(1)}, f32[56,512]{1,0:T(8,128)S(1)}, u32[]{:S(2)}, u32[]{:S(2)}) collective-permute-start(f32[56,512]{1,0:T(8,128)S(1)} %add_add_fusion.1), channel_id=1, source_target_pairs={{0,8},{1,9},{2,10},{3,11},{4,12},{5,13},{6,14},{7,15},{8,0},{9,1},... | collective-permute-start | bytes 344072 | tf_op jit(solution)/shard_map/ppermute | solution.py:486
  48.0 1.2 %collective-permute-done.3 = f32[56,512]{1,0:T(8,128)S(1)} collective-permute-done((f32[56,512]{1,0:T(8,128)S(1)}, f32[56,512]{1,0:T(8,128)S(1)}, u32[]{:S(2)}, u32[]{:S(2)}) %collective-permute-start.3) | collective-permute-done | bytes 114720 | tf_op jit(solution)/shard_map/ppermute | solution.py:486
  49.2 2.3 %collective-permute-start.8 = (f32[56,512]{1,0:T(8,128)S(1)}, f32[56,512]{1,0:T(8,128)S(1)}, u32[]{:S(2)}, u32[]{:S(2)}) collective-permute-start(f32[56,512]{1,0:T(8,128)S(1)} %add_add_fusion.2.x0), channel_id=1, source_target_pairs={{0,12},{1,13},{2,14},{3,15},{4,0},{5,1},{6,2},{7,3},{8,4},{9,5},{1... | collective-permute-start | bytes 344072 | tf_op jit(solution)/shard_map/ppermute | solution.py:486
  53.2 4.4 %collective-permute-start.17 = (f32[56,512]{1,0:T(8,128)S(1)}, f32[56,512]{1,0:T(8,128)S(1)}, u32[]{:S(2)}, u32[]{:S(2)}) collective-permute-start(f32[56,512]{1,0:T(8,128)S(1)} %add_add_fusion.y0), channel_id=1, source_target_pairs={{0,3},{1,0},{2,1},{3,2},{4,7},{5,4},{6,5},{7,6},{8,11},{9,8},{10,9... | collective-permute-start | bytes 344072 | tf_op jit(solution)/shard_map/ppermute | solution.py:486
  57.5 1.3 %collective-permute-start.16 = (f32[56,512]{1,0:T(8,128)S(1)}, f32[56,512]{1,0:T(8,128)S(1)}, u32[]{:S(2)}, u32[]{:S(2)}) collective-permute-start(f32[56,512]{1,0:T(8,128)S(1)} %add_add_fusion.y0), channel_id=1, source_target_pairs={{0,2},{1,3},{2,0},{3,1},{4,6},{5,7},{6,4},{7,5},{8,10},{9,11},{10,... | collective-permute-start | bytes 344072 | tf_op jit(solution)/shard_map/ppermute | solution.py:486
  59.3 3.5 %stage_state.1 = (f32[4,2048,128]{2,1,0:T(8,128)S(1)}, bf16[64,4096]{1,0:T(8,128)(2,1)S(1)}) custom-call(s32[2,128]{1,0:T(2,128)S(1)} %get-tuple-element.26.plan_ref, f32[512,512]{1,0:T(8,128)S(1)} %bitcast.20, f32[2048,512]{1,0:T(8,128)} %bitcast.34), custom_call_target="tpu_custom_call" | custom-call | bytes 12582912 | tf_op jit(solution)/shard_map/stage_state/pallas_call | solution.py:501
  63.8 1.2 %collective-permute-done.15.y1 = f32[56,512]{1,0:T(8,128)S(1)} collective-permute-done((f32[56,512]{1,0:T(8,128)S(1)}, f32[56,512]{1,0:T(8,128)S(1)}, u32[]{:S(2)}, u32[]{:S(2)}) %collective-permute-start.15) | collective-permute-done | bytes 114720 | tf_op jit(solution)/shard_map/ppermute | solution.py:486
  65.1 7.9 %scan.1 = (bf16[3,128,512]{2,1,0:T(8,128)(2,1)}, f32[2048,512]{1,0:T(8,128)}) custom-call(s32[3]{0:T(128)S(1)} %pad_add_fusion.pos_ref, s32[1,128]{1,0:T(1,128)S(1)} %bitcast.32, f32[56,512]{1,0:T(8,128)S(1)} %add_add_fusion.2.x0, f32[56,512]{1,0:T(8,128)S(1)} %collective-permute-done.6.x1, f32[56,512]{1,0:T(8,128)S(1)} %collective-permute-done.7.x2, ...), custom_call_target="tpu_custom_call" | custom-call | tf_op jit(solution)/shard_map/scan/pallas_call | solution.py:512
  (52 shorter events, 5.6 us)
Async XLA Ops:
  3.3 17.1 %all-to-all-start = ((f32[16,24,128]{2,1,0:T(8,128)}), f32[16,24,128]{2,1,0:T(8,128)S(1)}, u32[]{:S(2)}, u32[]{:S(2)}) async-start(f32[16,24,128]{2,1,0:T(8,128)} %bitcast.7), calls=%async_computation | async-start | bytes 393216 | tf_op jit(solution)/shard_map/all_to_all | solution.py:421
  20.4 38.9 %all-to-all-start.1 = ((f32[32,16,512]{2,1,0:T(8,128)}), f32[32,16,512]{2,1,0:T(8,128)S(1)}, u32[]{:S(2)}, u32[]{:S(2)}) async-start(f32[32,16,512]{2,1,0:T(8,128)} %pick_state.1), calls=%async_computation.1 | async-start | bytes 2097152 | tf_op jit(solution)/shard_map/all_to_all | solution.py:494
  25.8 39.3 %copy-start.1 = (bf16[512,512]{1,0:T(8,128)(2,1)S(1)}, bf16[512,512]{1,0:T(8,128)(2,1)}, u32[]{:S(2)}) copy-start(bf16[512,512]{1,0:T(8,128)(2,1)} %dtw_ref.1) | copy-start | bytes 1572868
  25.8 39.3 %copy-start.2 = (bf16[3,128,512]{2,1,0:T(8,128)(2,1)S(1)}, bf16[3,128,512]{2,1,0:T(8,128)(2,1)}, u32[]{:S(2)}) copy-start(bf16[3,128,512]{2,1,0:T(8,128)(2,1)} %get-tuple-element.43.gate_ref) | copy-start | bytes 1179652
  25.8 39.2 %copy-start.4 = (f32[16,512]{1,0:T(8,128)S(1)}, f32[16,512]{1,0:T(8,128)}, u32[]{:S(2)}) copy-start(f32[16,512]{1,0:T(8,128)} %rate_ref.1) | copy-start | bytes 98308
  25.8 39.2 %copy-start.8 = (f32[512]{0:T(512)S(1)}, f32[512]{0:T(512)}, u32[]{:S(2)}) copy-start(f32[512]{0:T(512)} %param.18) | copy-start | bytes 6148
  28.0 10.2 %collective-permute-start = (f32[56,512]{1,0:T(8,128)S(1)}, f32[56,512]{1,0:T(8,128)S(1)}, u32[]{:S(2)}, u32[]{:S(2)}) collective-permute-start(f32[56,512]{1,0:T(8,128)S(1)} %get-tuple-element.32), channel_id=1, source_target_pairs={{0,4},{1,5},{2,6},{3,7},{4,8},{5,9},{6,10},{7,11},{8,12},{9,13},{1... | collective-permute-start | bytes 344072 | tf_op jit(solution)/shard_map/ppermute | solution.py:486
  29.6 10.0 %collective-permute-start.1 = (f32[56,512]{1,0:T(8,128)S(1)}, f32[56,512]{1,0:T(8,128)S(1)}, u32[]{:S(2)}, u32[]{:S(2)}) collective-permute-start(f32[56,512]{1,0:T(8,128)S(1)} %get-tuple-element.33), channel_id=1, source_target_pairs={{0,8},{1,9},{2,10},{3,11},{4,12},{5,13},{6,14},{7,15},{8,0},{9,1},... | collective-permute-start | bytes 344072 | tf_op jit(solution)/shard_map/ppermute | solution.py:486
  32.3 7.3 %collective-permute-start.2 = (f32[56,512]{1,0:T(8,128)S(1)}, f32[56,512]{1,0:T(8,128)S(1)}, u32[]{:S(2)}, u32[]{:S(2)}) collective-permute-start(f32[56,512]{1,0:T(8,128)S(1)} %get-tuple-element.34), channel_id=1, source_target_pairs={{0,12},{1,13},{2,14},{3,15},{4,0},{5,1},{6,2},{7,3},{8,4},{9,5},{1... | collective-permute-start | bytes 344072 | tf_op jit(solution)/shard_map/ppermute | solution.py:486
  33.8 8.7 %collective-permute-start.9 = (f32[56,512]{1,0:T(8,128)S(1)}, f32[56,512]{1,0:T(8,128)S(1)}, u32[]{:S(2)}, u32[]{:S(2)}) collective-permute-start(f32[56,512]{1,0:T(8,128)S(1)} %get-tuple-element.36), channel_id=1, source_target_pairs={{0,1},{1,2},{2,3},{3,0},{4,5},{5,6},{6,7},{7,4},{8,9},{9,10},{10,1... | collective-permute-start | bytes 344072 | tf_op jit(solution)/shard_map/ppermute | solution.py:486
  35.3 7.7 %collective-permute-start.10 = (f32[56,512]{1,0:T(8,128)S(1)}, f32[56,512]{1,0:T(8,128)S(1)}, u32[]{:S(2)}, u32[]{:S(2)}) collective-permute-start(f32[56,512]{1,0:T(8,128)S(1)} %get-tuple-element.37), channel_id=1, source_target_pairs={{0,2},{1,3},{2,0},{3,1},{4,6},{5,7},{6,4},{7,5},{8,10},{9,11},{10,... | collective-permute-start | bytes 344072 | tf_op jit(solution)/shard_map/ppermute | solution.py:486
  38.3 6.1 %collective-permute-start.11 = (f32[56,512]{1,0:T(8,128)S(1)}, f32[56,512]{1,0:T(8,128)S(1)}, u32[]{:S(2)}, u32[]{:S(2)}) collective-permute-start(f32[56,512]{1,0:T(8,128)S(1)} %get-tuple-element.38), channel_id=1, source_target_pairs={{0,3},{1,0},{2,1},{3,2},{4,7},{5,4},{6,5},{7,6},{8,11},{9,8},{10,9... | collective-permute-start | bytes 344072 | tf_op jit(solution)/shard_map/ppermute | solution.py:486
  39.7 7.5 %collective-permute-start.5 = (f32[56,512]{1,0:T(8,128)S(1)}, f32[56,512]{1,0:T(8,128)S(1)}, u32[]{:S(2)}, u32[]{:S(2)}) collective-permute-start(f32[56,512]{1,0:T(8,128)S(1)} %add_add_fusion.3), channel_id=1, source_target_pairs={{0,3},{1,0},{2,1},{3,2},{4,7},{5,4},{6,5},{7,6},{8,11},{9,8},{10,9... | collective-permute-start | bytes 344072 | tf_op jit(solution)/shard_map/ppermute | solution.py:486
  41.1 6.9 %collective-permute-start.4 = (f32[56,512]{1,0:T(8,128)S(1)}, f32[56,512]{1,0:T(8,128)S(1)}, u32[]{:S(2)}, u32[]{:S(2)}) collective-permute-start(f32[56,512]{1,0:T(8,128)S(1)} %add_add_fusion.3), channel_id=1, source_target_pairs={{0,2},{1,3},{2,0},{3,1},{4,6},{5,7},{6,4},{7,5},{8,10},{9,11},{10,... | collective-permute-start | bytes 344072 | tf_op jit(solution)/shard_map/ppermute | solution.py:486
  42.5 6.7 %collective-permute-start.3 = (f32[56,512]{1,0:T(8,128)S(1)}, f32[56,512]{1,0:T(8,128)S(1)}, u32[]{:S(2)}, u32[]{:S(2)}) collective-permute-start(f32[56,512]{1,0:T(8,128)S(1)} %add_add_fusion.3), channel_id=1, source_target_pairs={{0,1},{1,2},{2,3},{3,0},{4,5},{5,6},{6,7},{7,4},{8,9},{9,10},{10,1... | collective-permute-start | bytes 344072 | tf_op jit(solution)/shard_map/ppermute | solution.py:486
  44.4 8.1 %collective-permute-start.14 = (f32[56,512]{1,0:T(8,128)S(1)}, f32[56,512]{1,0:T(8,128)S(1)}, u32[]{:S(2)}, u32[]{:S(2)}) collective-permute-start(f32[56,512]{1,0:T(8,128)S(1)} %add_add_fusion.1), channel_id=1, source_target_pairs={{0,12},{1,13},{2,14},{3,15},{4,0},{5,1},{6,2},{7,3},{8,4},{9,5},{1... | collective-permute-start | bytes 344072 | tf_op jit(solution)/shard_map/ppermute | solution.py:486
  45.1 8.0 %collective-permute-start.13 = (f32[56,512]{1,0:T(8,128)S(1)}, f32[56,512]{1,0:T(8,128)S(1)}, u32[]{:S(2)}, u32[]{:S(2)}) collective-permute-start(f32[56,512]{1,0:T(8,128)S(1)} %add_add_fusion.1), channel_id=1, source_target_pairs={{0,8},{1,9},{2,10},{3,11},{4,12},{5,13},{6,14},{7,15},{8,0},{9,1},... | collective-permute-start | bytes 344072 | tf_op jit(solution)/shard_map/ppermute | solution.py:486
  47.1 6.0 %collective-permute-start.12 = (f32[56,512]{1,0:T(8,128)S(1)}, f32[56,512]{1,0:T(8,128)S(1)}, u32[]{:S(2)}, u32[]{:S(2)}) collective-permute-start(f32[56,512]{1,0:T(8,128)S(1)} %add_add_fusion.1), channel_id=1, source_target_pairs={{0,4},{1,5},{2,6},{3,7},{4,8},{5,9},{6,10},{7,11},{8,12},{9,13},{1... | collective-permute-start | bytes 344072 | tf_op jit(solution)/shard_map/ppermute | solution.py:486
  49.2 9.6 %collective-permute-start.8 = (f32[56,512]{1,0:T(8,128)S(1)}, f32[56,512]{1,0:T(8,128)S(1)}, u32[]{:S(2)}, u32[]{:S(2)}) collective-permute-start(f32[56,512]{1,0:T(8,128)S(1)} %add_add_fusion.2.x0), channel_id=1, source_target_pairs={{0,12},{1,13},{2,14},{3,15},{4,0},{5,1},{6,2},{7,3},{8,4},{9,5},{1... | collective-permute-start | bytes 344072 | tf_op jit(solution)/shard_map/ppermute | solution.py:486
  51.5 11.4 %collective-permute-start.7 = (f32[56,512]{1,0:T(8,128)S(1)}, f32[56,512]{1,0:T(8,128)S(1)}, u32[]{:S(2)}, u32[]{:S(2)}) collective-permute-start(f32[56,512]{1,0:T(8,128)S(1)} %add_add_fusion.2.x0), channel_id=1, source_target_pairs={{0,8},{1,9},{2,10},{3,11},{4,12},{5,13},{6,14},{7,15},{8,0},{9,1},... | collective-permute-start | bytes 344072 | tf_op jit(solution)/shard_map/ppermute | solution.py:486
  52.5 10.4 %collective-permute-start.6 = (f32[56,512]{1,0:T(8,128)S(1)}, f32[56,512]{1,0:T(8,128)S(1)}, u32[]{:S(2)}, u32[]{:S(2)}) collective-permute-start(f32[56,512]{1,0:T(8,128)S(1)} %add_add_fusion.2.x0), channel_id=1, source_target_pairs={{0,4},{1,5},{2,6},{3,7},{4,8},{5,9},{6,10},{7,11},{8,12},{9,13},{1... | collective-permute-start | bytes 344072 | tf_op jit(solution)/shard_map/ppermute | solution.py:486
  53.2 9.7 %collective-permute-start.17 = (f32[56,512]{1,0:T(8,128)S(1)}, f32[56,512]{1,0:T(8,128)S(1)}, u32[]{:S(2)}, u32[]{:S(2)}) collective-permute-start(f32[56,512]{1,0:T(8,128)S(1)} %add_add_fusion.y0), channel_id=1, source_target_pairs={{0,3},{1,0},{2,1},{3,2},{4,7},{5,4},{6,5},{7,6},{8,11},{9,8},{10,9... | collective-permute-start | bytes 344072 | tf_op jit(solution)/shard_map/ppermute | solution.py:486
  57.5 6.3 %collective-permute-start.16 = (f32[56,512]{1,0:T(8,128)S(1)}, f32[56,512]{1,0:T(8,128)S(1)}, u32[]{:S(2)}, u32[]{:S(2)}) collective-permute-start(f32[56,512]{1,0:T(8,128)S(1)} %add_add_fusion.y0), channel_id=1, source_target_pairs={{0,2},{1,3},{2,0},{3,1},{4,6},{5,7},{6,4},{7,5},{8,10},{9,11},{10,... | collective-permute-start | bytes 344072 | tf_op jit(solution)/shard_map/ppermute | solution.py:486
  58.8 6.2 %collective-permute-start.15 = (f32[56,512]{1,0:T(8,128)S(1)}, f32[56,512]{1,0:T(8,128)S(1)}, u32[]{:S(2)}, u32[]{:S(2)}) collective-permute-start(f32[56,512]{1,0:T(8,128)S(1)} %add_add_fusion.y0), channel_id=1, source_target_pairs={{0,1},{1,2},{2,3},{3,0},{4,5},{5,6},{6,7},{7,4},{8,9},{9,10},{10,1... | collective-permute-start | bytes 344072 | tf_op jit(solution)/shard_map/ppermute | solution.py:486
  (8 other events, 185.7 us)

commit v4 on v3

--- a/solution.py
+++ b/solution.py
@@ -289,7 +289,7 @@
     lax.fori_loop(0, buckets, patch, 0)
 
 
-PIECES = (48, 32, 16, 16, 16)
+PIECES = (64, 48, 16)
 
 
 def scan_kernel(pos_ref, active_ref, x0, x1, x2, x3, y0, y1, y2, y3, state_s,

time: 73.7 us -> 73.5 us (level)
  no operation moved by 1% of the time
where the time goes in v4:
time: 73.5 us; the launch traced here: 73.2 us
  starting transfers between devices  41.7 us (57%)
  Pallas kernels  22.7 us (31%)
  waiting for transfers between devices  7.29 us (10%)
  between operations  1.08 us (1%)
    ppermute x18, starting transfers between devices, gathered(): lax.ppermute(parts[d - 1], 'wa', shift(axis, d))  27.7 us
    all_to_all x1, starting transfers between devices, on_device(): lax.all_to_all(out_cache.reshape(peers, compact, 128), 'req', split_axis=...  8.6 us
    pallas_call x1, Pallas kernels, on_device(): pl.pallas_call(scan_kernel, out_shape=(sds((steps, slots, width), BF16),...  7.77 us
    ppermute x18, waiting for transfers between devices, gathered(): lax.ppermute(parts[d - 1], 'wa', shift(axis, d))  5.53 us
    all_to_all x1, starting transfers between devices, on_device(): lax.all_to_all(out_state, 'req', split_axis=0, concat_axis=0, tiled=True)  5.48 us
    pallas_call x1, Pallas kernels, on_device(): pl.pallas_call(stage_kernel, out_shape=(sds((tiles, slots * states, 128),...  3.62 us
    pallas_call x1, Pallas kernels, on_device(): pl.pallas_call(pick_state_kernel, out_shape=pltpu.HBM((buckets, states, w...  3.47 us
    pallas_call x1, Pallas kernels, on_device(): pl.pallas_call(conv_kernel, out_shape=(sds((steps, slots, width), BF16),...  3.14 us
  transfers between devices with their start and end apart: 20, of which 7 were waited for; matrix products, arithmetic and copies ran while one was open for 0% of the time, Pallas kernels for 17%

profile of v4, /device:TPU:32, one launch (start us, length us, event | category | flops | bytes accessed | tf_op | source)
XLA Modules:
  0.0 73.2 jit_solution(13254550042554636730)
XLA Ops:
  0.7 2.5 %pick_cache.1 = (f32[384,128]{1,0:T(8,128)}, s32[2,128]{1,0:T(2,128)S(1)}) custom-call(s32[3]{0:T(128)S(1)} %pad_add_fusion.pos_ref, s32[1,128]{1,0:T(1,128)} %bitcast.37, s32[1,128]{1,0:T(1,128)} %bitcast.26, bf16[3,128,512]{2,1,0:T(8,128)(2,1)} %bitcast.35), custom_call_target="tpu_custom_call" | custom-call | tf_op jit(solution)/shard_map/pick_cache/pallas_call | solution.py:405
  3.3 8.6 %all-to-all-start = ((f32[16,24,128]{2,1,0:T(8,128)}), f32[16,24,128]{2,1,0:T(8,128)S(1)}, u32[]{:S(2)}, u32[]{:S(2)}) async-start(f32[16,24,128]{2,1,0:T(8,128)} %bitcast.7), calls=%async_computation | async-start | bytes 393216 | tf_op jit(solution)/shard_map/all_to_all | solution.py:421
  11.9 3.5 %pick_state.1 = f32[32,16,512]{2,1,0:T(8,128)} custom-call(s32[2,128]{1,0:T(2,128)S(1)} %get-tuple-element.26.plan_ref, f32[2048,512]{1,0:T(8,128)} %bitcast.33), custom_call_target="tpu_custom_call" | custom-call | flops 1 | bytes 1 | tf_op jit(solution)/shard_map/pick_state/pallas_call | solution.py:425
  15.5 3.1 %convolve.1 = (bf16[3,128,512]{2,1,0:T(8,128)(2,1)S(1)}, bf16[3,128,512]{2,1,0:T(8,128)(2,1)}, bf16[3,128,512]{2,1,0:T(8,128)(2,1)}, bf16[96,512]{1,0:T(8,128)(2,1)S(1)}) custom-call(s32[3]{0:T(128)S(1)} %pad_add_fusion.pos_ref, s32[1,128]{1,0:T(1,128)} %bitcast.38, s32[1,128]{1,0:T(1,128)} %bitcast.27, s32[1,128]{1,0:T(1,128)} %bitcast.31, ...), custom_call_target="tpu_custom_call" | custom-call | tf_op jit(solution)/shard_map/convolve/pallas_call | solution.py:441
  18.6 1.8 %all-to-all-done = f32[16,24,128]{2,1,0:T(8,128)S(1)} async-done(((f32[16,24,128]{2,1,0:T(8,128)}), f32[16,24,128]{2,1,0:T(8,128)S(1)}, u32[]{:S(2)}, u32[]{:S(2)}) %all-to-all-start) | async-done | bytes 196640 | tf_op jit(solution)/shard_map/all_to_all | solution.py:421
  20.4 5.5 %all-to-all-start.1 = ((f32[32,16,512]{2,1,0:T(8,128)}), f32[32,16,512]{2,1,0:T(8,128)S(1)}, u32[]{:S(2)}, u32[]{:S(2)}) async-start(f32[32,16,512]{2,1,0:T(8,128)} %pick_state.1), calls=%async_computation.1 | async-start | bytes 2097152 | tf_op jit(solution)/shard_map/all_to_all | solution.py:494
  26.0 2.2 %project.1 = (bf16[384,512]{1,0:T(8,128)(2,1)}, f32[56,512]{1,0:T(8,128)S(1)}, f32[56,512]{1,0:T(8,128)S(1)}, f32[56,512]{1,0:T(8,128)S(1)}, f32[56,512]{1,0:T(8...) custom-call(s32[3]{0:T(128)S(1)} %pad_add_fusion.pos_ref, ...), custom_call_target="tpu_custom_call" | custom-call | tf_op jit(solution)/shard_map/project/pallas_call | solution.py:467
  28.2 1.6 %collective-permute-start = (f32[56,512]{1,0:T(8,128)S(1)}, f32[56,512]{1,0:T(8,128)S(1)}, u32[]{:S(2)}, u32[]{:S(2)}) collective-permute-start(f32[56,512]{1,0:T(8,128)S(1)} %get-tuple-element.32), channel_id=1, source_target_pairs={{0,4},{1,5},{2,6},{3,7},{4,8},{5,9},{6,10},{7,11},{8,12},{9,13},{1... | collective-permute-start | bytes 344072 | tf_op jit(solution)/shard_map/ppermute | solution.py:486
  29.8 2.7 %collective-permute-start.1 = (f32[56,512]{1,0:T(8,128)S(1)}, f32[56,512]{1,0:T(8,128)S(1)}, u32[]{:S(2)}, u32[]{:S(2)}) collective-permute-start(f32[56,512]{1,0:T(8,128)S(1)} %get-tuple-element.33), channel_id=1, source_target_pairs={{0,8},{1,9},{2,10},{3,11},{4,12},{5,13},{6,14},{7,15},{8,0},{9,1},... | collective-permute-start | bytes 344072 | tf_op jit(solution)/shard_map/ppermute | solution.py:486
  32.5 1.4 %collective-permute-start.2 = (f32[56,512]{1,0:T(8,128)S(1)}, f32[56,512]{1,0:T(8,128)S(1)}, u32[]{:S(2)}, u32[]{:S(2)}) collective-permute-start(f32[56,512]{1,0:T(8,128)S(1)} %get-tuple-element.34), channel_id=1, source_target_pairs={{0,12},{1,13},{2,14},{3,15},{4,0},{5,1},{6,2},{7,3},{8,4},{9,5},{1... | collective-permute-start | bytes 344072 | tf_op jit(solution)/shard_map/ppermute | solution.py:486
  33.9 1.6 %collective-permute-start.9 = (f32[56,512]{1,0:T(8,128)S(1)}, f32[56,512]{1,0:T(8,128)S(1)}, u32[]{:S(2)}, u32[]{:S(2)}) collective-permute-start(f32[56,512]{1,0:T(8,128)S(1)} %get-tuple-element.36), channel_id=1, source_target_pairs={{0,1},{1,2},{2,3},{3,0},{4,5},{5,6},{6,7},{7,4},{8,9},{9,10},{10,1... | collective-permute-start | bytes 344072 | tf_op jit(solution)/shard_map/ppermute | solution.py:486
  35.5 2.9 %collective-permute-start.10 = (f32[56,512]{1,0:T(8,128)S(1)}, f32[56,512]{1,0:T(8,128)S(1)}, u32[]{:S(2)}, u32[]{:S(2)}) collective-permute-start(f32[56,512]{1,0:T(8,128)S(1)} %get-tuple-element.37), channel_id=1, source_target_pairs={{0,2},{1,3},{2,0},{3,1},{4,6},{5,7},{6,4},{7,5},{8,10},{9,11},{10,... | collective-permute-start | bytes 344072 | tf_op jit(solution)/shard_map/ppermute | solution.py:486
  38.4 1.4 %collective-permute-start.11 = (f32[56,512]{1,0:T(8,128)S(1)}, f32[56,512]{1,0:T(8,128)S(1)}, u32[]{:S(2)}, u32[]{:S(2)}) collective-permute-start(f32[56,512]{1,0:T(8,128)S(1)} %get-tuple-element.38), channel_id=1, source_target_pairs={{0,3},{1,0},{2,1},{3,2},{4,7},{5,4},{6,5},{7,6},{8,11},{9,8},{10,9... | collective-permute-start | bytes 344072 | tf_op jit(solution)/shard_map/ppermute | solution.py:486
  39.8 1.4 %collective-permute-start.5 = (f32[56,512]{1,0:T(8,128)S(1)}, f32[56,512]{1,0:T(8,128)S(1)}, u32[]{:S(2)}, u32[]{:S(2)}) collective-permute-start(f32[56,512]{1,0:T(8,128)S(1)} %add_add_fusion.3), channel_id=1, source_target_pairs={{0,3},{1,0},{2,1},{3,2},{4,7},{5,4},{6,5},{7,6},{8,11},{9,8},{10,9... | collective-permute-start | bytes 344072 | tf_op jit(solution)/shard_map/ppermute | solution.py:486
  41.3 1.4 %collective-permute-start.4 = (f32[56,512]{1,0:T(8,128)S(1)}, f32[56,512]{1,0:T(8,128)S(1)}, u32[]{:S(2)}, u32[]{:S(2)}) collective-permute-start(f32[56,512]{1,0:T(8,128)S(1)} %add_add_fusion.3), channel_id=1, source_target_pairs={{0,2},{1,3},{2,0},{3,1},{4,6},{5,7},{6,4},{7,5},{8,10},{9,11},{10,... | collective-permute-start | bytes 344072 | tf_op jit(solution)/shard_map/ppermute | solution.py:486
  43.2 1.3 %collective-permute-done.11 = f32[56,512]{1,0:T(8,128)S(1)} collective-permute-done((f32[56,512]{1,0:T(8,128)S(1)}, f32[56,512]{1,0:T(8,128)S(1)}, u32[]{:S(2)}, u32[]{:S(2)}) %collective-permute-start.11) | collective-permute-done | bytes 114720 | tf_op jit(solution)/shard_map/ppermute | solution.py:486
  45.2 2.0 %collective-permute-start.13 = (f32[56,512]{1,0:T(8,128)S(1)}, f32[56,512]{1,0:T(8,128)S(1)}, u32[]{:S(2)}, u32[]{:S(2)}) collective-permute-start(f32[56,512]{1,0:T(8,128)S(1)} %add_add_fusion.1), channel_id=1, source_target_pairs={{0,8},{1,9},{2,10},{3,11},{4,12},{5,13},{6,14},{7,15},{8,0},{9,1},... | collective-permute-start | bytes 344072 | tf_op jit(solution)/shard_map/ppermute | solution.py:486
  48.1 1.2 %collective-permute-done.3 = f32[56,512]{1,0:T(8,128)S(1)} collective-permute-done((f32[56,512]{1,0:T(8,128)S(1)}, f32[56,512]{1,0:T(8,128)S(1)}, u32[]{:S(2)}, u32[]{:S(2)}) %collective-permute-start.3) | collective-permute-done | bytes 114720 | tf_op jit(solution)/shard_map/ppermute | solution.py:486
  49.3 2.3 %collective-permute-start.8 = (f32[56,512]{1,0:T(8,128)S(1)}, f32[56,512]{1,0:T(8,128)S(1)}, u32[]{:S(2)}, u32[]{:S(2)}) collective-permute-start(f32[56,512]{1,0:T(8,128)S(1)} %add_add_fusion.2.x0), channel_id=1, source_target_pairs={{0,12},{1,13},{2,14},{3,15},{4,0},{5,1},{6,2},{7,3},{8,4},{9,5},{1... | collective-permute-start | bytes 344072 | tf_op jit(solution)/shard_map/ppermute | solution.py:486
  53.3 4.4 %collective-permute-start.17 = (f32[56,512]{1,0:T(8,128)S(1)}, f32[56,512]{1,0:T(8,128)S(1)}, u32[]{:S(2)}, u32[]{:S(2)}) collective-permute-start(f32[56,512]{1,0:T(8,128)S(1)} %add_add_fusion.y0), channel_id=1, source_target_pairs={{0,3},{1,0},{2,1},{3,2},{4,7},{5,4},{6,5},{7,6},{8,11},{9,8},{10,9... | collective-permute-start | bytes 344072 | tf_op jit(solution)/shard_map/ppermute | solution.py:486
  57.7 1.3 %collective-permute-start.16 = (f32[56,512]{1,0:T(8,128)S(1)}, f32[56,512]{1,0:T(8,128)S(1)}, u32[]{:S(2)}, u32[]{:S(2)}) collective-permute-start(f32[56,512]{1,0:T(8,128)S(1)} %add_add_fusion.y0), channel_id=1, source_target_pairs={{0,2},{1,3},{2,0},{3,1},{4,6},{5,7},{6,4},{7,5},{8,10},{9,11},{10,... | collective-permute-start | bytes 344072 | tf_op jit(solution)/shard_map/ppermute | solution.py:486
  59.5 3.6 %stage_state.1 = (f32[4,2048,128]{2,1,0:T(8,128)S(1)}, bf16[64,4096]{1,0:T(8,128)(2,1)S(1)}) custom-call(s32[2,128]{1,0:T(2,128)S(1)} %get-tuple-element.26.plan_ref, f32[512,512]{1,0:T(8,128)S(1)} %bitcast.20, f32[2048,512]{1,0:T(8,128)} %bitcast.34), custom_call_target="tpu_custom_call" | custom-call | bytes 12582912 | tf_op jit(solution)/shard_map/stage_state/pallas_call | solution.py:501
  64.0 1.2 %collective-permute-done.15.y1 = f32[56,512]{1,0:T(8,128)S(1)} collective-permute-done((f32[56,512]{1,0:T(8,128)S(1)}, f32[56,512]{1,0:T(8,128)S(1)}, u32[]{:S(2)}, u32[]{:S(2)}) %collective-permute-start.15) | collective-permute-done | bytes 114720 | tf_op jit(solution)/shard_map/ppermute | solution.py:486
  65.2 7.8 %scan.1 = (bf16[3,128,512]{2,1,0:T(8,128)(2,1)}, f32[2048,512]{1,0:T(8,128)}) custom-call(s32[3]{0:T(128)S(1)} %pad_add_fusion.pos_ref, s32[1,128]{1,0:T(1,128)S(1)} %bitcast.32, f32[56,512]{1,0:T(8,128)S(1)} %add_add_fusion.2.x0, f32[56,512]{1,0:T(8,128)S(1)} %collective-permute-done.6.x1, f32[56,512]{1,0:T(8,128)S(1)} %collective-permute-done.7.x2, ...), custom_call_target="tpu_custom_call" | custom-call | tf_op jit(solution)/shard_map/scan/pallas_call | solution.py:512
  (52 shorter events, 5.5 us)
Async XLA Ops:
  3.3 17.1 %all-to-all-start = ((f32[16,24,128]{2,1,0:T(8,128)}), f32[16,24,128]{2,1,0:T(8,128)S(1)}, u32[]{:S(2)}, u32[]{:S(2)}) async-start(f32[16,24,128]{2,1,0:T(8,128)} %bitcast.7), calls=%async_computation | async-start | bytes 393216 | tf_op jit(solution)/shard_map/all_to_all | solution.py:421
  20.4 39.1 %all-to-all-start.1 = ((f32[32,16,512]{2,1,0:T(8,128)}), f32[32,16,512]{2,1,0:T(8,128)S(1)}, u32[]{:S(2)}, u32[]{:S(2)}) async-start(f32[32,16,512]{2,1,0:T(8,128)} %pick_state.1), calls=%async_computation.1 | async-start | bytes 2097152 | tf_op jit(solution)/shard_map/all_to_all | solution.py:494
  25.9 39.3 %copy-start.1 = (bf16[512,512]{1,0:T(8,128)(2,1)S(1)}, bf16[512,512]{1,0:T(8,128)(2,1)}, u32[]{:S(2)}) copy-start(bf16[512,512]{1,0:T(8,128)(2,1)} %dtw_ref.1) | copy-start | bytes 1572868
  25.9 39.3 %copy-start.2 = (bf16[3,128,512]{2,1,0:T(8,128)(2,1)S(1)}, bf16[3,128,512]{2,1,0:T(8,128)(2,1)}, u32[]{:S(2)}) copy-start(bf16[3,128,512]{2,1,0:T(8,128)(2,1)} %get-tuple-element.43.gate_ref) | copy-start | bytes 1179652
  25.9 39.2 %copy-start.4 = (f32[16,512]{1,0:T(8,128)S(1)}, f32[16,512]{1,0:T(8,128)}, u32[]{:S(2)}) copy-start(f32[16,512]{1,0:T(8,128)} %rate_ref.1) | copy-start | bytes 98308
  26.0 39.2 %copy-start.8 = (f32[512]{0:T(512)S(1)}, f32[512]{0:T(512)}, u32[]{:S(2)}) copy-start(f32[512]{0:T(512)} %param.18) | copy-start | bytes 6148
  28.2 10.2 %collective-permute-start = (f32[56,512]{1,0:T(8,128)S(1)}, f32[56,512]{1,0:T(8,128)S(1)}, u32[]{:S(2)}, u32[]{:S(2)}) collective-permute-start(f32[56,512]{1,0:T(8,128)S(1)} %get-tuple-element.32), channel_id=1, source_target_pairs={{0,4},{1,5},{2,6},{3,7},{4,8},{5,9},{6,10},{7,11},{8,12},{9,13},{1... | collective-permute-start | bytes 344072 | tf_op jit(solution)/shard_map/ppermute | solution.py:486
  29.8 10.0 %collective-permute-start.1 = (f32[56,512]{1,0:T(8,128)S(1)}, f32[56,512]{1,0:T(8,128)S(1)}, u32[]{:S(2)}, u32[]{:S(2)}) collective-permute-start(f32[56,512]{1,0:T(8,128)S(1)} %get-tuple-element.33), channel_id=1, source_target_pairs={{0,8},{1,9},{2,10},{3,11},{4,12},{5,13},{6,14},{7,15},{8,0},{9,1},... | collective-permute-start | bytes 344072 | tf_op jit(solution)/shard_map/ppermute | solution.py:486
  32.5 7.3 %collective-permute-start.2 = (f32[56,512]{1,0:T(8,128)S(1)}, f32[56,512]{1,0:T(8,128)S(1)}, u32[]{:S(2)}, u32[]{:S(2)}) collective-permute-start(f32[56,512]{1,0:T(8,128)S(1)} %get-tuple-element.34), channel_id=1, source_target_pairs={{0,12},{1,13},{2,14},{3,15},{4,0},{5,1},{6,2},{7,3},{8,4},{9,5},{1... | collective-permute-start | bytes 344072 | tf_op jit(solution)/shard_map/ppermute | solution.py:486
  33.9 8.7 %collective-permute-start.9 = (f32[56,512]{1,0:T(8,128)S(1)}, f32[56,512]{1,0:T(8,128)S(1)}, u32[]{:S(2)}, u32[]{:S(2)}) collective-permute-start(f32[56,512]{1,0:T(8,128)S(1)} %get-tuple-element.36), channel_id=1, source_target_pairs={{0,1},{1,2},{2,3},{3,0},{4,5},{5,6},{6,7},{7,4},{8,9},{9,10},{10,1... | collective-permute-start | bytes 344072 | tf_op jit(solution)/shard_map/ppermute | solution.py:486
  35.5 7.7 %collective-permute-start.10 = (f32[56,512]{1,0:T(8,128)S(1)}, f32[56,512]{1,0:T(8,128)S(1)}, u32[]{:S(2)}, u32[]{:S(2)}) collective-permute-start(f32[56,512]{1,0:T(8,128)S(1)} %get-tuple-element.37), channel_id=1, source_target_pairs={{0,2},{1,3},{2,0},{3,1},{4,6},{5,7},{6,4},{7,5},{8,10},{9,11},{10,... | collective-permute-start | bytes 344072 | tf_op jit(solution)/shard_map/ppermute | solution.py:486
  38.4 6.1 %collective-permute-start.11 = (f32[56,512]{1,0:T(8,128)S(1)}, f32[56,512]{1,0:T(8,128)S(1)}, u32[]{:S(2)}, u32[]{:S(2)}) collective-permute-start(f32[56,512]{1,0:T(8,128)S(1)} %get-tuple-element.38), channel_id=1, source_target_pairs={{0,3},{1,0},{2,1},{3,2},{4,7},{5,4},{6,5},{7,6},{8,11},{9,8},{10,9... | collective-permute-start | bytes 344072 | tf_op jit(solution)/shard_map/ppermute | solution.py:486
  39.8 7.5 %collective-permute-start.5 = (f32[56,512]{1,0:T(8,128)S(1)}, f32[56,512]{1,0:T(8,128)S(1)}, u32[]{:S(2)}, u32[]{:S(2)}) collective-permute-start(f32[56,512]{1,0:T(8,128)S(1)} %add_add_fusion.3), channel_id=1, source_target_pairs={{0,3},{1,0},{2,1},{3,2},{4,7},{5,4},{6,5},{7,6},{8,11},{9,8},{10,9... | collective-permute-start | bytes 344072 | tf_op jit(solution)/shard_map/ppermute | solution.py:486
  41.3 6.9 %collective-permute-start.4 = (f32[56,512]{1,0:T(8,128)S(1)}, f32[56,512]{1,0:T(8,128)S(1)}, u32[]{:S(2)}, u32[]{:S(2)}) collective-permute-start(f32[56,512]{1,0:T(8,128)S(1)} %add_add_fusion.3), channel_id=1, source_target_pairs={{0,2},{1,3},{2,0},{3,1},{4,6},{5,7},{6,4},{7,5},{8,10},{9,11},{10,... | collective-permute-start | bytes 344072 | tf_op jit(solution)/shard_map/ppermute | solution.py:486
  42.6 6.7 %collective-permute-start.3 = (f32[56,512]{1,0:T(8,128)S(1)}, f32[56,512]{1,0:T(8,128)S(1)}, u32[]{:S(2)}, u32[]{:S(2)}) collective-permute-start(f32[56,512]{1,0:T(8,128)S(1)} %add_add_fusion.3), channel_id=1, source_target_pairs={{0,1},{1,2},{2,3},{3,0},{4,5},{5,6},{6,7},{7,4},{8,9},{9,10},{10,1... | collective-permute-start | bytes 344072 | tf_op jit(solution)/shard_map/ppermute | solution.py:486
  44.5 8.1 %collective-permute-start.14 = (f32[56,512]{1,0:T(8,128)S(1)}, f32[56,512]{1,0:T(8,128)S(1)}, u32[]{:S(2)}, u32[]{:S(2)}) collective-permute-start(f32[56,512]{1,0:T(8,128)S(1)} %add_add_fusion.1), channel_id=1, source_target_pairs={{0,12},{1,13},{2,14},{3,15},{4,0},{5,1},{6,2},{7,3},{8,4},{9,5},{1... | collective-permute-start | bytes 344072 | tf_op jit(solution)/shard_map/ppermute | solution.py:486
  45.2 8.0 %collective-permute-start.13 = (f32[56,512]{1,0:T(8,128)S(1)}, f32[56,512]{1,0:T(8,128)S(1)}, u32[]{:S(2)}, u32[]{:S(2)}) collective-permute-start(f32[56,512]{1,0:T(8,128)S(1)} %add_add_fusion.1), channel_id=1, source_target_pairs={{0,8},{1,9},{2,10},{3,11},{4,12},{5,13},{6,14},{7,15},{8,0},{9,1},... | collective-permute-start | bytes 344072 | tf_op jit(solution)/shard_map/ppermute | solution.py:486
  47.3 6.0 %collective-permute-start.12 = (f32[56,512]{1,0:T(8,128)S(1)}, f32[56,512]{1,0:T(8,128)S(1)}, u32[]{:S(2)}, u32[]{:S(2)}) collective-permute-start(f32[56,512]{1,0:T(8,128)S(1)} %add_add_fusion.1), channel_id=1, source_target_pairs={{0,4},{1,5},{2,6},{3,7},{4,8},{5,9},{6,10},{7,11},{8,12},{9,13},{1... | collective-permute-start | bytes 344072 | tf_op jit(solution)/shard_map/ppermute | solution.py:486
  49.3 9.7 %collective-permute-start.8 = (f32[56,512]{1,0:T(8,128)S(1)}, f32[56,512]{1,0:T(8,128)S(1)}, u32[]{:S(2)}, u32[]{:S(2)}) collective-permute-start(f32[56,512]{1,0:T(8,128)S(1)} %add_add_fusion.2.x0), channel_id=1, source_target_pairs={{0,12},{1,13},{2,14},{3,15},{4,0},{5,1},{6,2},{7,3},{8,4},{9,5},{1... | collective-permute-start | bytes 344072 | tf_op jit(solution)/shard_map/ppermute | solution.py:486
  51.6 11.5 %collective-permute-start.7 = (f32[56,512]{1,0:T(8,128)S(1)}, f32[56,512]{1,0:T(8,128)S(1)}, u32[]{:S(2)}, u32[]{:S(2)}) collective-permute-start(f32[56,512]{1,0:T(8,128)S(1)} %add_add_fusion.2.x0), channel_id=1, source_target_pairs={{0,8},{1,9},{2,10},{3,11},{4,12},{5,13},{6,14},{7,15},{8,0},{9,1},... | collective-permute-start | bytes 344072 | tf_op jit(solution)/shard_map/ppermute | solution.py:486
  52.6 10.5 %collective-permute-start.6 = (f32[56,512]{1,0:T(8,128)S(1)}, f32[56,512]{1,0:T(8,128)S(1)}, u32[]{:S(2)}, u32[]{:S(2)}) collective-permute-start(f32[56,512]{1,0:T(8,128)S(1)} %add_add_fusion.2.x0), channel_id=1, source_target_pairs={{0,4},{1,5},{2,6},{3,7},{4,8},{5,9},{6,10},{7,11},{8,12},{9,13},{1... | collective-permute-start | bytes 344072 | tf_op jit(solution)/shard_map/ppermute | solution.py:486
  53.3 9.8 %collective-permute-start.17 = (f32[56,512]{1,0:T(8,128)S(1)}, f32[56,512]{1,0:T(8,128)S(1)}, u32[]{:S(2)}, u32[]{:S(2)}) collective-permute-start(f32[56,512]{1,0:T(8,128)S(1)} %add_add_fusion.y0), channel_id=1, source_target_pairs={{0,3},{1,0},{2,1},{3,2},{4,7},{5,4},{6,5},{7,6},{8,11},{9,8},{10,9... | collective-permute-start | bytes 344072 | tf_op jit(solution)/shard_map/ppermute | solution.py:486
  57.7 6.3 %collective-permute-start.16 = (f32[56,512]{1,0:T(8,128)S(1)}, f32[56,512]{1,0:T(8,128)S(1)}, u32[]{:S(2)}, u32[]{:S(2)}) collective-permute-start(f32[56,512]{1,0:T(8,128)S(1)} %add_add_fusion.y0), channel_id=1, source_target_pairs={{0,2},{1,3},{2,0},{3,1},{4,6},{5,7},{6,4},{7,5},{8,10},{9,11},{10,... | collective-permute-start | bytes 344072 | tf_op jit(solution)/shard_map/ppermute | solution.py:486
  59.0 6.2 %collective-permute-start.15 = (f32[56,512]{1,0:T(8,128)S(1)}, f32[56,512]{1,0:T(8,128)S(1)}, u32[]{:S(2)}, u32[]{:S(2)}) collective-permute-start(f32[56,512]{1,0:T(8,128)S(1)} %add_add_fusion.y0), channel_id=1, source_target_pairs={{0,1},{1,2},{2,3},{3,0},{4,5},{5,6},{6,7},{7,4},{8,9},{9,10},{10,1... | collective-permute-start | bytes 344072 | tf_op jit(solution)/shard_map/ppermute | solution.py:486
  (8 other events, 186.3 us)

commit v5 on v3

--- a/solution.py
+++ b/solution.py
@@ -248,18 +248,19 @@
         step_ref[rows, :] = jnp.where(alive, soft, 0.0)
 
 
+PITCH = 24
+
+
 def stage_kernel(plan_ref, got_ref, state_ref, out_ref, spread_ref, sems):
-    tiles, rows, _ = out_ref.shape
-    buckets = sems.shape[1]
-    states = got_ref.shape[0] // buckets
-    parts = sems.shape[0]
+    tiles = out_ref.shape[0]
+    buckets = sems.shape[0]
+    states = state_ref.shape[1]
     copies = []
     for l in range(tiles):
-        for i in range(parts):
-            here = pl.ds(i * (rows // parts), rows // parts)
-            copies.append(
-                pltpu.make_async_copy(state_ref.at[here, pl.ds(l * 128, 128)], out_ref.at[l, here], sems.at[i, l])
-            )
+        lanes = pl.ds(l * 128, 128)
+        copies.append(
+            pltpu.make_async_copy(state_ref.at[:, :, lanes], out_ref.at[l, :, pl.ds(0, states), :], sems.at[l])
+        )
     for copy in copies:
         copy.start()
     shape = spread_ref.shape
@@ -273,16 +274,14 @@
 
         @pl.when(gone >= 0)
         def _():
-            rows = pl.ds(pl.multiple_of(gone * states, states), states)
             for l in range(tiles):
-                out_ref[l, rows, :] = jnp.zeros((states, 128), F32)
+                out_ref[l, gone, 0:states, :] = jnp.zeros((states, 128), F32)
 
         @pl.when(here >= 0)
         def _():
-            rows = pl.ds(pl.multiple_of(here * states, states), states)
             there = pl.ds(pl.multiple_of(b * states, states), states)
             for l in range(tiles):
-                out_ref[l, rows, :] = got_ref[there, l * 128 : (l + 1) * 128]
+                out_ref[l, here, 0:states, :] = got_ref[there, l * 128 : (l + 1) * 128]
 
         return carry
 
@@ -303,11 +302,14 @@
     def stores(k):
         first = sum(PIECES[:k])
         slots_here = pl.ds(first, PIECES[k])
-        rows = pl.ds(first * states, PIECES[k] * states)
         copies = [pltpu.make_async_copy(gated_ref.at[:, slots_here], gated_out.at[:, slots_here], out_sems.at[k, tiles])]
         for l in range(tiles):
             copies.append(
-                pltpu.make_async_copy(final_s.at[l, rows], out_ref.at[rows, pl.ds(l * 128, 128)], out_sems.at[k, l])
+                pltpu.make_async_copy(
+                    final_s.reshape(tiles, slots, PITCH, 128).at[l, slots_here, pl.ds(0, states), :],
+                    out_ref.at[slots_here, :, pl.ds(l * 128, 128)],
+                    out_sems.at[k, l],
+                )
             )
         return copies
 
@@ -337,7 +339,7 @@
                 dxs.append(dt * cv)
                 accs.append(gain_ref[:, lanes] * cv)
         for n in range(states):
-            place = pl.ds(base * states + n, 8, stride=states)
+            place = pl.ds(base * PITCH + n, 8, stride=PITCH)
             gives = [wide_s[rows, n * 128 : (n + 1) * 128] for rows in lows]
             takes = [wide_s[rows, (states + n) * 128 : (states + n + 1) * 128] for rows in lows]
             for l in range(tiles):
@@ -500,24 +502,24 @@
     tiles = width // 128
     staged, spread = pl.pallas_call(
         stage_kernel,
-        out_shape=(sds((tiles, slots * states, 128), F32), sds((4 * states, 2 * states * 128), BF16)),
+        out_shape=(sds((tiles, slots, PITCH, 128), F32), sds((4 * states, 2 * states * 128), BF16)),
         in_specs=[SM, VM, HB],
         out_specs=(VM, VM),
-        scratch_shapes=[pltpu.SemaphoreType.DMA((1, buckets))],
+        scratch_shapes=[pltpu.SemaphoreType.DMA((buckets,))],
         compiler_params=pltpu.CompilerParams(vmem_limit_bytes=8 * MIB),
         cost_estimate=pl.CostEstimate(flops=0, bytes_accessed=12 * MIB, transcendentals=0),
         name="stage_state",
-    )(plan, got_state.reshape(buckets * states, width), state_rows)
+    )(plan, got_state.reshape(buckets * states, width), in_hbm(ssm_state))
 
     gated_out, state_out = pl.pallas_call(
         scan_kernel,
-        out_shape=(sds((steps, slots, width), BF16), sds((slots * states, width), F32)),
+        out_shape=(sds((steps, slots, width), BF16), sds((slots, states, width), F32)),
         in_specs=[SM] + [VM] * 17,
         out_specs=(HB, HB),
         scratch_shapes=[
             pltpu.VMEM((slots, 128), F32),
             pltpu.VMEM((states, width), F32),
-            pltpu.VMEM((tiles, slots * states, 128), F32),
+            pltpu.VMEM((tiles, slots * PITCH, 128), F32),
             pltpu.VMEM((total, width), F32),
             pltpu.VMEM((total, width), F32),
             pltpu.VMEM((total, 128), F32),
@@ -526,15 +528,15 @@
             pltpu.VMEM((total, 2 * states * 128), F32),
             pltpu.SemaphoreType.DMA((len(PIECES), tiles + 1)),
         ],
-        compiler_params=pltpu.CompilerParams(vmem_limit_bytes=20 * MIB),
+        compiler_params=pltpu.CompilerParams(vmem_limit_bytes=24 * MIB),
         name="scan",
     )(
-        pos, active.reshape(1, slots), *last_x, *last_y, staged, spread, conv_all, gate, dtproj_weight, dt_row,
+        pos, active.reshape(1, slots), *last_x, *last_y, staged.reshape(tiles, slots * PITCH, 128), spread, conv_all, gate, dtproj_weight, dt_row,
         a_rate, gain,
     )
     return (
         gated_out,
-        state_out.reshape(slots, states, width),
+        state_out,
         jnp.transpose(cache_out, (1, 0, 2)),
     )
 

time: 73.7 us -> 73.5 us (level)
  transfers between devices with their start and end apart: 20 -> 20, of which waited for: 7 -> 8; matrix products, arithmetic and copies ran while one was open for 0% -> 0% of each run, Pallas kernels for 17% -> 17%
where the time goes in v5:
time: 73.5 us; the launch traced here: 73.2 us
  starting transfers between devices  41.5 us (56%)
  Pallas kernels  22.7 us (31%)
  waiting for transfers between devices  7.49 us (10%)
  between operations  1.08 us (1%)
    ppermute x18, starting transfers between devices, gathered(): lax.ppermute(parts[d - 1], 'wa', shift(axis, d))  27.6 us
    all_to_all x1, starting transfers between devices, on_device(): lax.all_to_all(out_cache.reshape(peers, compact, 128), 'req', split_axis=...  8.6 us
    pallas_call x1, Pallas kernels, on_device(): pl.pallas_call(scan_kernel, out_shape=(sds((steps, slots, width), BF16),...  7.93 us
    ppermute x18, waiting for transfers between devices, gathered(): lax.ppermute(parts[d - 1], 'wa', shift(axis, d))  5.59 us
    all_to_all x1, starting transfers between devices, on_device(): lax.all_to_all(out_state, 'req', split_axis=0, concat_axis=0, tiled=True)  5.3 us
    pallas_call x1, Pallas kernels, on_device(): pl.pallas_call(stage_kernel, out_shape=(sds((tiles, slots, PITCH, 128), F...  3.59 us
    pallas_call x1, Pallas kernels, on_device(): pl.pallas_call(pick_state_kernel, out_shape=pltpu.HBM((buckets, states, w...  3.33 us
    pallas_call x1, Pallas kernels, on_device(): pl.pallas_call(conv_kernel, out_shape=(sds((steps, slots, width), BF16),...  3.14 us
  transfers between devices with their start and end apart: 20, of which 8 were waited for; matrix products, arithmetic and copies ran while one was open for 0% of the time, Pallas kernels for 17%

profile of v5, /device:TPU:32, one launch (start us, length us, event | category | flops | bytes accessed | tf_op | source)
XLA Modules:
  0.0 73.2 jit_solution(17923618689492643195)
XLA Ops:
  0.7 2.5 %pick_cache.1 = (f32[384,128]{1,0:T(8,128)}, s32[2,128]{1,0:T(2,128)S(1)}) custom-call(s32[3]{0:T(128)S(1)} %pad_add_fusion.pos_ref, s32[1,128]{1,0:T(1,128)} %bitcast.37, s32[1,128]{1,0:T(1,128)} %bitcast.27, bf16[3,128,512]{2,1,0:T(8,128)(2,1)} %bitcast.35), custom_call_target="tpu_custom_call" | custom-call | tf_op jit(solution)/shard_map/pick_cache/pallas_call | solution.py:407
  3.3 8.6 %all-to-all-start = ((f32[16,24,128]{2,1,0:T(8,128)}), f32[16,24,128]{2,1,0:T(8,128)S(1)}, u32[]{:S(2)}, u32[]{:S(2)}) async-start(f32[16,24,128]{2,1,0:T(8,128)} %bitcast.7), calls=%async_computation | async-start | bytes 393216 | tf_op jit(solution)/shard_map/all_to_all | solution.py:423
  11.9 3.3 %pick_state.1 = f32[32,16,512]{2,1,0:T(8,128)} custom-call(s32[2,128]{1,0:T(2,128)S(1)} %get-tuple-element.26.plan_ref, f32[2048,512]{1,0:T(8,128)} %bitcast.34), custom_call_target="tpu_custom_call" | custom-call | flops 1 | bytes 1 | tf_op jit(solution)/shard_map/pick_state/pallas_call | solution.py:427
  15.4 3.1 %convolve.1 = (bf16[3,128,512]{2,1,0:T(8,128)(2,1)S(1)}, bf16[3,128,512]{2,1,0:T(8,128)(2,1)}, bf16[3,128,512]{2,1,0:T(8,128)(2,1)}, bf16[96,512]{1,0:T(8,128)(2,1)S(1)}) custom-call(s32[3]{0:T(128)S(1)} %pad_add_fusion.pos_ref, s32[1,128]{1,0:T(1,128)} %bitcast.38, s32[1,128]{1,0:T(1,128)} %bitcast.28, s32[1,128]{1,0:T(1,128)} %bitcast.32, ...), custom_call_target="tpu_custom_call" | custom-call | tf_op jit(solution)/shard_map/convolve/pallas_call | solution.py:443
  18.5 1.9 %all-to-all-done = f32[16,24,128]{2,1,0:T(8,128)S(1)} async-done(((f32[16,24,128]{2,1,0:T(8,128)}), f32[16,24,128]{2,1,0:T(8,128)S(1)}, u32[]{:S(2)}, u32[]{:S(2)}) %all-to-all-start) | async-done | bytes 196640 | tf_op jit(solution)/shard_map/all_to_all | solution.py:423
  20.4 5.3 %all-to-all-start.1 = ((f32[32,16,512]{2,1,0:T(8,128)}), f32[32,16,512]{2,1,0:T(8,128)S(1)}, u32[]{:S(2)}, u32[]{:S(2)}) async-start(f32[32,16,512]{2,1,0:T(8,128)} %pick_state.1), calls=%async_computation.1 | async-start | bytes 2097152 | tf_op jit(solution)/shard_map/all_to_all | solution.py:496
  25.8 2.2 %project.1 = (bf16[384,512]{1,0:T(8,128)(2,1)}, f32[56,512]{1,0:T(8,128)S(1)}, f32[56,512]{1,0:T(8,128)S(1)}, f32[56,512]{1,0:T(8,128)S(1)}, f32[56,512]{1,0:T(8...) custom-call(s32[3]{0:T(128)S(1)} %pad_add_fusion.pos_ref, ...), custom_call_target="tpu_custom_call" | custom-call | tf_op jit(solution)/shard_map/project/pallas_call | solution.py:469
  28.0 1.6 %collective-permute-start = (f32[56,512]{1,0:T(8,128)S(1)}, f32[56,512]{1,0:T(8,128)S(1)}, u32[]{:S(2)}, u32[]{:S(2)}) collective-permute-start(f32[56,512]{1,0:T(8,128)S(1)} %get-tuple-element.32), channel_id=1, source_target_pairs={{0,4},{1,5},{2,6},{3,7},{4,8},{5,9},{6,10},{7,11},{8,12},{9,13},{1... | collective-permute-start | bytes 344072 | tf_op jit(solution)/shard_map/ppermute | solution.py:488
  29.6 2.7 %collective-permute-start.1 = (f32[56,512]{1,0:T(8,128)S(1)}, f32[56,512]{1,0:T(8,128)S(1)}, u32[]{:S(2)}, u32[]{:S(2)}) collective-permute-start(f32[56,512]{1,0:T(8,128)S(1)} %get-tuple-element.33), channel_id=1, source_target_pairs={{0,8},{1,9},{2,10},{3,11},{4,12},{5,13},{6,14},{7,15},{8,0},{9,1},... | collective-permute-start | bytes 344072 | tf_op jit(solution)/shard_map/ppermute | solution.py:488
  32.3 1.4 %collective-permute-start.2 = (f32[56,512]{1,0:T(8,128)S(1)}, f32[56,512]{1,0:T(8,128)S(1)}, u32[]{:S(2)}, u32[]{:S(2)}) collective-permute-start(f32[56,512]{1,0:T(8,128)S(1)} %get-tuple-element.34), channel_id=1, source_target_pairs={{0,12},{1,13},{2,14},{3,15},{4,0},{5,1},{6,2},{7,3},{8,4},{9,5},{1... | collective-permute-start | bytes 344072 | tf_op jit(solution)/shard_map/ppermute | solution.py:488
  33.8 1.6 %collective-permute-start.9 = (f32[56,512]{1,0:T(8,128)S(1)}, f32[56,512]{1,0:T(8,128)S(1)}, u32[]{:S(2)}, u32[]{:S(2)}) collective-permute-start(f32[56,512]{1,0:T(8,128)S(1)} %get-tuple-element.36), channel_id=1, source_target_pairs={{0,1},{1,2},{2,3},{3,0},{4,5},{5,6},{6,7},{7,4},{8,9},{9,10},{10,1... | collective-permute-start | bytes 344072 | tf_op jit(solution)/shard_map/ppermute | solution.py:488
  35.3 2.9 %collective-permute-start.10 = (f32[56,512]{1,0:T(8,128)S(1)}, f32[56,512]{1,0:T(8,128)S(1)}, u32[]{:S(2)}, u32[]{:S(2)}) collective-permute-start(f32[56,512]{1,0:T(8,128)S(1)} %get-tuple-element.37), channel_id=1, source_target_pairs={{0,2},{1,3},{2,0},{3,1},{4,6},{5,7},{6,4},{7,5},{8,10},{9,11},{10,... | collective-permute-start | bytes 344072 | tf_op jit(solution)/shard_map/ppermute | solution.py:488
  38.2 1.4 %collective-permute-start.11 = (f32[56,512]{1,0:T(8,128)S(1)}, f32[56,512]{1,0:T(8,128)S(1)}, u32[]{:S(2)}, u32[]{:S(2)}) collective-permute-start(f32[56,512]{1,0:T(8,128)S(1)} %get-tuple-element.38), channel_id=1, source_target_pairs={{0,3},{1,0},{2,1},{3,2},{4,7},{5,4},{6,5},{7,6},{8,11},{9,8},{10,9... | collective-permute-start | bytes 344072 | tf_op jit(solution)/shard_map/ppermute | solution.py:488
  39.6 1.5 %collective-permute-start.5 = (f32[56,512]{1,0:T(8,128)S(1)}, f32[56,512]{1,0:T(8,128)S(1)}, u32[]{:S(2)}, u32[]{:S(2)}) collective-permute-start(f32[56,512]{1,0:T(8,128)S(1)} %add_add_fusion.3), channel_id=1, source_target_pairs={{0,3},{1,0},{2,1},{3,2},{4,7},{5,4},{6,5},{7,6},{8,11},{9,8},{10,9... | collective-permute-start | bytes 344072 | tf_op jit(solution)/shard_map/ppermute | solution.py:488
  41.1 1.4 %collective-permute-start.4 = (f32[56,512]{1,0:T(8,128)S(1)}, f32[56,512]{1,0:T(8,128)S(1)}, u32[]{:S(2)}, u32[]{:S(2)}) collective-permute-start(f32[56,512]{1,0:T(8,128)S(1)} %add_add_fusion.3), channel_id=1, source_target_pairs={{0,2},{1,3},{2,0},{3,1},{4,6},{5,7},{6,4},{7,5},{8,10},{9,11},{10,... | collective-permute-start | bytes 344072 | tf_op jit(solution)/shard_map/ppermute | solution.py:488
  43.0 1.3 %collective-permute-done.11 = f32[56,512]{1,0:T(8,128)S(1)} collective-permute-done((f32[56,512]{1,0:T(8,128)S(1)}, f32[56,512]{1,0:T(8,128)S(1)}, u32[]{:S(2)}, u32[]{:S(2)}) %collective-permute-start.11) | collective-permute-done | bytes 114720 | tf_op jit(solution)/shard_map/ppermute | solution.py:488
  45.1 2.0 %collective-permute-start.13 = (f32[56,512]{1,0:T(8,128)S(1)}, f32[56,512]{1,0:T(8,128)S(1)}, u32[]{:S(2)}, u32[]{:S(2)}) collective-permute-start(f32[56,512]{1,0:T(8,128)S(1)} %add_add_fusion.1), channel_id=1, source_target_pairs={{0,8},{1,9},{2,10},{3,11},{4,12},{5,13},{6,14},{7,15},{8,0},{9,1},... | collective-permute-start | bytes 344072 | tf_op jit(solution)/shard_map/ppermute | solution.py:488
  48.0 1.2 %collective-permute-done.3 = f32[56,512]{1,0:T(8,128)S(1)} collective-permute-done((f32[56,512]{1,0:T(8,128)S(1)}, f32[56,512]{1,0:T(8,128)S(1)}, u32[]{:S(2)}, u32[]{:S(2)}) %collective-permute-start.3) | collective-permute-done | bytes 114720 | tf_op jit(solution)/shard_map/ppermute | solution.py:488
  49.2 2.3 %collective-permute-start.8 = (f32[56,512]{1,0:T(8,128)S(1)}, f32[56,512]{1,0:T(8,128)S(1)}, u32[]{:S(2)}, u32[]{:S(2)}) collective-permute-start(f32[56,512]{1,0:T(8,128)S(1)} %add_add_fusion.2.x0), channel_id=1, source_target_pairs={{0,12},{1,13},{2,14},{3,15},{4,0},{5,1},{6,2},{7,3},{8,4},{9,5},{1... | collective-permute-start | bytes 344072 | tf_op jit(solution)/shard_map/ppermute | solution.py:488
  53.1 4.4 %collective-permute-start.17 = (f32[56,512]{1,0:T(8,128)S(1)}, f32[56,512]{1,0:T(8,128)S(1)}, u32[]{:S(2)}, u32[]{:S(2)}) collective-permute-start(f32[56,512]{1,0:T(8,128)S(1)} %add_add_fusion.y0), channel_id=1, source_target_pairs={{0,3},{1,0},{2,1},{3,2},{4,7},{5,4},{6,5},{7,6},{8,11},{9,8},{10,9... | collective-permute-start | bytes 344072 | tf_op jit(solution)/shard_map/ppermute | solution.py:488
  57.5 1.3 %collective-permute-start.16 = (f32[56,512]{1,0:T(8,128)S(1)}, f32[56,512]{1,0:T(8,128)S(1)}, u32[]{:S(2)}, u32[]{:S(2)}) collective-permute-start(f32[56,512]{1,0:T(8,128)S(1)} %add_add_fusion.y0), channel_id=1, source_target_pairs={{0,2},{1,3},{2,0},{3,1},{4,6},{5,7},{6,4},{7,5},{8,10},{9,11},{10,... | collective-permute-start | bytes 344072 | tf_op jit(solution)/shard_map/ppermute | solution.py:488
  59.3 3.6 %stage_state.1 = (f32[4,128,24,128]{3,2,1,0:T(8,128)S(1)}, bf16[64,4096]{1,0:T(8,128)(2,1)S(1)}) custom-call(s32[2,128]{1,0:T(2,128)S(1)} %get-tuple-element.26.plan_ref, f32[512,512]{1,0:T(8,128)S(1)} %bitcast.21, f32[128,16,512]{2,1,0:T(8,128)} %state_ref.1), custom_call_target="tpu_custom_call" | custom-call | bytes 12582912 | tf_op jit(solution)/shard_map/stage_state/pallas_call | solution.py:503
  63.8 1.2 %collective-permute-done.15.y1 = f32[56,512]{1,0:T(8,128)S(1)} collective-permute-done((f32[56,512]{1,0:T(8,128)S(1)}, f32[56,512]{1,0:T(8,128)S(1)}, u32[]{:S(2)}, u32[]{:S(2)}) %collective-permute-start.15) | collective-permute-done | bytes 114720 | tf_op jit(solution)/shard_map/ppermute | solution.py:488
  65.1 7.9 %scan.1 = (bf16[3,128,512]{2,1,0:T(8,128)(2,1)}, f32[128,16,512]{2,1,0:T(8,128)}) custom-call(s32[3]{0:T(128)S(1)} %pad_add_fusion.pos_ref, s32[1,128]{1,0:T(1,128)S(1)} %bitcast.33, f32[56,512]{1,0:T(8,128)S(1)} %add_add_fusion.2.x0, f32[56,512]{1,0:T(8,128)S(1)} %collective-permute-done.6.x1, f32[56,512]{1,0:T(8,128)S(1)} %collective-permute-done.7.x2, ...), custom_call_target="tpu_custom_call" | custom-call | tf_op jit(solution)/shard_map/scan/pallas_call | solution.py:514
  (52 shorter events, 5.5 us)
Async XLA Ops:
  3.3 17.1 %all-to-all-start = ((f32[16,24,128]{2,1,0:T(8,128)}), f32[16,24,128]{2,1,0:T(8,128)S(1)}, u32[]{:S(2)}, u32[]{:S(2)}) async-start(f32[16,24,128]{2,1,0:T(8,128)} %bitcast.7), calls=%async_computation | async-start | bytes 393216 | tf_op jit(solution)/shard_map/all_to_all | solution.py:423
  20.4 38.9 %all-to-all-start.1 = ((f32[32,16,512]{2,1,0:T(8,128)}), f32[32,16,512]{2,1,0:T(8,128)S(1)}, u32[]{:S(2)}, u32[]{:S(2)}) async-start(f32[32,16,512]{2,1,0:T(8,128)} %pick_state.1), calls=%async_computation.1 | async-start | bytes 2097152 | tf_op jit(solution)/shard_map/all_to_all | solution.py:496
  25.7 39.3 %copy-start.1 = (bf16[512,512]{1,0:T(8,128)(2,1)S(1)}, bf16[512,512]{1,0:T(8,128)(2,1)}, u32[]{:S(2)}) copy-start(bf16[512,512]{1,0:T(8,128)(2,1)} %dtw_ref.1) | copy-start | bytes 1572868
  25.8 39.3 %copy-start.2 = (bf16[3,128,512]{2,1,0:T(8,128)(2,1)S(1)}, bf16[3,128,512]{2,1,0:T(8,128)(2,1)}, u32[]{:S(2)}) copy-start(bf16[3,128,512]{2,1,0:T(8,128)(2,1)} %get-tuple-element.43.gate_ref) | copy-start | bytes 1179652
  25.8 39.2 %copy-start.4 = (f32[16,512]{1,0:T(8,128)S(1)}, f32[16,512]{1,0:T(8,128)}, u32[]{:S(2)}) copy-start(f32[16,512]{1,0:T(8,128)} %rate_ref.1) | copy-start | bytes 98308
  25.8 39.2 %copy-start.8 = (f32[512]{0:T(512)S(1)}, f32[512]{0:T(512)}, u32[]{:S(2)}) copy-start(f32[512]{0:T(512)} %param.18) | copy-start | bytes 6148
  28.0 10.2 %collective-permute-start = (f32[56,512]{1,0:T(8,128)S(1)}, f32[56,512]{1,0:T(8,128)S(1)}, u32[]{:S(2)}, u32[]{:S(2)}) collective-permute-start(f32[56,512]{1,0:T(8,128)S(1)} %get-tuple-element.32), channel_id=1, source_target_pairs={{0,4},{1,5},{2,6},{3,7},{4,8},{5,9},{6,10},{7,11},{8,12},{9,13},{1... | collective-permute-start | bytes 344072 | tf_op jit(solution)/shard_map/ppermute | solution.py:488
  29.6 10.0 %collective-permute-start.1 = (f32[56,512]{1,0:T(8,128)S(1)}, f32[56,512]{1,0:T(8,128)S(1)}, u32[]{:S(2)}, u32[]{:S(2)}) collective-permute-start(f32[56,512]{1,0:T(8,128)S(1)} %get-tuple-element.33), channel_id=1, source_target_pairs={{0,8},{1,9},{2,10},{3,11},{4,12},{5,13},{6,14},{7,15},{8,0},{9,1},... | collective-permute-start | bytes 344072 | tf_op jit(solution)/shard_map/ppermute | solution.py:488
  32.3 7.3 %collective-permute-start.2 = (f32[56,512]{1,0:T(8,128)S(1)}, f32[56,512]{1,0:T(8,128)S(1)}, u32[]{:S(2)}, u32[]{:S(2)}) collective-permute-start(f32[56,512]{1,0:T(8,128)S(1)} %get-tuple-element.34), channel_id=1, source_target_pairs={{0,12},{1,13},{2,14},{3,15},{4,0},{5,1},{6,2},{7,3},{8,4},{9,5},{1... | collective-permute-start | bytes 344072 | tf_op jit(solution)/shard_map/ppermute | solution.py:488
  33.8 8.7 %collective-permute-start.9 = (f32[56,512]{1,0:T(8,128)S(1)}, f32[56,512]{1,0:T(8,128)S(1)}, u32[]{:S(2)}, u32[]{:S(2)}) collective-permute-start(f32[56,512]{1,0:T(8,128)S(1)} %get-tuple-element.36), channel_id=1, source_target_pairs={{0,1},{1,2},{2,3},{3,0},{4,5},{5,6},{6,7},{7,4},{8,9},{9,10},{10,1... | collective-permute-start | bytes 344072 | tf_op jit(solution)/shard_map/ppermute | solution.py:488
  35.3 7.7 %collective-permute-start.10 = (f32[56,512]{1,0:T(8,128)S(1)}, f32[56,512]{1,0:T(8,128)S(1)}, u32[]{:S(2)}, u32[]{:S(2)}) collective-permute-start(f32[56,512]{1,0:T(8,128)S(1)} %get-tuple-element.37), channel_id=1, source_target_pairs={{0,2},{1,3},{2,0},{3,1},{4,6},{5,7},{6,4},{7,5},{8,10},{9,11},{10,... | collective-permute-start | bytes 344072 | tf_op jit(solution)/shard_map/ppermute | solution.py:488
  38.2 6.1 %collective-permute-start.11 = (f32[56,512]{1,0:T(8,128)S(1)}, f32[56,512]{1,0:T(8,128)S(1)}, u32[]{:S(2)}, u32[]{:S(2)}) collective-permute-start(f32[56,512]{1,0:T(8,128)S(1)} %get-tuple-element.38), channel_id=1, source_target_pairs={{0,3},{1,0},{2,1},{3,2},{4,7},{5,4},{6,5},{7,6},{8,11},{9,8},{10,9... | collective-permute-start | bytes 344072 | tf_op jit(solution)/shard_map/ppermute | solution.py:488
  39.6 7.5 %collective-permute-start.5 = (f32[56,512]{1,0:T(8,128)S(1)}, f32[56,512]{1,0:T(8,128)S(1)}, u32[]{:S(2)}, u32[]{:S(2)}) collective-permute-start(f32[56,512]{1,0:T(8,128)S(1)} %add_add_fusion.3), channel_id=1, source_target_pairs={{0,3},{1,0},{2,1},{3,2},{4,7},{5,4},{6,5},{7,6},{8,11},{9,8},{10,9... | collective-permute-start | bytes 344072 | tf_op jit(solution)/shard_map/ppermute | solution.py:488
  41.1 6.9 %collective-permute-start.4 = (f32[56,512]{1,0:T(8,128)S(1)}, f32[56,512]{1,0:T(8,128)S(1)}, u32[]{:S(2)}, u32[]{:S(2)}) collective-permute-start(f32[56,512]{1,0:T(8,128)S(1)} %add_add_fusion.3), channel_id=1, source_target_pairs={{0,2},{1,3},{2,0},{3,1},{4,6},{5,7},{6,4},{7,5},{8,10},{9,11},{10,... | collective-permute-start | bytes 344072 | tf_op jit(solution)/shard_map/ppermute | solution.py:488
  42.4 6.7 %collective-permute-start.3 = (f32[56,512]{1,0:T(8,128)S(1)}, f32[56,512]{1,0:T(8,128)S(1)}, u32[]{:S(2)}, u32[]{:S(2)}) collective-permute-start(f32[56,512]{1,0:T(8,128)S(1)} %add_add_fusion.3), channel_id=1, source_target_pairs={{0,1},{1,2},{2,3},{3,0},{4,5},{5,6},{6,7},{7,4},{8,9},{9,10},{10,1... | collective-permute-start | bytes 344072 | tf_op jit(solution)/shard_map/ppermute | solution.py:488
  44.4 8.1 %collective-permute-start.14 = (f32[56,512]{1,0:T(8,128)S(1)}, f32[56,512]{1,0:T(8,128)S(1)}, u32[]{:S(2)}, u32[]{:S(2)}) collective-permute-start(f32[56,512]{1,0:T(8,128)S(1)} %add_add_fusion.1), channel_id=1, source_target_pairs={{0,12},{1,13},{2,14},{3,15},{4,0},{5,1},{6,2},{7,3},{8,4},{9,5},{1... | collective-permute-start | bytes 344072 | tf_op jit(solution)/shard_map/ppermute | solution.py:488
  45.1 8.0 %collective-permute-start.13 = (f32[56,512]{1,0:T(8,128)S(1)}, f32[56,512]{1,0:T(8,128)S(1)}, u32[]{:S(2)}, u32[]{:S(2)}) collective-permute-start(f32[56,512]{1,0:T(8,128)S(1)} %add_add_fusion.1), channel_id=1, source_target_pairs={{0,8},{1,9},{2,10},{3,11},{4,12},{5,13},{6,14},{7,15},{8,0},{9,1},... | collective-permute-start | bytes 344072 | tf_op jit(solution)/shard_map/ppermute | solution.py:488
  47.1 6.0 %collective-permute-start.12 = (f32[56,512]{1,0:T(8,128)S(1)}, f32[56,512]{1,0:T(8,128)S(1)}, u32[]{:S(2)}, u32[]{:S(2)}) collective-permute-start(f32[56,512]{1,0:T(8,128)S(1)} %add_add_fusion.1), channel_id=1, source_target_pairs={{0,4},{1,5},{2,6},{3,7},{4,8},{5,9},{6,10},{7,11},{8,12},{9,13},{1... | collective-permute-start | bytes 344072 | tf_op jit(solution)/shard_map/ppermute | solution.py:488
  49.2 9.6 %collective-permute-start.8 = (f32[56,512]{1,0:T(8,128)S(1)}, f32[56,512]{1,0:T(8,128)S(1)}, u32[]{:S(2)}, u32[]{:S(2)}) collective-permute-start(f32[56,512]{1,0:T(8,128)S(1)} %add_add_fusion.2.x0), channel_id=1, source_target_pairs={{0,12},{1,13},{2,14},{3,15},{4,0},{5,1},{6,2},{7,3},{8,4},{9,5},{1... | collective-permute-start | bytes 344072 | tf_op jit(solution)/shard_map/ppermute | solution.py:488
  51.5 11.4 %collective-permute-start.7 = (f32[56,512]{1,0:T(8,128)S(1)}, f32[56,512]{1,0:T(8,128)S(1)}, u32[]{:S(2)}, u32[]{:S(2)}) collective-permute-start(f32[56,512]{1,0:T(8,128)S(1)} %add_add_fusion.2.x0), channel_id=1, source_target_pairs={{0,8},{1,9},{2,10},{3,11},{4,12},{5,13},{6,14},{7,15},{8,0},{9,1},... | collective-permute-start | bytes 344072 | tf_op jit(solution)/shard_map/ppermute | solution.py:488
  52.5 10.4 %collective-permute-start.6 = (f32[56,512]{1,0:T(8,128)S(1)}, f32[56,512]{1,0:T(8,128)S(1)}, u32[]{:S(2)}, u32[]{:S(2)}) collective-permute-start(f32[56,512]{1,0:T(8,128)S(1)} %add_add_fusion.2.x0), channel_id=1, source_target_pairs={{0,4},{1,5},{2,6},{3,7},{4,8},{5,9},{6,10},{7,11},{8,12},{9,13},{1... | collective-permute-start | bytes 344072 | tf_op jit(solution)/shard_map/ppermute | solution.py:488
  53.1 9.8 %collective-permute-start.17 = (f32[56,512]{1,0:T(8,128)S(1)}, f32[56,512]{1,0:T(8,128)S(1)}, u32[]{:S(2)}, u32[]{:S(2)}) collective-permute-start(f32[56,512]{1,0:T(8,128)S(1)} %add_add_fusion.y0), channel_id=1, source_target_pairs={{0,3},{1,0},{2,1},{3,2},{4,7},{5,4},{6,5},{7,6},{8,11},{9,8},{10,9... | collective-permute-start | bytes 344072 | tf_op jit(solution)/shard_map/ppermute | solution.py:488
  57.5 6.3 %collective-permute-start.16 = (f32[56,512]{1,0:T(8,128)S(1)}, f32[56,512]{1,0:T(8,128)S(1)}, u32[]{:S(2)}, u32[]{:S(2)}) collective-permute-start(f32[56,512]{1,0:T(8,128)S(1)} %add_add_fusion.y0), channel_id=1, source_target_pairs={{0,2},{1,3},{2,0},{3,1},{4,6},{5,7},{6,4},{7,5},{8,10},{9,11},{10,... | collective-permute-start | bytes 344072 | tf_op jit(solution)/shard_map/ppermute | solution.py:488
  58.8 6.2 %collective-permute-start.15 = (f32[56,512]{1,0:T(8,128)S(1)}, f32[56,512]{1,0:T(8,128)S(1)}, u32[]{:S(2)}, u32[]{:S(2)}) collective-permute-start(f32[56,512]{1,0:T(8,128)S(1)} %add_add_fusion.y0), channel_id=1, source_target_pairs={{0,1},{1,2},{2,3},{3,0},{4,5},{5,6},{6,7},{7,4},{8,9},{9,10},{10,1... | collective-permute-start | bytes 344072 | tf_op jit(solution)/shard_map/ppermute | solution.py:488
  (8 other events, 185.5 us)
